TPU v7x, 32 devices: a whole 2x2x4 slice. The times are simulated.
32 devices in a mesh: el: 4 (over y, x), ph: 8 (over z, core).
Axes of the slice: x: 2, y: 2, z: 4, core: 2. Of those that a mesh axis runs over, the one named last changes fastest.
Arguments:
- elec_dev: float32 [128, 96, 256], P(('el', 'ph')), may hold values from -6 to 6
- phon_dev: float32 [8, 48, 96, 256], P('ph', 'el'), may hold values from -6 to 6
- elec_source: float32 [128, 96, 256], P(('el', 'ph')), may hold values from -6 to 6
- phon_source: float32 [8, 48, 96, 256], P('ph', 'el'), may hold values from -6 to 6
- elec_rate: float32 [128, 256], P(('el', 'ph')), may hold values from 0.75 to 3
- phon_rate: float32 [8, 48, 256], P('ph', 'el'), may hold values from 0.75 to 3
- tiles: bfloat16 [4, 8, 128, 256, 256], P('el', 'ph'), may hold values from -0.09375 to 0.09375
- tile_rows: int32 [4, 8, 128], P('el', 'ph'), may hold values from 0 to 31, as said below
- tile_cols: int32 [4, 8, 128], P('el', 'ph'), may hold values from 0 to 47, as said below
- tile_count: int32 [4, 8], P('el', 'ph'), may hold values from 16 to 128, as said below
Outputs:
- elec_out: float32 [128, 96, 256], P(('el', 'ph'))
- phon_out: float32 [8, 48, 96, 256], P('ph', 'el')
Inputs may be any that keep to these rules, and one draw needn't show every extreme that they name: `tile_rows`: block of each slot's tile among the 32 electron blocks of its pattern row; the slots of one cell name distinct (row, column) pairs. `tile_cols`: block of each slot's tile among the 48 phonon blocks of its pattern column. Slots 0 to tile_count - 1 of a cell are live; some cell is full in every draw.
All inputs are finite; a program needn't handle non-finite values.
Results may differ from a plain program's by a relative error of at most 0.0021.
Values may be sent and summed in bfloat16 or wider, within the bound.
No kernel may reach another device: no remote copies, remote signals or barrier semaphores. Data moves between devices by JAX's collectives and lax.ppermute only.
A program may use at most 128 MiB of HBM per device.

v0:
```python
import jax
import jax.numpy as jnp
from jax import lax
from jax.sharding import PartitionSpec as P

ITERS = 3


tile_group = 8


def tile_pass(tile_set, row_ids, col_ids, first_slot, end_slot, elec_blocks, phon_blocks):
    zero_totals = (
        jnp.zeros(elec_blocks.shape, jnp.float32),
        jnp.zeros(phon_blocks.shape, jnp.float32),
    )

    def one_group(group_index, totals):
        elec_total, phon_total = totals
        slot_start = group_index * tile_group
        block_tiles = lax.dynamic_slice_in_dim(tile_set, slot_start, tile_group, 0)
        group_rows = lax.dynamic_slice_in_dim(row_ids, slot_start, tile_group, 0)
        group_cols = lax.dynamic_slice_in_dim(col_ids, slot_start, tile_group, 0)
        places = slot_start + jnp.arange(tile_group, dtype=jnp.int32)
        active = (places >= first_slot) & (places < end_slot)
        weight_mask = jnp.where(active, 1.0, 0.0).astype(jnp.float32)[:, None, None]
        elec_in = jnp.take(elec_blocks, group_rows, axis=0)
        phon_in = jnp.take(phon_blocks, group_cols, axis=0)
        to_phonon = (
            jnp.einsum("tka,tab->tkb", elec_in, block_tiles, preferred_element_type=jnp.float32)
            * weight_mask
        )
        to_electron = (
            jnp.einsum("tkb,tab->tka", phon_in, block_tiles, preferred_element_type=jnp.float32)
            * weight_mask
        )
        elec_total = elec_total.at[group_rows].add(to_electron)
        phon_total = phon_total.at[group_cols].add(to_phonon)
        return (elec_total, phon_total)

    return lax.fori_loop(
        first_slot // tile_group, (end_slot + tile_group - 1) // tile_group, one_group, zero_totals
    )


def local(
    elec_dev,
    phon_dev,
    elec_source,
    phon_source,
    elec_rate,
    phon_rate,
    tiles,
    tile_rows,
    tile_cols,
    tile_count,
):
    tile_set = tiles[0, 0]
    row_ids = tile_rows[0, 0]
    col_ids = tile_cols[0, 0]
    live_count = tile_count[0]
    own_end = live_count[0]
    elec_range = lax.all_gather(elec_dev.astype(jnp.bfloat16), "ph", axis=0, tiled=True)
    phon_range = lax.all_gather(phon_dev[0].astype(jnp.bfloat16), "el", axis=0, tiled=True)
    elec_now = elec_dev
    phon_now = phon_dev[0]
    for sweep_index in range(ITERS):
        elec_drag, phon_drag = tile_pass(
            tile_set, row_ids, col_ids, 0, own_end, elec_range, phon_range
        )
        elec_now = (
            elec_source + lax.psum_scatter(elec_drag, "ph", scatter_dimension=0, tiled=True)
        ) / elec_rate[:, None, :]
        phon_now = (
            phon_source[0] + lax.psum_scatter(phon_drag, "el", scatter_dimension=0, tiled=True)
        ) / phon_rate[0][:, None, :]
        if sweep_index + 1 < ITERS:
            elec_range = lax.all_gather(elec_now.astype(jnp.bfloat16), "ph", axis=0, tiled=True)
            phon_range = lax.all_gather(phon_now.astype(jnp.bfloat16), "el", axis=0, tiled=True)
    return (elec_now, phon_now[None])


def solution(mesh):
    in_specs = (
        P(("el", "ph"), None, None),
        P("ph", "el", None, None),
        P(("el", "ph"), None, None),
        P("ph", "el", None, None),
        P(("el", "ph"), None),
        P("ph", "el", None),
        P("el", "ph", None, None, None),
        P("el", "ph", None),
        P("el", "ph", None),
        P("el", "ph"),
    )
    out_specs = (P(("el", "ph"), None, None), P("ph", "el", None, None))
    return jax.shard_map(local, mesh=mesh, in_specs=in_specs, out_specs=out_specs, check_vma=False)
```

profile of v0, /device:TPU:0, one launch (start us, length us, event | category | flops | bytes accessed | tf_op | source)
XLA Modules:
  0.0 1220.7 jit_solution(766342646286129343)
XLA Ops:
  11.9 26.1 %all-gather.8.cloned.1.call-done = bf16[32,96,256]{2,1,0:T(8,128)(2,1)} async-done(((bf16[4,96,256]{2,1,0:T(8,128)(2,1)}), bf16[32,96,256]{2,1,0:T(8,128)(2,1)}) %all-gather.8.cloned.1.call-update) | async-done | bytes 1572880 | tf_op jit(solution)/shard_map/all_gather | solution.py:63
  38.0 39.5 %all-gather.18.cloned.1.call-done = bf16[1,48,96,256]{3,2,0,1:T(8,128)(2,1)} async-done(((bf16[1,12,96,256]{3,2,0,1:T(8,128)(2,1)}), bf16[1,48,96,256]{3,2,0,1:T(8,128)(2,1)}) %all-gather.18.cloned.1.call-update) | async-done | bytes 2359312 | tf_op jit(solution)/shard_map/all_gather | solution.py:64
  82.2 28.6 %while.36 = (s32[]{:T(128)}, f32[32,96,256]{2,1,0:T(8,128)}, f32[48,96,256]{2,1,0:T(8,128)}, s32[]{:T(128)}, s32[128]{0:T(128)S(1)}, /*index=5*/s32[128]{0:T(128...) while((s32[]{:T(128)}, f32[32,96,256]{2,1,0:T(8,128)}, ...), condition=%wide.region_3.6_spmd, body=%wide.region_0.5_spmd.sunk | while | flops 202508432 | bytes 10756743 | solution.py:41
  86.5 3.1 scatter_fusion.1
  93.5 3.0 scatter_fusion
  107.8 3.0 scatter_fusion
  111.5 240.5 %reduce-scatter.9.cloned.1.call-done = f32[4,96,256]{2,1,0:T(8,128)} async-done(((f32[32,96,256]{2,1,0:T(8,128)}), f32[4,96,256]{2,1,0:T(8,128)}) %reduce-scatter.9.cloned.1.call-update) | async-done | bytes 393232 | tf_op jit(solution)/shard_map/reduce_scatter | solution.py:72
  353.8 57.2 %reduce-scatter.7.cloned.1.call-done = f32[12,96,256]{2,1,0:T(8,128)} async-done(((f32[48,96,256]{2,1,0:T(8,128)}), f32[12,96,256]{2,1,0:T(8,128)}) %reduce-scatter.7.cloned.1.call-update) | async-done | bytes 1179664 | tf_op jit(solution)/shard_map/reduce_scatter | solution.py:75
  413.4 24.8 %all-gather.12.cloned.1.call-done = bf16[32,96,256]{2,1,0:T(8,128)(2,1)} async-done(((bf16[4,96,256]{2,1,0:T(8,128)(2,1)}), bf16[32,96,256]{2,1,0:T(8,128)(2,1)}) %all-gather.12.cloned.1.call-update) | async-done | bytes 1572880 | tf_op jit(solution)/shard_map/all_gather | solution.py:78
  438.2 39.3 %all-gather.10.cloned.1.call-done = bf16[48,96,256]{2,1,0:T(8,128)(2,1)} async-done(((bf16[12,96,256]{2,1,0:T(8,128)(2,1)}), bf16[48,96,256]{2,1,0:T(8,128)(2,1)}) %all-gather.10.cloned.1.call-update) | async-done | bytes 2359312 | tf_op jit(solution)/shard_map/all_gather | solution.py:79
  482.2 28.6 %while.37 = (s32[]{:T(128)}, f32[32,96,256]{2,1,0:T(8,128)}, f32[48,96,256]{2,1,0:T(8,128)}, s32[]{:T(128)}, s32[128]{0:T(128)S(1)}, /*index=5*/s32[128]{0:T(128...) while((s32[]{:T(128)}, f32[32,96,256]{2,1,0:T(8,128)}, ...), condition=%wide.region_9.12_spmd, body=%wide.region_6.11_spmd.sunk | while | flops 202508432 | bytes 10756743 | solution.py:41
  486.5 3.1 scatter_fusion.3
  493.5 3.0 scatter_fusion.2
  507.8 3.0 scatter_fusion.2
  511.7 240.3 %reduce-scatter.13.cloned.1.call-done = f32[4,96,256]{2,1,0:T(8,128)} async-done(((f32[32,96,256]{2,1,0:T(8,128)}), f32[4,96,256]{2,1,0:T(8,128)}) %reduce-scatter.13.cloned.1.call-update) | async-done | bytes 393232 | tf_op jit(solution)/shard_map/reduce_scatter | solution.py:72
  753.8 57.5 %reduce-scatter.11.cloned.1.call-done = f32[12,96,256]{2,1,0:T(8,128)} async-done(((f32[48,96,256]{2,1,0:T(8,128)}), f32[12,96,256]{2,1,0:T(8,128)}) %reduce-scatter.11.cloned.1.call-update) | async-done | bytes 1179664 | tf_op jit(solution)/shard_map/reduce_scatter | solution.py:75
  813.6 25.0 %all-gather.16.cloned.1.call-done = bf16[32,96,256]{2,1,0:T(8,128)(2,1)} async-done(((bf16[4,96,256]{2,1,0:T(8,128)(2,1)}), bf16[32,96,256]{2,1,0:T(8,128)(2,1)}) %all-gather.16.cloned.1.call-update) | async-done | bytes 1572880 | tf_op jit(solution)/shard_map/all_gather | solution.py:78
  838.5 39.3 %all-gather.14.cloned.1.call-done = bf16[48,96,256]{2,1,0:T(8,128)(2,1)} async-done(((bf16[12,96,256]{2,1,0:T(8,128)(2,1)}), bf16[48,96,256]{2,1,0:T(8,128)(2,1)}) %all-gather.14.cloned.1.call-update) | async-done | bytes 2359312 | tf_op jit(solution)/shard_map/all_gather | solution.py:79
  882.6 28.6 %while.38 = (s32[]{:T(128)}, f32[32,96,256]{2,1,0:T(8,128)}, f32[48,96,256]{2,1,0:T(8,128)}, s32[]{:T(128)}, s32[128]{0:T(128)S(1)}, /*index=5*/s32[128]{0:T(128...) while((s32[]{:T(128)}, f32[32,96,256]{2,1,0:T(8,128)}, ...), condition=%wide.region_15.18_spmd, body=%wide.region_12.17_spmd.sunk | while | flops 202508432 | bytes 10756743 | solution.py:41
  886.9 3.1 scatter_fusion.5
  893.9 3.0 scatter_fusion.4
  908.2 3.0 scatter_fusion.4
  911.8 240.5 %reduce-scatter.15.cloned.1.call-done = f32[4,96,256]{2,1,0:T(8,128)} async-done(((f32[32,96,256]{2,1,0:T(8,128)}), f32[4,96,256]{2,1,0:T(8,128)}) %reduce-scatter.15.cloned.1.call-update) | async-done | bytes 393232 | tf_op jit(solution)/shard_map/reduce_scatter | solution.py:72
  1154.1 57.3 %reduce-scatter.17.cloned.1.call-done = f32[12,96,256]{2,1,0:T(8,128)} async-done(((f32[48,96,256]{2,1,0:T(8,128)}), f32[12,96,256]{2,1,0:T(8,128)}) %reduce-scatter.17.cloned.1.call-update) | async-done | bytes 1179664 | tf_op jit(solution)/shard_map/reduce_scatter | solution.py:75
  (102 shorter events, 90.9 us)
Async XLA Ops:
  7.2 30.8 %all-gather.8.cloned.1.call-start = ((), (), s32[]{:S(2)}) async-start(), calls=%async_computation.6 | async-start | bytes 1769472 | tf_op jit(solution)/shard_map/all_gather | solution.py:63
  8.9 68.5 %all-gather.18.cloned.1.call-start = ((), (), s32[]{:S(2)}) async-start(), calls=%async_computation.17 | async-start | bytes 2949120 | tf_op jit(solution)/shard_map/all_gather | solution.py:64
  11.2 340.8 %reduce-scatter.9.cloned.1.call-start = ((), (), s32[]{:S(2)}) async-start(), calls=%async_computation.9 | async-start | bytes 3538944 | tf_op jit(solution)/shard_map/reduce_scatter | solution.py:72
  77.5 4.7 copy-start.2
  77.5 4.7 copy-start.3
  110.8 241.1 %copy-start.1 = (f32[4,96,256]{2,1,0:T(8,128)S(1)}, f32[4,96,256]{2,1,0:T(8,128)}, u32[]{:S(2)}) copy-start(f32[4,96,256]{2,1,0:T(8,128)} %param.22) | copy-start | bytes 1179652
  110.8 241.1 %copy-start.4 = (f32[4,256]{1,0:T(4,128)S(1)}, f32[4,256]{1,0:T(4,128)}, u32[]{:S(2)}) copy-start(f32[4,256]{1,0:T(4,128)} %param.24) | copy-start | bytes 12292
  110.9 242.9 %copy-start.5 = (f32[1,12,256]{2,0,1:T(1,128)S(1)}, f32[1,12,256]{2,0,1:T(1,128)}, u32[]{:S(2)}) copy-start(f32[1,12,256]{2,0,1:T(1,128)} %param.25) | copy-start | bytes 36868
  110.9 300.2 %copy-start = (f32[1,12,96,256]{3,2,1,0:T(8,128)S(1)}, f32[1,12,96,256]{3,2,1,0:T(8,128)}, u32[]{:S(2)}) copy-start(f32[1,12,96,256]{3,2,1,0:T(8,128)} %param.23) | copy-start | bytes 3538948
  110.9 300.1 %reduce-scatter.7.cloned.1.call-start = ((), (), s32[]{:S(2)}) async-start(), calls=%async_computation.7 | async-start | bytes 5898240 | tf_op jit(solution)/shard_map/reduce_scatter | solution.py:75
  111.5 326.7 %all-gather.12.cloned.1.call-start = ((), (), s32[]{:S(2)}) async-start(), calls=%async_computation.10 | async-start | bytes 1769472 | tf_op jit(solution)/shard_map/all_gather | solution.py:78
  353.7 123.8 %all-gather.10.cloned.1.call-start = ((), (), s32[]{:S(2)}) async-start(), calls=%async_computation.8 | async-start | bytes 2949120 | tf_op jit(solution)/shard_map/all_gather | solution.py:79
  413.3 338.7 %reduce-scatter.13.cloned.1.call-start = ((), (), s32[]{:S(2)}) async-start(), calls=%async_computation.13 | async-start | bytes 3538944 | tf_op jit(solution)/shard_map/reduce_scatter | solution.py:72
  510.9 300.4 %reduce-scatter.11.cloned.1.call-start = ((), (), s32[]{:S(2)}) async-start(), calls=%async_computation.11 | async-start | bytes 5898240 | tf_op jit(solution)/shard_map/reduce_scatter | solution.py:75
  511.6 326.9 %all-gather.16.cloned.1.call-start = ((), (), s32[]{:S(2)}) async-start(), calls=%async_computation.14 | async-start | bytes 1769472 | tf_op jit(solution)/shard_map/all_gather | solution.py:78
  753.7 124.1 %all-gather.14.cloned.1.call-start = ((), (), s32[]{:S(2)}) async-start(), calls=%async_computation.12 | async-start | bytes 2949120 | tf_op jit(solution)/shard_map/all_gather | solution.py:79
  813.5 338.8 %reduce-scatter.15.cloned.1.call-start = ((), (), s32[]{:S(2)}) async-start(), calls=%async_computation.15 | async-start | bytes 3538944 | tf_op jit(solution)/shard_map/reduce_scatter | solution.py:72
  911.2 300.2 %reduce-scatter.17.cloned.1.call-start = ((), (), s32[]{:S(2)}) async-start(), calls=%async_computation.16 | async-start | bytes 5898240 | tf_op jit(solution)/shard_map/reduce_scatter | solution.py:75
Sparse Core Ops, SparseCore 0:
  10.2 27.7 all-gather.7
  40.4 37.0 all-gather.17
  111.0 240.9 reduce-scatter.8
  354.8 56.1 reduce-scatter.6
  413.1 25.0 all-gather.11
  440.5 37.0 all-gather.9
  511.0 240.9 reduce-scatter.12
  755.0 56.2 reduce-scatter.10
  813.5 25.0 all-gather.15
  840.8 37.0 all-gather.13
  911.3 240.9 reduce-scatter.14
  1155.2 56.2 reduce-scatter.16
where the time goes:
time: 1230 us; the launch traced here: 1220 us
  waiting for transfers between devices  1090 us (89%)
  other arithmetic  56.9 us (5%)
  local copies, waits for them, and re-layouts  39.4 us (3%)
  matrix products  19.6 us (2%)
  between operations  14.9 us (1%)
    reduce_scatter x3, waiting for transfers between devices, local(): lax.psum_scatter(elec_drag, 'ph', scatter_dimension=0, tiled=True)  721 us
    reduce_scatter x3, waiting for transfers between devices, local(): lax.psum_scatter(phon_drag, 'el', scatter_dimension=0, tiled=True)  172 us
    all_gather x2, waiting for transfers between devices, local(): lax.all_gather(phon_now.astype(jnp.bfloat16), 'el', axis=0, tiled=True)  78.6 us
    all_gather x2, waiting for transfers between devices, local(): lax.all_gather(elec_now.astype(jnp.bfloat16), 'ph', axis=0, tiled=True)  49.8 us
    all_gather x1, waiting for transfers between devices, local(): lax.all_gather(phon_dev[0].astype(jnp.bfloat16), 'el', axis=0, tiled=True)  39.5 us
    all_gather x1, waiting for transfers between devices, local(): lax.all_gather(elec_dev.astype(jnp.bfloat16), 'ph', axis=0, tiled=True)  26.1 us
  transfers between devices with their start and end apart: 12, of which 12 were waited for; matrix products, arithmetic and copies ran while one was open for 1% of the time, Pallas kernels for 0%

commit v1 on v0

v1 whole, which is shorter than its diff:
```python
import functools
import math

import jax
import jax.numpy as jnp
from jax import lax
from jax.experimental import pallas as pl
from jax.experimental.pallas import tpu as pltpu
from jax.sharding import PartitionSpec as P

ITERS = 3
DEPTH = 4
LEVELS = 32767.0
SMALLEST = 1e-33


def partner(size, step):
    if size & (size - 1) == 0:
        return lambda place: place ^ step
    return lambda place: (place + step) % size


def source_of(size, step, place):
    if size & (size - 1) == 0:
        return place ^ step
    return (place - step) % size


def send(value, axis, size, place_of):
    return lax.ppermute(value, axis, [(place, place_of(place)) for place in range(size)])


def encode(block):
    peak = jnp.maximum(jnp.max(jnp.abs(block), axis=0, keepdims=True), SMALLEST)
    coded = jnp.round(block * (LEVELS / peak)).astype(jnp.int32).astype(jnp.int16)
    return coded, peak * (1.0 / LEVELS)


def drag_body(piece_count, group, transposed, whole_outs, coded_outs, *refs):
    ids_in, ids_out, group_count, tiles = refs[:4]
    pieces = refs[4 : 4 + piece_count]
    at = 4 + piece_count
    wholes = refs[at : at + whole_outs]
    coded = refs[at + whole_outs : at + whole_outs + coded_outs]
    scales = refs[at + whole_outs + coded_outs : at + whole_outs + 2 * coded_outs]
    vectors, totals, held, piece_sems, tile_sems, out_sems = refs[at + whole_outs + 2 * coded_outs :]
    span = pieces[0].shape[0]
    loads = [
        pltpu.make_async_copy(
            pieces[index], vectors.at[pl.ds(index * span, span)], piece_sems.at[index]
        )
        for index in range(piece_count)
    ]
    for load in loads:
        load.start()
    groups = group_count[0]

    def fetch(index):
        slot = lax.rem(index, DEPTH)
        return pltpu.make_async_copy(
            tiles.at[pl.ds(index * group, group)], held.at[slot], tile_sems.at[slot]
        )

    for ahead in range(DEPTH - 1):

        @pl.when(ahead < groups)
        def _():
            fetch(ahead).start()

    totals[...] = jnp.zeros_like(totals)
    for load in loads:
        load.wait()

    def one_group(index, carry):
        @pl.when(index + DEPTH - 1 < groups)
        def _():
            fetch(index + DEPTH - 1).start()

        fetch(index).wait()
        slot = lax.rem(index, DEPTH)
        for inner in range(group):
            place = index * group + inner
            product = lax.dot_general(
                vectors[ids_in[place]],
                held[slot, inner],
                (((1,), (1 if transposed else 0,)), ((), ())),
                preferred_element_type=jnp.float32,
            )
            target = ids_out[place]
            totals[target] = totals[target] + product
        return carry

    lax.fori_loop(0, groups, one_group, 0)
    stores = []
    first = 0
    for index in range(whole_outs):
        size = wholes[index].shape[0]
        stores.append(
            pltpu.make_async_copy(
                totals.at[pl.ds(first, size)], wholes[index], out_sems.at[index]
            )
        )
        first += size
    for store in stores:
        store.start()
    for index in range(coded_outs):
        size = coded[index].shape[0]
        for block in range(size):
            coded_block, scale = encode(totals[first + block])
            coded[index][block] = coded_block
            scales[index][pl.ds(block, 1)] = scale
        first += size
    for store in stores:
        store.wait()


def drag(ids_in, ids_out, group_count, tile_set, group, pieces, transposed, whole_sizes, coded_sizes):
    span, rows, lanes = pieces[0].shape
    blocks_out = sum(whole_sizes) + sum(coded_sizes)
    any_space = pl.BlockSpec(memory_space=pl.ANY)
    smem = pl.BlockSpec(memory_space=pltpu.SMEM)
    vmem = pl.BlockSpec(memory_space=pltpu.VMEM)
    side = tile_set.shape[-1]
    return pl.pallas_call(
        functools.partial(
            drag_body, len(pieces), group, transposed, len(whole_sizes), len(coded_sizes)
        ),
        out_shape=[jax.ShapeDtypeStruct((size, rows, lanes), jnp.float32) for size in whole_sizes]
        + [jax.ShapeDtypeStruct((size, rows, lanes), jnp.int16) for size in coded_sizes]
        + [jax.ShapeDtypeStruct((size, lanes), jnp.float32) for size in coded_sizes],
        in_specs=[smem, smem, smem, any_space] + [any_space] * len(pieces),
        out_specs=[any_space] * len(whole_sizes) + [vmem] * (2 * len(coded_sizes)),
        scratch_shapes=[
            pltpu.VMEM((span * len(pieces), rows, lanes), jnp.bfloat16),
            pltpu.VMEM((blocks_out + 1, rows, lanes), jnp.float32),
            pltpu.VMEM((DEPTH, group, side, side), jnp.bfloat16),
            pltpu.SemaphoreType.DMA((len(pieces),)),
            pltpu.SemaphoreType.DMA((DEPTH,)),
            pltpu.SemaphoreType.DMA((max(len(whole_sizes), 1),)),
        ],
        compiler_params=pltpu.CompilerParams(vmem_limit_bytes=40 * 1024 * 1024),
        cost_estimate=pl.CostEstimate(
            flops=2 * tile_set.shape[0] * rows * side * side,
            bytes_accessed=tile_set.shape[0] * side * side * 2,
            transcendentals=0,
        ),
    )(ids_in, ids_out, group_count, tile_set, *pieces)


def pair_body(piece_count, mine, theirs, whole, *rest):
    coded, scales = rest[:piece_count], rest[piece_count:]
    span = whole.shape[0]
    whole[...] = mine[pl.ds(0, span)] + theirs[pl.ds(0, span)]
    for index in range(piece_count):
        for block in range(span):
            place = (index + 1) * span + block
            coded_block, scale = encode(mine[place] + theirs[place])
            coded[index][block] = coded_block
            scales[index][pl.ds(block, 1)] = scale


def pair_sum(mine, theirs, piece_count):
    blocks, rows, lanes = mine.shape
    span = blocks // (piece_count + 1)
    vmem = pl.BlockSpec(memory_space=pltpu.VMEM)
    return pl.pallas_call(
        functools.partial(pair_body, piece_count),
        out_shape=[jax.ShapeDtypeStruct((span, rows, lanes), jnp.float32)]
        + [jax.ShapeDtypeStruct((span, rows, lanes), jnp.int16)] * piece_count
        + [jax.ShapeDtypeStruct((span, lanes), jnp.float32)] * piece_count,
        in_specs=[vmem, vmem],
        out_specs=[vmem] * (1 + 2 * piece_count),
        compiler_params=pltpu.CompilerParams(vmem_limit_bytes=32 * 1024 * 1024),
    )(mine, theirs)


def renew(source, own, coded, scales, rate):
    total = own
    for values, scale in zip(coded, scales):
        total = total + values.astype(jnp.float32) * scale[:, None, :]
    return (source + total) / rate[:, None, :]


def local(
    n_el,
    n_ph,
    elec_dev,
    phon_dev,
    elec_source,
    phon_source,
    elec_rate,
    phon_rate,
    tiles,
    tile_rows,
    tile_cols,
    tile_count,
):
    tile_set = tiles[0, 0]
    slots = tile_set.shape[0]
    group = math.gcd(slots, 8)
    elec_span = elec_dev.shape[0]
    phon_span = phon_dev.shape[1]
    elec_blocks = elec_span * n_ph
    phon_blocks = phon_span * n_el
    cores = 2 if n_ph % 2 == 0 else 1
    n_z = n_ph // cores
    el_place = lax.axis_index("el")
    ph_place = lax.axis_index("ph")
    z_place, core_place = ph_place // cores, ph_place % cores

    def el_piece(owner):
        return owner ^ el_place if n_el & (n_el - 1) == 0 else (el_place - owner) % n_el

    live = jnp.arange(slots, dtype=jnp.int32) < tile_count[0, 0]
    row_ids, col_ids = tile_rows[0, 0], tile_cols[0, 0]
    col_owner = col_ids // phon_span
    row_owner = row_ids // elec_span
    row_z, row_core = row_owner // cores, row_owner % cores
    if n_el & (n_el - 1) == 0:
        phon_in = phon_out = col_owner ^ el_place
    else:
        phon_in, phon_out = (el_place - col_owner) % n_el, (col_owner - el_place) % n_el
    if n_z & (n_z - 1) == 0:
        elec_in = elec_out = row_z ^ z_place
    else:
        elec_in, elec_out = (z_place - row_z) % n_z, (row_z - z_place) % n_z
    other_core = (row_core != core_place).astype(jnp.int32)
    phon_in = phon_in * phon_span + col_ids % phon_span
    phon_out = phon_out * phon_span + col_ids % phon_span
    elec_in = (other_core * n_z + elec_in) * elec_span + row_ids % elec_span
    elec_out = (other_core * n_z + elec_out) * elec_span + row_ids % elec_span
    phon_out = jnp.where(live, phon_out, phon_blocks)
    elec_out = jnp.where(live, elec_out, elec_blocks)
    group_count = (tile_count[0] + (group - 1)) // group

    def over_el(values):
        return [
            send(value, "el", n_el, partner(n_el, step + 1)) for step, value in enumerate(values)
        ]

    def over_z(values):
        def place_of(step):
            z_of = partner(n_z, step)
            return lambda place: z_of(place // cores) * cores + place % cores

        return [send(value, "ph", n_ph, place_of(step + 1)) for step, value in enumerate(values)]

    def over_core(value):
        return send(value, "ph", n_ph, lambda place: place ^ 1)

    def spread_phon(value):
        return [value] + over_el([value] * (n_el - 1))

    def spread_elec(value):
        same_core = [value] + over_z([value] * (n_z - 1))
        if cores == 1:
            return same_core
        return same_core + [over_core(piece) for piece in same_core]

    def elec_sweep(phon_pieces):
        half = elec_blocks // cores
        halves = drag(
            phon_in, elec_out, group_count, tile_set, group, phon_pieces, True, [half] * cores, []
        )
        theirs = over_core(halves[1]) if cores == 2 else jnp.zeros_like(halves[0])
        own, *rest = pair_sum(halves[0], theirs, n_z - 1)
        coded, scales = over_z(rest[: n_z - 1]), over_z(rest[n_z - 1 :])
        return renew(elec_source, own, coded, scales, elec_rate)

    def phon_sweep(elec_pieces):
        own, *rest = drag(
            elec_in, phon_out, group_count, tile_set, group, elec_pieces, False,
            [phon_span], [phon_span] * (n_el - 1),
        )
        coded, scales = over_el(rest[: n_el - 1]), over_el(rest[n_el - 1 :])
        return renew(phon_source[0], own, coded, scales, phon_rate[0])

    elec_now, phon_now = elec_dev, phon_dev[0]
    for _ in range(ITERS):
        elec_pieces = spread_elec(elec_now.astype(jnp.bfloat16))
        phon_pieces = spread_phon(phon_now.astype(jnp.bfloat16))
        phon_now = phon_sweep(elec_pieces)
        elec_now = elec_sweep(phon_pieces)
    return (elec_now, phon_now[None])


def solution(mesh):
    in_specs = (
        P(("el", "ph"), None, None),
        P("ph", "el", None, None),
        P(("el", "ph"), None, None),
        P("ph", "el", None, None),
        P(("el", "ph"), None),
        P("ph", "el", None),
        P("el", "ph", None, None, None),
        P("el", "ph", None),
        P("el", "ph", None),
        P("el", "ph"),
    )
    out_specs = (P(("el", "ph"), None, None), P("ph", "el", None, None))
    body = functools.partial(local, mesh.shape["el"], mesh.shape["ph"])
    return jax.shard_map(body, mesh=mesh, in_specs=in_specs, out_specs=out_specs, check_vma=False)
```

time: 1230 us -> 372 us (0.30)
  waiting for transfers between devices: 1090 us -> 223 us
  starting transfers between devices: 0.49 us -> 112 us
  other arithmetic: 56.9 us -> 6.89 us
  local copies, waits for them, and re-layouts: 39.4 us -> 0.03 us
  Pallas kernels: 0 us -> 27.5 us
  matrix products: 19.6 us -> 0 us
  between operations: 14.9 us -> 1.59 us
    reduce_scatter x6 -> x0, waiting for transfers between devices: 893 us -> none  [the longest x3 721 us: local(): lax.psum_scatter(elec_drag, 'ph', scatter_dimension=0, tiled=True)]
    ppermute x0 -> x69, waiting for transfers between devices: none -> 223 us  [send(): lax.ppermute(value, axis, [(place, place_of(place)) for place in range(si...]
    all_gather x6 -> x0, waiting for transfers between devices: 194 us -> none  [the longest x2 78.6 us: local(): lax.all_gather(phon_now.astype(jnp.bfloat16), 'el', axis=0, tiled=True)]
    ppermute x0 -> x69, starting transfers between devices: none -> 112 us  [send(): lax.ppermute(value, axis, [(place, place_of(place)) for place in range(si...]
    scatter-add x12 -> x0, other arithmetic: 36.3 us -> none  [the longest x6 18.2 us: one_group(): elec_total = elec_total.at[group_rows].add(to_electron)]
    pallas_call x0 -> x9, Pallas kernels: none -> 27.5 us  [the longest x6 26.6 us: drag(): pl.pallas_call(functools.partial(drag_body, len(pieces), group, transpose...]
    gather x12 -> x0, local copies, waits for them, and re-layouts: 25.3 us -> none  [the longest x6 13.4 us: one_group(): phon_in = jnp.take(phon_blocks, group_cols, axis=0)]
    dot_general x12 -> x0, matrix products: 19.6 us -> none  [the longest x6 10.1 us: one_group(): jnp.einsum('tkb,tab->tka', phon_in, block_tiles, preferred_element_type=j...]
  transfers between devices with their start and end apart: 12 -> 69, of which waited for: 12 -> 25; matrix products, arithmetic and copies ran while one was open for 1% -> 0% of each run, Pallas kernels for 0% -> 4%
where the time goes in v1:
time: 372 us; the launch traced here: 371 us
  waiting for transfers between devices  223 us (60%)
  starting transfers between devices  112 us (30%)
  Pallas kernels  27.5 us (7%)
  other arithmetic  6.89 us (2%)
    ppermute x69, waiting for transfers between devices, send(): lax.ppermute(value, axis, [(place, place_of(place)) for place in range(si...  223 us
    ppermute x69, starting transfers between devices, send(): lax.ppermute(value, axis, [(place, place_of(place)) for place in range(si...  112 us
    pallas_call x6, Pallas kernels, drag(): pl.pallas_call(functools.partial(drag_body, len(pieces), group, transpose...  26.6 us
  transfers between devices with their start and end apart: 69, of which 25 were waited for; matrix products, arithmetic and copies ran while one was open for 0% of the time, Pallas kernels for 4%

profile of v1, /device:TPU:0, one launch (start us, length us, event | category | flops | bytes accessed | tf_op | source)
XLA Modules:
  0.0 371.4 jit_solution(6615444191901771868)
XLA Ops:
  13.1 8.8 %collective-permute-done.34.refs_6_ = bf16[4,96,256]{2,1,0:T(8,128)(2,1)S(1)} collective-permute-done((bf16[4,96,256]{2,1,0:T(8,128)(2,1)S(1)}, bf16[4,96,256]{2,1,0:T(8,128)(2,1)S(1)}, u32[]{:S(2)}, u32[]{:S(2)}) %collective-permute-start.34) | collective-permute-done | bytes 196640 | tf_op jit(solution)/shard_map/ppermute | solution.py:30
  23.6 5.3 %shard_map.118 = (f32[12,96,256]{2,1,0:T(8,128)S(1)}, s16[12,96,256]{2,1,0:T(8,128)(2,1)S(1)}, s16[12,96,256]{2,1,0:T(8,128)(2,1)S(1)}, s16[12,96,256]{2,1,0:T(8...) custom-call(s32[128]{0:T(128)S(1)} %get-tuple-element.107.refs_0_, ...), custom_call_target="tpu_custom_call" | custom-call | flops 1610612736 | bytes 16777216 | tf_op jit(solution)/shard_map/pallas_call | solution.py:124
  29.0 5.8 %collective-permute-start.40 = (s16[12,96,256]{2,1,0:T(8,128)(2,1)S(1)}, s16[12,96,256]{2,1,0:T(8,128)(2,1)S(1)}, u32[]{:S(2)}, u32[]{:S(2)}) collective-permute-start(s16[12,96,256]{2,1,0:T(8,128)(2,1)S(1)} %get-tuple-element.76), channel_id=1, source_target_pairs={{0,8},{8,0},{16,24},{24,16},{1,9},{9,1},{17,25},{25,17},{2,10},{10... | collective-permute-start | bytes 1769480 | tf_op jit(solution)/shard_map/ppermute | solution.py:30
  38.5 35.4 %collective-permute-done.41 = f32[12,256]{1,0:T(8,128)S(1)} collective-permute-done((f32[12,256]{1,0:T(8,128)S(1)}, f32[12,256]{1,0:T(8,128)S(1)}, u32[]{:S(2)}, u32[]{:S(2)}) %collective-permute-start.41) | collective-permute-done | bytes 12320 | tf_op jit(solution)/shard_map/ppermute | solution.py:30
  88.6 32.4 %collective-permute-done.1.refs_6_ = bf16[12,96,256]{2,1,0:T(8,128)(2,1)S(1)} collective-permute-done((bf16[12,96,256]{2,1,0:T(8,128)(2,1)S(1)}, bf16[12,96,256]{2,1,0:T(8,128)(2,1)S(1)}, u32[]{:S(2)}, u32[]{:S(2)}) %collective-permute-start.1) | collective-permute-done | bytes 589856 | tf_op jit(solution)/shard_map/ppermute | solution.py:30
  124.6 8.1 %collective-permute-done.47.refs_6_ = bf16[12,96,256]{2,1,0:T(8,128)(2,1)S(1)} collective-permute-done((bf16[12,96,256]{2,1,0:T(8,128)(2,1)S(1)}, bf16[12,96,256]{2,1,0:T(8,128)(2,1)S(1)}, u32[]{:S(2)}, u32[]{:S(2)}) %collective-permute-start.47) | collective-permute-done | bytes 589856 | tf_op jit(solution)/shard_map/ppermute | solution.py:30
  142.1 7.7 %collective-permute-start.6 = (s16[4,96,256]{2,1,0:T(8,128)(2,1)S(1)}, s16[4,96,256]{2,1,0:T(8,128)(2,1)S(1)}, u32[]{:S(2)}, u32[]{:S(2)}) collective-permute-start(s16[4,96,256]{2,1,0:T(8,128)(2,1)S(1)} %get-tuple-element.55), channel_id=1, source_target_pairs={{0,4},{1,5},{2,6},{3,7},{4,0},{5,1},{6,2},{7,3},{8,12},{9,13},{10,... | collective-permute-start | bytes 589832 | tf_op jit(solution)/shard_map/ppermute | solution.py:30
  149.8 5.8 %collective-permute-start.7 = (f32[4,256]{1,0:T(4,128)S(1)}, f32[4,256]{1,0:T(4,128)S(1)}, u32[]{:S(2)}, u32[]{:S(2)}) collective-permute-start(f32[4,256]{1,0:T(4,128)S(1)} %get-tuple-element.56), channel_id=1, source_target_pairs={{0,4},{1,5},{2,6},{3,7},{4,0},{5,1},{6,2},{7,3},{8,12},{9,13},{10,... | collective-permute-start | bytes 12296 | tf_op jit(solution)/shard_map/ppermute | solution.py:30
  156.3 11.4 %collective-permute-done.7 = f32[4,256]{1,0:T(4,128)S(1)} collective-permute-done((f32[4,256]{1,0:T(4,128)S(1)}, f32[4,256]{1,0:T(4,128)S(1)}, u32[]{:S(2)}, u32[]{:S(2)}) %collective-permute-start.7) | collective-permute-done | bytes 4128 | tf_op jit(solution)/shard_map/ppermute | solution.py:30
  182.5 5.1 %collective-permute-done.53 = f32[4,256]{1,0:T(4,128)S(1)} collective-permute-done((f32[4,256]{1,0:T(4,128)S(1)}, f32[4,256]{1,0:T(4,128)S(1)}, u32[]{:S(2)}, u32[]{:S(2)}) %collective-permute-start.53) | collective-permute-done | bytes 4128 | tf_op jit(solution)/shard_map/ppermute | solution.py:30
  195.7 9.3 %collective-permute-done.11.refs_6_ = bf16[4,96,256]{2,1,0:T(8,128)(2,1)S(1)} collective-permute-done((bf16[4,96,256]{2,1,0:T(8,128)(2,1)S(1)}, bf16[4,96,256]{2,1,0:T(8,128)(2,1)S(1)}, u32[]{:S(2)}, u32[]{:S(2)}) %collective-permute-start.11) | collective-permute-done | bytes 196640 | tf_op jit(solution)/shard_map/ppermute | solution.py:30
  206.8 5.3 %shard_map.115 = (f32[12,96,256]{2,1,0:T(8,128)S(1)}, s16[12,96,256]{2,1,0:T(8,128)(2,1)S(1)}, s16[12,96,256]{2,1,0:T(8,128)(2,1)S(1)}, s16[12,96,256]{2,1,0:T(8...) custom-call(s32[128]{0:T(128)S(1)} %get-tuple-element.107.refs_0_, ...), custom_call_target="tpu_custom_call" | custom-call | flops 1610612736 | bytes 16777216 | tf_op jit(solution)/shard_map/pallas_call | solution.py:124
  214.9 7.0 %collective-permute-start.57 = (bf16[4,96,256]{2,1,0:T(8,128)(2,1)S(1)}, bf16[4,96,256]{2,1,0:T(8,128)(2,1)S(1)}, u32[]{:S(2)}, u32[]{:S(2)}) collective-permute-start(bf16[4,96,256]{2,1,0:T(8,128)(2,1)S(1)} %get-tuple-element.104.refs_4_), channel_id=1, source_target_pairs={{0,4},{1,5},{2,6},{3,7},{4,0},{5,1},{6,2},{7,3},{8,12},{9,13},{10,... | collective-permute-start | bytes 589832 | tf_op jit(solution)/shard_map/ppermute | solution.py:30
  223.8 10.1 %collective-permute-done.57.refs_6_ = bf16[4,96,256]{2,1,0:T(8,128)(2,1)S(1)} collective-permute-done((bf16[4,96,256]{2,1,0:T(8,128)(2,1)S(1)}, bf16[4,96,256]{2,1,0:T(8,128)(2,1)S(1)}, u32[]{:S(2)}, u32[]{:S(2)}) %collective-permute-start.57) | collective-permute-done | bytes 196640 | tf_op jit(solution)/shard_map/ppermute | solution.py:30
  237.9 5.5 %shard_map.121 = (f32[12,96,256]{2,1,0:T(8,128)S(1)}, s16[12,96,256]{2,1,0:T(8,128)(2,1)S(1)}, s16[12,96,256]{2,1,0:T(8,128)(2,1)S(1)}, s16[12,96,256]{2,1,0:T(8...) custom-call(s32[128]{0:T(128)S(1)} %get-tuple-element.107.refs_0_, ...), custom_call_target="tpu_custom_call" | custom-call | flops 1610612736 | bytes 16777216 | tf_op jit(solution)/shard_map/pallas_call | solution.py:124
  243.4 5.9 %collective-permute-start.64 = (f32[12,256]{1,0:T(8,128)S(1)}, f32[12,256]{1,0:T(8,128)S(1)}, u32[]{:S(2)}, u32[]{:S(2)}) collective-permute-start(f32[12,256]{1,0:T(8,128)S(1)} %get-tuple-element.93), channel_id=1, source_target_pairs={{0,8},{8,0},{16,24},{24,16},{1,9},{9,1},{17,25},{25,17},{2,10},{10... | collective-permute-start | bytes 36872 | tf_op jit(solution)/shard_map/ppermute | solution.py:30
  254.3 9.0 %collective-permute-done.66 = f32[12,256]{1,0:T(8,128)S(1)} collective-permute-done((f32[12,256]{1,0:T(8,128)S(1)}, f32[12,256]{1,0:T(8,128)S(1)}, u32[]{:S(2)}, u32[]{:S(2)}) %collective-permute-start.66) | collective-permute-done | bytes 12320 | tf_op jit(solution)/shard_map/ppermute | solution.py:30
  266.8 24.4 %collective-permute-done.19 = s16[12,96,256]{2,1,0:T(8,128)(2,1)S(1)} collective-permute-done((s16[12,96,256]{2,1,0:T(8,128)(2,1)S(1)}, s16[12,96,256]{2,1,0:T(8,128)(2,1)S(1)}, u32[]{:S(2)}, u32[]{:S(2)}) %collective-permute-start.19) | collective-permute-done | bytes 589856 | tf_op jit(solution)/shard_map/ppermute | solution.py:30
  291.2 11.4 %collective-permute-done.65 = s16[12,96,256]{2,1,0:T(8,128)(2,1)S(1)} collective-permute-done((s16[12,96,256]{2,1,0:T(8,128)(2,1)S(1)}, s16[12,96,256]{2,1,0:T(8,128)(2,1)S(1)}, u32[]{:S(2)}, u32[]{:S(2)}) %collective-permute-start.65) | collective-permute-done | bytes 589856 | tf_op jit(solution)/shard_map/ppermute | solution.py:30
  308.8 12.8 %collective-permute-done.23.refs_5_ = bf16[12,96,256]{2,1,0:T(8,128)(2,1)S(1)} collective-permute-done((bf16[12,96,256]{2,1,0:T(8,128)(2,1)S(1)}, bf16[12,96,256]{2,1,0:T(8,128)(2,1)S(1)}, u32[]{:S(2)}, u32[]{:S(2)}) %collective-permute-start.23) | collective-permute-done | bytes 589856 | tf_op jit(solution)/shard_map/ppermute | solution.py:30
  321.5 10.6 %collective-permute-done.24.refs_6_ = bf16[12,96,256]{2,1,0:T(8,128)(2,1)S(1)} collective-permute-done((bf16[12,96,256]{2,1,0:T(8,128)(2,1)S(1)}, bf16[12,96,256]{2,1,0:T(8,128)(2,1)S(1)}, u32[]{:S(2)}, u32[]{:S(2)}) %collective-permute-start.24) | collective-permute-done | bytes 589856 | tf_op jit(solution)/shard_map/ppermute | solution.py:30
  339.5 7.3 %collective-permute-start.27 = (s16[4,96,256]{2,1,0:T(8,128)(2,1)S(1)}, s16[4,96,256]{2,1,0:T(8,128)(2,1)S(1)}, u32[]{:S(2)}, u32[]{:S(2)}) collective-permute-start(s16[4,96,256]{2,1,0:T(8,128)(2,1)S(1)} %get-tuple-element.69), channel_id=1, source_target_pairs={{0,2},{1,3},{2,0},{3,1},{4,6},{5,7},{6,4},{7,5},{8,10},{9,11},{10,... | collective-permute-start | bytes 589832 | tf_op jit(solution)/shard_map/ppermute | solution.py:30
  346.8 5.5 %collective-permute-start.29 = (s16[4,96,256]{2,1,0:T(8,128)(2,1)S(1)}, s16[4,96,256]{2,1,0:T(8,128)(2,1)S(1)}, u32[]{:S(2)}, u32[]{:S(2)}) collective-permute-start(s16[4,96,256]{2,1,0:T(8,128)(2,1)S(1)} %get-tuple-element.71), channel_id=1, source_target_pairs={{0,4},{1,5},{2,6},{3,7},{4,0},{5,1},{6,2},{7,3},{8,12},{9,13},{10,... | collective-permute-start | bytes 589832 | tf_op jit(solution)/shard_map/ppermute | solution.py:30
  361.1 5.6 %collective-permute-start.32 = (f32[4,256]{1,0:T(4,128)S(1)}, f32[4,256]{1,0:T(4,128)S(1)}, u32[]{:S(2)}, u32[]{:S(2)}) collective-permute-start(f32[4,256]{1,0:T(4,128)S(1)} %get-tuple-element.74), channel_id=1, source_target_pairs={{0,6},{1,7},{2,4},{3,5},{4,2},{5,3},{6,0},{7,1},{8,14},{9,15},{10,... | collective-permute-start | bytes 12296 | tf_op jit(solution)/shard_map/ppermute | solution.py:30
  (141 shorter events, 114.3 us)
Async XLA Ops:
  29.0 53.4 %collective-permute-start.40 = (s16[12,96,256]{2,1,0:T(8,128)(2,1)S(1)}, s16[12,96,256]{2,1,0:T(8,128)(2,1)S(1)}, u32[]{:S(2)}, u32[]{:S(2)}) collective-permute-start(s16[12,96,256]{2,1,0:T(8,128)(2,1)S(1)} %get-tuple-element.76), channel_id=1, source_target_pairs={{0,8},{8,0},{16,24},{24,16},{1,9},{9,1},{17,25},{25,17},{2,10},{10... | collective-permute-start | bytes 1769480 | tf_op jit(solution)/shard_map/ppermute | solution.py:30
  34.8 49.4 %collective-permute-start.42 = (s16[12,96,256]{2,1,0:T(8,128)(2,1)S(1)}, s16[12,96,256]{2,1,0:T(8,128)(2,1)S(1)}, u32[]{:S(2)}, u32[]{:S(2)}) collective-permute-start(s16[12,96,256]{2,1,0:T(8,128)(2,1)S(1)} %get-tuple-element.78), channel_id=1, source_target_pairs={{0,16},{8,24},{16,0},{24,8},{1,17},{9,25},{17,1},{25,9},{2,18},{10... | collective-permute-start | bytes 1769480 | tf_op jit(solution)/shard_map/ppermute | solution.py:30
  34.8 49.4 %collective-permute-start.44 = (s16[12,96,256]{2,1,0:T(8,128)(2,1)S(1)}, s16[12,96,256]{2,1,0:T(8,128)(2,1)S(1)}, u32[]{:S(2)}, u32[]{:S(2)}) collective-permute-start(s16[12,96,256]{2,1,0:T(8,128)(2,1)S(1)} %get-tuple-element.80), channel_id=1, source_target_pairs={{0,24},{8,16},{16,8},{24,0},{1,25},{9,17},{17,9},{25,1},{2,26},{10... | collective-permute-start | bytes 1769480 | tf_op jit(solution)/shard_map/ppermute | solution.py:30
  36.4 50.4 %collective-permute-start = (bf16[12,96,256]{2,1,0:T(8,128)(2,1)S(1)}, bf16[12,96,256]{2,1,0:T(8,128)(2,1)S(1)}, u32[]{:S(2)}, u32[]{:S(2)}) collective-permute-start(bf16[12,96,256]{2,1,0:T(8,128)(2,1)S(1)} %convert_bitcast_fusion.refs_4_), channel_id=1, source_target_pairs={{0,8},{8,0},{16,24},{24,16},{1,9},{9,1},{17,25},{25,17},{2,10},{10... | collective-permute-start | bytes 1769480 | tf_op jit(solution)/shard_map/ppermute | solution.py:30
  38.4 35.5 %collective-permute-start.41 = (f32[12,256]{1,0:T(8,128)S(1)}, f32[12,256]{1,0:T(8,128)S(1)}, u32[]{:S(2)}, u32[]{:S(2)}) collective-permute-start(f32[12,256]{1,0:T(8,128)S(1)} %get-tuple-element.77), channel_id=1, source_target_pairs={{0,8},{8,0},{16,24},{24,16},{1,9},{9,1},{17,25},{25,17},{2,10},{10... | collective-permute-start | bytes 36872 | tf_op jit(solution)/shard_map/ppermute | solution.py:30
  82.3 38.6 %collective-permute-start.1 = (bf16[12,96,256]{2,1,0:T(8,128)(2,1)S(1)}, bf16[12,96,256]{2,1,0:T(8,128)(2,1)S(1)}, u32[]{:S(2)}, u32[]{:S(2)}) collective-permute-start(bf16[12,96,256]{2,1,0:T(8,128)(2,1)S(1)} %convert_bitcast_fusion.refs_4_), channel_id=1, source_target_pairs={{0,16},{8,24},{16,0},{24,8},{1,17},{9,25},{17,1},{25,9},{2,18},{10... | collective-permute-start | bytes 1769480 | tf_op jit(solution)/shard_map/ppermute | solution.py:30
  82.4 38.6 %collective-permute-start.2 = (bf16[12,96,256]{2,1,0:T(8,128)(2,1)S(1)}, bf16[12,96,256]{2,1,0:T(8,128)(2,1)S(1)}, u32[]{:S(2)}, u32[]{:S(2)}) collective-permute-start(bf16[12,96,256]{2,1,0:T(8,128)(2,1)S(1)} %convert_bitcast_fusion.refs_4_), channel_id=1, source_target_pairs={{0,24},{8,16},{16,8},{24,0},{1,25},{9,17},{17,9},{25,1},{2,26},{10... | collective-permute-start | bytes 1769480 | tf_op jit(solution)/shard_map/ppermute | solution.py:30
  85.0 39.5 %collective-permute-start.46 = (bf16[12,96,256]{2,1,0:T(8,128)(2,1)S(1)}, bf16[12,96,256]{2,1,0:T(8,128)(2,1)S(1)}, u32[]{:S(2)}, u32[]{:S(2)}) collective-permute-start(bf16[12,96,256]{2,1,0:T(8,128)(2,1)S(1)} %fusion.3.refs_4_), channel_id=1, source_target_pairs={{0,8},{8,0},{16,24},{24,16},{1,9},{9,1},{17,25},{25,17},{2,10},{10... | collective-permute-start | bytes 1769480 | tf_op jit(solution)/shard_map/ppermute | solution.py:30
  86.8 45.9 %collective-permute-start.47 = (bf16[12,96,256]{2,1,0:T(8,128)(2,1)S(1)}, bf16[12,96,256]{2,1,0:T(8,128)(2,1)S(1)}, u32[]{:S(2)}, u32[]{:S(2)}) collective-permute-start(bf16[12,96,256]{2,1,0:T(8,128)(2,1)S(1)} %fusion.3.refs_4_), channel_id=1, source_target_pairs={{0,16},{8,24},{16,0},{24,8},{1,17},{9,25},{17,1},{25,9},{2,18},{10... | collective-permute-start | bytes 1769480 | tf_op jit(solution)/shard_map/ppermute | solution.py:30
  86.8 45.9 %collective-permute-start.48 = (bf16[12,96,256]{2,1,0:T(8,128)(2,1)S(1)}, bf16[12,96,256]{2,1,0:T(8,128)(2,1)S(1)}, u32[]{:S(2)}, u32[]{:S(2)}) collective-permute-start(bf16[12,96,256]{2,1,0:T(8,128)(2,1)S(1)} %fusion.3.refs_4_), channel_id=1, source_target_pairs={{0,24},{8,16},{16,8},{24,0},{1,25},{9,17},{17,9},{25,1},{2,26},{10... | collective-permute-start | bytes 1769480 | tf_op jit(solution)/shard_map/ppermute | solution.py:30
  140.0 30.8 %collective-permute-start.4 = (s16[4,96,256]{2,1,0:T(8,128)(2,1)S(1)}, s16[4,96,256]{2,1,0:T(8,128)(2,1)S(1)}, u32[]{:S(2)}, u32[]{:S(2)}) collective-permute-start(s16[4,96,256]{2,1,0:T(8,128)(2,1)S(1)} %get-tuple-element.53), channel_id=1, source_target_pairs={{0,2},{1,3},{2,0},{3,1},{4,6},{5,7},{6,4},{7,5},{8,10},{9,11},{10,... | collective-permute-start | bytes 589832 | tf_op jit(solution)/shard_map/ppermute | solution.py:30
  142.1 30.1 %collective-permute-start.6 = (s16[4,96,256]{2,1,0:T(8,128)(2,1)S(1)}, s16[4,96,256]{2,1,0:T(8,128)(2,1)S(1)}, u32[]{:S(2)}, u32[]{:S(2)}) collective-permute-start(s16[4,96,256]{2,1,0:T(8,128)(2,1)S(1)} %get-tuple-element.55), channel_id=1, source_target_pairs={{0,4},{1,5},{2,6},{3,7},{4,0},{5,1},{6,2},{7,3},{8,12},{9,13},{10,... | collective-permute-start | bytes 589832 | tf_op jit(solution)/shard_map/ppermute | solution.py:30
  149.8 22.4 %collective-permute-start.8 = (s16[4,96,256]{2,1,0:T(8,128)(2,1)S(1)}, s16[4,96,256]{2,1,0:T(8,128)(2,1)S(1)}, u32[]{:S(2)}, u32[]{:S(2)}) collective-permute-start(s16[4,96,256]{2,1,0:T(8,128)(2,1)S(1)} %get-tuple-element.57), channel_id=1, source_target_pairs={{0,6},{1,7},{2,4},{3,5},{4,2},{5,3},{6,0},{7,1},{8,14},{9,15},{10,... | collective-permute-start | bytes 589832 | tf_op jit(solution)/shard_map/ppermute | solution.py:30
  167.7 19.9 %collective-permute-start.50 = (s16[4,96,256]{2,1,0:T(8,128)(2,1)S(1)}, s16[4,96,256]{2,1,0:T(8,128)(2,1)S(1)}, u32[]{:S(2)}, u32[]{:S(2)}) collective-permute-start(s16[4,96,256]{2,1,0:T(8,128)(2,1)S(1)} %get-tuple-element.85), channel_id=1, source_target_pairs={{0,2},{1,3},{2,0},{3,1},{4,6},{5,7},{6,4},{7,5},{8,10},{9,11},{10,... | collective-permute-start | bytes 589832 | tf_op jit(solution)/shard_map/ppermute | solution.py:30
  212.1 51.2 %collective-permute-start.17 = (s16[12,96,256]{2,1,0:T(8,128)(2,1)S(1)}, s16[12,96,256]{2,1,0:T(8,128)(2,1)S(1)}, u32[]{:S(2)}, u32[]{:S(2)}) collective-permute-start(s16[12,96,256]{2,1,0:T(8,128)(2,1)S(1)} %get-tuple-element.60), channel_id=1, source_target_pairs={{0,8},{8,0},{16,24},{24,16},{1,9},{9,1},{17,25},{25,17},{2,10},{10... | collective-permute-start | bytes 1769480 | tf_op jit(solution)/shard_map/ppermute | solution.py:30
  250.9 40.4 %collective-permute-start.19 = (s16[12,96,256]{2,1,0:T(8,128)(2,1)S(1)}, s16[12,96,256]{2,1,0:T(8,128)(2,1)S(1)}, u32[]{:S(2)}, u32[]{:S(2)}) collective-permute-start(s16[12,96,256]{2,1,0:T(8,128)(2,1)S(1)} %get-tuple-element.62), channel_id=1, source_target_pairs={{0,16},{8,24},{16,0},{24,8},{1,17},{9,25},{17,1},{25,9},{2,18},{10... | collective-permute-start | bytes 1769480 | tf_op jit(solution)/shard_map/ppermute | solution.py:30
  251.4 39.8 %collective-permute-start.21 = (s16[12,96,256]{2,1,0:T(8,128)(2,1)S(1)}, s16[12,96,256]{2,1,0:T(8,128)(2,1)S(1)}, u32[]{:S(2)}, u32[]{:S(2)}) collective-permute-start(s16[12,96,256]{2,1,0:T(8,128)(2,1)S(1)} %get-tuple-element.64), channel_id=1, source_target_pairs={{0,24},{8,16},{16,8},{24,0},{1,25},{9,17},{17,9},{25,1},{2,26},{10... | collective-permute-start | bytes 1769480 | tf_op jit(solution)/shard_map/ppermute | solution.py:30
  263.3 27.9 %collective-permute-start.63 = (s16[12,96,256]{2,1,0:T(8,128)(2,1)S(1)}, s16[12,96,256]{2,1,0:T(8,128)(2,1)S(1)}, u32[]{:S(2)}, u32[]{:S(2)}) collective-permute-start(s16[12,96,256]{2,1,0:T(8,128)(2,1)S(1)} %get-tuple-element.92), channel_id=1, source_target_pairs={{0,8},{8,0},{16,24},{24,16},{1,9},{9,1},{17,25},{25,17},{2,10},{10... | collective-permute-start | bytes 1769480 | tf_op jit(solution)/shard_map/ppermute | solution.py:30
  263.3 39.3 %collective-permute-start.65 = (s16[12,96,256]{2,1,0:T(8,128)(2,1)S(1)}, s16[12,96,256]{2,1,0:T(8,128)(2,1)S(1)}, u32[]{:S(2)}, u32[]{:S(2)}) collective-permute-start(s16[12,96,256]{2,1,0:T(8,128)(2,1)S(1)} %get-tuple-element.94), channel_id=1, source_target_pairs={{0,16},{8,24},{16,0},{24,8},{1,17},{9,25},{17,1},{25,9},{2,18},{10... | collective-permute-start | bytes 1769480 | tf_op jit(solution)/shard_map/ppermute | solution.py:30
  263.3 39.3 %collective-permute-start.67 = (s16[12,96,256]{2,1,0:T(8,128)(2,1)S(1)}, s16[12,96,256]{2,1,0:T(8,128)(2,1)S(1)}, u32[]{:S(2)}, u32[]{:S(2)}) collective-permute-start(s16[12,96,256]{2,1,0:T(8,128)(2,1)S(1)} %get-tuple-element.96), channel_id=1, source_target_pairs={{0,24},{8,16},{16,8},{24,0},{1,25},{9,17},{17,9},{25,1},{2,26},{10... | collective-permute-start | bytes 1769480 | tf_op jit(solution)/shard_map/ppermute | solution.py:30
  305.6 26.5 %collective-permute-start.24 = (bf16[12,96,256]{2,1,0:T(8,128)(2,1)S(1)}, bf16[12,96,256]{2,1,0:T(8,128)(2,1)S(1)}, u32[]{:S(2)}, u32[]{:S(2)}) collective-permute-start(bf16[12,96,256]{2,1,0:T(8,128)(2,1)S(1)} %get-tuple-element.103.refs_4_), channel_id=1, source_target_pairs={{0,16},{8,24},{16,0},{24,8},{1,17},{9,25},{17,1},{25,9},{2,18},{10... | collective-permute-start | bytes 1769480 | tf_op jit(solution)/shard_map/ppermute | solution.py:30
  306.4 25.8 %collective-permute-start.25 = (bf16[12,96,256]{2,1,0:T(8,128)(2,1)S(1)}, bf16[12,96,256]{2,1,0:T(8,128)(2,1)S(1)}, u32[]{:S(2)}, u32[]{:S(2)}) collective-permute-start(bf16[12,96,256]{2,1,0:T(8,128)(2,1)S(1)} %get-tuple-element.103.refs_4_), channel_id=1, source_target_pairs={{0,24},{8,16},{16,8},{24,0},{1,25},{9,17},{17,9},{25,1},{2,26},{10... | collective-permute-start | bytes 1769480 | tf_op jit(solution)/shard_map/ppermute | solution.py:30
  339.5 30.9 %collective-permute-start.27 = (s16[4,96,256]{2,1,0:T(8,128)(2,1)S(1)}, s16[4,96,256]{2,1,0:T(8,128)(2,1)S(1)}, u32[]{:S(2)}, u32[]{:S(2)}) collective-permute-start(s16[4,96,256]{2,1,0:T(8,128)(2,1)S(1)} %get-tuple-element.69), channel_id=1, source_target_pairs={{0,2},{1,3},{2,0},{3,1},{4,6},{5,7},{6,4},{7,5},{8,10},{9,11},{10,... | collective-permute-start | bytes 589832 | tf_op jit(solution)/shard_map/ppermute | solution.py:30
  346.8 23.6 %collective-permute-start.29 = (s16[4,96,256]{2,1,0:T(8,128)(2,1)S(1)}, s16[4,96,256]{2,1,0:T(8,128)(2,1)S(1)}, u32[]{:S(2)}, u32[]{:S(2)}) collective-permute-start(s16[4,96,256]{2,1,0:T(8,128)(2,1)S(1)} %get-tuple-element.71), channel_id=1, source_target_pairs={{0,4},{1,5},{2,6},{3,7},{4,0},{5,1},{6,2},{7,3},{8,12},{9,13},{10,... | collective-permute-start | bytes 589832 | tf_op jit(solution)/shard_map/ppermute | solution.py:30
  (50 other events, 687.7 us)

commit v2 on v1

--- a/solution.py
+++ b/solution.py
@@ -10,7 +10,10 @@
 
 ITERS = 3
 DEPTH = 4
-LEVELS = 32767.0
+COST = 1024
+LEVELS = 32000.0
+HIGHEST = 126.0
+TAIL = 16
 SMALLEST = 1e-33
 
 
@@ -20,30 +23,48 @@
     return lambda place: (place + step) % size
 
 
-def source_of(size, step, place):
-    if size & (size - 1) == 0:
-        return place ^ step
-    return (place - step) % size
-
-
 def send(value, axis, size, place_of):
     return lax.ppermute(value, axis, [(place, place_of(place)) for place in range(size)])
 
 
-def encode(block):
-    peak = jnp.maximum(jnp.max(jnp.abs(block), axis=0, keepdims=True), SMALLEST)
-    coded = jnp.round(block * (LEVELS / peak)).astype(jnp.int32).astype(jnp.int16)
-    return coded, peak * (1.0 / LEVELS)
-
-
-def drag_body(piece_count, group, transposed, whole_outs, coded_outs, *refs):
+def encode_piece(block_of, size, coded):
+    rows, lanes = block_of(0).shape
+    row = lax.broadcasted_iota(jnp.int32, (TAIL, lanes), 0)
+    tails = [jnp.zeros((TAIL, lanes), jnp.float32) for _ in range(tail_rows(size) // TAIL)]
+    for index in range(size):
+        block = block_of(index)
+        peak = jnp.maximum(jnp.max(jnp.abs(block), axis=0, keepdims=True), SMALLEST)
+        power = jnp.minimum(jnp.floor(jnp.log2(peak)) + 1.0, HIGHEST)
+        scaled = jnp.round(block * (jnp.exp2(-power) * LEVELS))
+        coded[pl.ds(index * rows, rows), :] = scaled.astype(jnp.int32).astype(jnp.int16)
+        tails[index // TAIL] = jnp.where(row == index % TAIL, power, tails[index // TAIL])
+    for index, tail in enumerate(tails):
+        coded[pl.ds(size * rows + index * TAIL, TAIL), :] = tail.astype(jnp.int32).astype(jnp.int16)
+
+
+def scales_of(coded, size, rows):
+    tails = [
+        coded[pl.ds(size * rows + index * TAIL, TAIL), :].astype(jnp.int32).astype(jnp.float32)
+        for index in range(tail_rows(size) // TAIL)
+    ]
+    return [
+        jnp.exp2(tails[index // TAIL][index % TAIL : index % TAIL + 1]) * (1.0 / LEVELS)
+        for index in range(size)
+    ]
+
+
+def tail_rows(size):
+    return -(-size // TAIL) * TAIL
+
+
+def drag_body(piece_count, group, transposed, whole_outs, coded_sizes, *refs):
+    coded_outs = len(coded_sizes)
     ids_in, ids_out, group_count, tiles = refs[:4]
     pieces = refs[4 : 4 + piece_count]
     at = 4 + piece_count
     wholes = refs[at : at + whole_outs]
     coded = refs[at + whole_outs : at + whole_outs + coded_outs]
-    scales = refs[at + whole_outs + coded_outs : at + whole_outs + 2 * coded_outs]
-    vectors, totals, held, piece_sems, tile_sems, out_sems = refs[at + whole_outs + 2 * coded_outs :]
+    vectors, totals, held, piece_sems, tile_sems, out_sems = refs[at + whole_outs + coded_outs :]
     span = pieces[0].shape[0]
     loads = [
         pltpu.make_async_copy(
@@ -104,14 +125,15 @@
     for store in stores:
         store.start()
     for index in range(coded_outs):
-        size = coded[index].shape[0]
-        for block in range(size):
-            coded_block, scale = encode(totals[first + block])
-            coded[index][block] = coded_block
-            scales[index][pl.ds(block, 1)] = scale
+        size = coded_sizes[index]
+        encode_piece(lambda block, first=first: totals[first + block], size, coded[index])
         first += size
     for store in stores:
         store.wait()
+
+
+def coded_shape(size, rows, lanes):
+    return jax.ShapeDtypeStruct((size * rows + tail_rows(size), lanes), jnp.int16)
 
 
 def drag(ids_in, ids_out, group_count, tile_set, group, pieces, transposed, whole_sizes, coded_sizes):
@@ -123,13 +145,12 @@
     side = tile_set.shape[-1]
     return pl.pallas_call(
         functools.partial(
-            drag_body, len(pieces), group, transposed, len(whole_sizes), len(coded_sizes)
+            drag_body, len(pieces), group, transposed, len(whole_sizes), coded_sizes
         ),
         out_shape=[jax.ShapeDtypeStruct((size, rows, lanes), jnp.float32) for size in whole_sizes]
-        + [jax.ShapeDtypeStruct((size, rows, lanes), jnp.int16) for size in coded_sizes]
-        + [jax.ShapeDtypeStruct((size, lanes), jnp.float32) for size in coded_sizes],
+        + [coded_shape(size, rows, lanes) for size in coded_sizes],
         in_specs=[smem, smem, smem, any_space] + [any_space] * len(pieces),
-        out_specs=[any_space] * len(whole_sizes) + [vmem] * (2 * len(coded_sizes)),
+        out_specs=[any_space] * len(whole_sizes) + [vmem] * len(coded_sizes),
         scratch_shapes=[
             pltpu.VMEM((span * len(pieces), rows, lanes), jnp.bfloat16),
             pltpu.VMEM((blocks_out + 1, rows, lanes), jnp.float32),
@@ -139,24 +160,16 @@
             pltpu.SemaphoreType.DMA((max(len(whole_sizes), 1),)),
         ],
         compiler_params=pltpu.CompilerParams(vmem_limit_bytes=40 * 1024 * 1024),
-        cost_estimate=pl.CostEstimate(
-            flops=2 * tile_set.shape[0] * rows * side * side,
-            bytes_accessed=tile_set.shape[0] * side * side * 2,
-            transcendentals=0,
-        ),
+        cost_estimate=small_cost(),
     )(ids_in, ids_out, group_count, tile_set, *pieces)
 
 
-def pair_body(piece_count, mine, theirs, whole, *rest):
-    coded, scales = rest[:piece_count], rest[piece_count:]
+def pair_body(mine, theirs, whole, *coded):
     span = whole.shape[0]
     whole[...] = mine[pl.ds(0, span)] + theirs[pl.ds(0, span)]
-    for index in range(piece_count):
-        for block in range(span):
-            place = (index + 1) * span + block
-            coded_block, scale = encode(mine[place] + theirs[place])
-            coded[index][block] = coded_block
-            scales[index][pl.ds(block, 1)] = scale
+    for index, piece in enumerate(coded):
+        first = (index + 1) * span
+        encode_piece(lambda block, first=first: mine[first + block] + theirs[first + block], span, piece)
 
 
 def pair_sum(mine, theirs, piece_count):
@@ -164,21 +177,43 @@
     span = blocks // (piece_count + 1)
     vmem = pl.BlockSpec(memory_space=pltpu.VMEM)
     return pl.pallas_call(
-        functools.partial(pair_body, piece_count),
+        pair_body,
         out_shape=[jax.ShapeDtypeStruct((span, rows, lanes), jnp.float32)]
-        + [jax.ShapeDtypeStruct((span, rows, lanes), jnp.int16)] * piece_count
-        + [jax.ShapeDtypeStruct((span, lanes), jnp.float32)] * piece_count,
+        + [coded_shape(span, rows, lanes)] * piece_count,
         in_specs=[vmem, vmem],
-        out_specs=[vmem] * (1 + 2 * piece_count),
+        out_specs=[vmem] * (1 + piece_count),
         compiler_params=pltpu.CompilerParams(vmem_limit_bytes=32 * 1024 * 1024),
+        cost_estimate=small_cost(),
     )(mine, theirs)
 
 
-def renew(source, own, coded, scales, rate):
-    total = own
-    for values, scale in zip(coded, scales):
-        total = total + values.astype(jnp.float32) * scale[:, None, :]
-    return (source + total) / rate[:, None, :]
+def small_cost():
+    return pl.CostEstimate(flops=COST, bytes_accessed=COST, transcendentals=0)
+
+
+def renew_body(source, own, rate, *refs):
+    coded, result = refs[:-1], refs[-1]
+    size, rows, _ = own.shape
+    scales = [scales_of(piece, size, rows) for piece in coded]
+    for index in range(size):
+        total = own[index]
+        for piece, scale in zip(coded, scales):
+            values = piece[pl.ds(index * rows, rows), :].astype(jnp.int32).astype(jnp.float32)
+            total = total + values * scale[index]
+        fresh = (source[index] + total) / rate[pl.ds(index, 1), :]
+        result[index] = fresh.astype(result.dtype)
+
+
+def renew(source, own, coded, rate, dtype):
+    vmem = pl.BlockSpec(memory_space=pltpu.VMEM)
+    return pl.pallas_call(
+        renew_body,
+        out_shape=jax.ShapeDtypeStruct(own.shape, dtype),
+        in_specs=[vmem] * (3 + len(coded)),
+        out_specs=vmem,
+        compiler_params=pltpu.CompilerParams(vmem_limit_bytes=32 * 1024 * 1024),
+        cost_estimate=small_cost(),
+    )(source, own, rate, *coded)
 
 
 def local(
@@ -208,9 +243,6 @@
     ph_place = lax.axis_index("ph")
     z_place, core_place = ph_place // cores, ph_place % cores
 
-    def el_piece(owner):
-        return owner ^ el_place if n_el & (n_el - 1) == 0 else (el_place - owner) % n_el
-
     live = jnp.arange(slots, dtype=jnp.int32) < tile_count[0, 0]
     row_ids, col_ids = tile_rows[0, 0], tile_cols[0, 0]
     col_owner = col_ids // phon_span
@@ -257,30 +289,31 @@
             return same_core
         return same_core + [over_core(piece) for piece in same_core]
 
-    def elec_sweep(phon_pieces):
+    def after(values, first):
+        return list(lax.optimization_barrier((list(values), list(first)))[0])
+
+    elec_now, phon_now = elec_dev.astype(jnp.bfloat16), phon_dev[0].astype(jnp.bfloat16)
+    for sweep in range(ITERS):
+        dtype = jnp.bfloat16 if sweep + 1 < ITERS else jnp.float32
+        phon_pieces, elec_pieces = spread_phon(phon_now), spread_elec(elec_now)
+        elec_pieces = after(elec_pieces, phon_pieces[1:3])
+        phon_own, *phon_coded = drag(
+            elec_in, phon_out, group_count, tile_set, group, elec_pieces, False,
+            [phon_span], [phon_span] * (n_el - 1),
+        )
+        phon_pieces = after(phon_pieces, [phon_own])
         half = elec_blocks // cores
         halves = drag(
             phon_in, elec_out, group_count, tile_set, group, phon_pieces, True, [half] * cores, []
         )
         theirs = over_core(halves[1]) if cores == 2 else jnp.zeros_like(halves[0])
-        own, *rest = pair_sum(halves[0], theirs, n_z - 1)
-        coded, scales = over_z(rest[: n_z - 1]), over_z(rest[n_z - 1 :])
-        return renew(elec_source, own, coded, scales, elec_rate)
-
-    def phon_sweep(elec_pieces):
-        own, *rest = drag(
-            elec_in, phon_out, group_count, tile_set, group, elec_pieces, False,
-            [phon_span], [phon_span] * (n_el - 1),
-        )
-        coded, scales = over_el(rest[: n_el - 1]), over_el(rest[n_el - 1 :])
-        return renew(phon_source[0], own, coded, scales, phon_rate[0])
-
-    elec_now, phon_now = elec_dev, phon_dev[0]
-    for _ in range(ITERS):
-        elec_pieces = spread_elec(elec_now.astype(jnp.bfloat16))
-        phon_pieces = spread_phon(phon_now.astype(jnp.bfloat16))
-        phon_now = phon_sweep(elec_pieces)
-        elec_now = elec_sweep(phon_pieces)
+        elec_own, *elec_coded = pair_sum(halves[0], theirs, n_z - 1)
+        phon_coded = over_el(phon_coded)
+        elec_coded = over_z(elec_coded)
+        (phon_own,) = after([phon_own], [elec_own])
+        phon_now = renew(phon_source[0], phon_own, phon_coded, phon_rate[0], dtype)
+        (elec_own,) = after([elec_own], [phon_now])
+        elec_now = renew(elec_source, elec_own, elec_coded, elec_rate, dtype)
     return (elec_now, phon_now[None])
 
 

time: 372 us -> 235 us (0.63)
  the two profiles are of different devices: /device:TPU:0 before, /device:TPU:24 now
where the time goes in v2:
time: 235 us; the launch traced here: 234 us
  waiting for transfers between devices  117 us (50%)
  starting transfers between devices  70.7 us (30%)
  Pallas kernels  42.4 us (18%)
  other arithmetic  2.38 us (1%)
    ppermute x51, waiting for transfers between devices, send(): lax.ppermute(value, axis, [(place, place_of(place)) for place in range(si...  117 us
    ppermute x51, starting transfers between devices, send(): lax.ppermute(value, axis, [(place, place_of(place)) for place in range(si...  70.7 us
    pallas_call x6, Pallas kernels, drag(): pl.pallas_call(functools.partial(drag_body, len(pieces), group, transpose...  37.2 us
  transfers between devices with their start and end apart: 51, of which 24 were waited for; matrix products, arithmetic and copies ran while one was open for 1% of the time, Pallas kernels for 11%

profile of v2, /device:TPU:24, one launch (start us, length us, event | category | flops | bytes accessed | tf_op | source)
XLA Modules:
  0.0 234.3 jit_solution(12737123650701164428)
XLA Ops:
  11.4 7.0 %collective-permute-start.3 = (bf16[4,96,256]{2,1,0:T(8,128)(2,1)S(1)}, bf16[4,96,256]{2,1,0:T(8,128)(2,1)S(1)}, u32[]{:S(2)}, u32[]{:S(2)}) collective-permute-start(bf16[4,96,256]{2,1,0:T(8,128)(2,1)S(1)} %convert_element_type.12.refs_4_), channel_id=1, source_target_pairs={{0,2},{1,3},{2,0},{3,1},{4,6},{5,7},{6,4},{7,5},{8,10},{9,11},{10,... | collective-permute-start | bytes 589832 | tf_op jit(solution)/shard_map/ppermute | solution.py:27
  18.4 3.3 %collective-permute-done.4.refs_6_ = bf16[4,96,256]{2,1,0:T(8,128)(2,1)S(1)} collective-permute-done((bf16[4,96,256]{2,1,0:T(8,128)(2,1)S(1)}, bf16[4,96,256]{2,1,0:T(8,128)(2,1)S(1)}, u32[]{:S(2)}, u32[]{:S(2)}) %collective-permute-start.4) | collective-permute-done | bytes 196640 | tf_op jit(solution)/shard_map/ppermute | solution.py:27
  22.4 3.4 %collective-permute-done.3.refs_5_ = bf16[4,96,256]{2,1,0:T(8,128)(2,1)S(1)} collective-permute-done((bf16[4,96,256]{2,1,0:T(8,128)(2,1)S(1)}, bf16[4,96,256]{2,1,0:T(8,128)(2,1)S(1)}, u32[]{:S(2)}, u32[]{:S(2)}) %collective-permute-start.3) | collective-permute-done | bytes 196640 | tf_op jit(solution)/shard_map/ppermute | solution.py:27
  27.5 7.0 %shard_map.113 = (f32[12,96,256]{2,1,0:T(8,128)S(1)}, s16[1168,256]{1,0:T(8,128)(2,1)S(1)}, s16[1168,256]{1,0:T(8,128)(2,1)S(1)}, s16[1168,256]{1,0:T(8,128)(2,1)S(1)}) custom-call(s32[128]{0:T(128)S(1)} %get-tuple-element.151.refs_0_, s32[128]{0:T(128)S(1)} %get-tuple-element.146.refs_1_, s32[1]{0:T(128)S(6)} %select_n.61.refs_2_, ...), custom_call_target="tpu_custom_call" | custom-call | flops 1024 | bytes 1024 | tf_op jit(solution)/shard_map/pallas_call | solution.py:146
  34.6 5.4 %shard_map.114 = (f32[16,96,256]{2,1,0:T(8,128)S(1)}, f32[16,96,256]{2,1,0:T(8,128)S(1)}) custom-call(s32[128]{0:T(128)S(1)} %get-tuple-element.147.refs_0_, s32[128]{0:T(128)S(1)} %get-tuple-element.150.refs_1_, s32[1]{0:T(128)S(6)} %select_n.61.refs_2_, bf16[128,256,256]{2,1,0:T(8,128)(2,1)} %bitcast.50, ...), custom_call_target="tpu_custom_call" | custom-call | flops 1024 | bytes 1024 | tf_op jit(solution)/shard_map/pallas_call | solution.py:146
  41.8 10.5 %collective-permute-start.12 = (s16[1168,256]{1,0:T(8,128)(2,1)S(1)}, s16[1168,256]{1,0:T(8,128)(2,1)S(1)}, u32[]{:S(2)}, u32[]{:S(2)}) collective-permute-start(s16[1168,256]{1,0:T(8,128)(2,1)S(1)} %get-tuple-element.92), channel_id=1, source_target_pairs={{0,16},{8,24},{16,0},{24,8},{1,17},{9,25},{17,1},{25,9},{2,18},{10... | collective-permute-start | bytes 1794056 | tf_op jit(solution)/shard_map/ppermute | solution.py:27
  52.8 3.6 %collective-permute-done.11.refs_0_ = s16[1168,256]{1,0:T(8,128)(2,1)S(1)} collective-permute-done((s16[1168,256]{1,0:T(8,128)(2,1)S(1)}, s16[1168,256]{1,0:T(8,128)(2,1)S(1)}, u32[]{:S(2)}, u32[]{:S(2)}) %collective-permute-start.11) | collective-permute-done | bytes 598048 | tf_op jit(solution)/shard_map/ppermute | solution.py:27
  57.1 20.7 %collective-permute-done.12.refs_1_ = s16[1168,256]{1,0:T(8,128)(2,1)S(1)} collective-permute-done((s16[1168,256]{1,0:T(8,128)(2,1)S(1)}, s16[1168,256]{1,0:T(8,128)(2,1)S(1)}, u32[]{:S(2)}, u32[]{:S(2)}) %collective-permute-start.12) | collective-permute-done | bytes 598048 | tf_op jit(solution)/shard_map/ppermute | solution.py:27
  83.2 7.8 %collective-permute-done.19.refs_7_ = bf16[4,96,256]{2,1,0:T(8,128)(2,1)S(1)} collective-permute-done((bf16[4,96,256]{2,1,0:T(8,128)(2,1)S(1)}, bf16[4,96,256]{2,1,0:T(8,128)(2,1)S(1)}, u32[]{:S(2)}, u32[]{:S(2)}) %collective-permute-start.19) | collective-permute-done | bytes 196640 | tf_op jit(solution)/shard_map/ppermute | solution.py:27
  93.8 5.1 %collective-permute-done.18.refs_6_ = bf16[4,96,256]{2,1,0:T(8,128)(2,1)S(1)} collective-permute-done((bf16[4,96,256]{2,1,0:T(8,128)(2,1)S(1)}, bf16[4,96,256]{2,1,0:T(8,128)(2,1)S(1)}, u32[]{:S(2)}, u32[]{:S(2)}) %collective-permute-start.18) | collective-permute-done | bytes 196640 | tf_op jit(solution)/shard_map/ppermute | solution.py:27
  98.9 3.2 %collective-permute-done.17.refs_5_ = bf16[4,96,256]{2,1,0:T(8,128)(2,1)S(1)} collective-permute-done((bf16[4,96,256]{2,1,0:T(8,128)(2,1)S(1)}, bf16[4,96,256]{2,1,0:T(8,128)(2,1)S(1)}, u32[]{:S(2)}, u32[]{:S(2)}) %collective-permute-start.17) | collective-permute-done | bytes 196640 | tf_op jit(solution)/shard_map/ppermute | solution.py:27
  103.8 7.0 %shard_map.118 = (f32[12,96,256]{2,1,0:T(8,128)S(1)}, s16[1168,256]{1,0:T(8,128)(2,1)S(1)}, s16[1168,256]{1,0:T(8,128)(2,1)S(1)}, s16[1168,256]{1,0:T(8,128)(2,1)S(1)}) custom-call(s32[128]{0:T(128)S(1)} %get-tuple-element.151.refs_0_, s32[128]{0:T(128)S(1)} %get-tuple-element.146.refs_1_, s32[1]{0:T(128)S(6)} %select_n.61.refs_2_, ...), custom_call_target="tpu_custom_call" | custom-call | flops 1024 | bytes 1024 | tf_op jit(solution)/shard_map/pallas_call | solution.py:146
  110.8 5.4 %shard_map.119 = (f32[16,96,256]{2,1,0:T(8,128)S(1)}, f32[16,96,256]{2,1,0:T(8,128)S(1)}) custom-call(s32[128]{0:T(128)S(1)} %get-tuple-element.147.refs_0_, s32[128]{0:T(128)S(1)} %get-tuple-element.150.refs_1_, s32[1]{0:T(128)S(6)} %select_n.61.refs_2_, bf16[128,256,256]{2,1,0:T(8,128)(2,1)} %bitcast.52, bf16[12,96,256]{2,1,0:T(8,128)(2,1)S(1)} %shard_map.116.refs_4_, ...), custom_call_target="tpu_custom_call" | custom-call | flops 1024 | bytes 1024 | tf_op jit(solution)/shard_map/pallas_call | solution.py:146
  118.1 9.5 %collective-permute-start.29 = (s16[1168,256]{1,0:T(8,128)(2,1)S(1)}, s16[1168,256]{1,0:T(8,128)(2,1)S(1)}, u32[]{:S(2)}, u32[]{:S(2)}) collective-permute-start(s16[1168,256]{1,0:T(8,128)(2,1)S(1)} %get-tuple-element.116), channel_id=1, source_target_pairs={{0,16},{8,24},{16,0},{24,8},{1,17},{9,25},{17,1},{25,9},{2,18},{10... | collective-permute-start | bytes 1794056 | tf_op jit(solution)/shard_map/ppermute | solution.py:27
  129.4 3.2 %collective-permute-done.28.refs_0_ = s16[1168,256]{1,0:T(8,128)(2,1)S(1)} collective-permute-done((s16[1168,256]{1,0:T(8,128)(2,1)S(1)}, s16[1168,256]{1,0:T(8,128)(2,1)S(1)}, u32[]{:S(2)}, u32[]{:S(2)}) %collective-permute-start.28) | collective-permute-done | bytes 598048 | tf_op jit(solution)/shard_map/ppermute | solution.py:27
  133.3 19.8 %collective-permute-done.29.refs_1_ = s16[1168,256]{1,0:T(8,128)(2,1)S(1)} collective-permute-done((s16[1168,256]{1,0:T(8,128)(2,1)S(1)}, s16[1168,256]{1,0:T(8,128)(2,1)S(1)}, u32[]{:S(2)}, u32[]{:S(2)}) %collective-permute-start.29) | collective-permute-done | bytes 598048 | tf_op jit(solution)/shard_map/ppermute | solution.py:27
  159.8 6.4 %collective-permute-done.39.refs_7_ = bf16[4,96,256]{2,1,0:T(8,128)(2,1)S(1)} collective-permute-done((bf16[4,96,256]{2,1,0:T(8,128)(2,1)S(1)}, bf16[4,96,256]{2,1,0:T(8,128)(2,1)S(1)}, u32[]{:S(2)}, u32[]{:S(2)}) %collective-permute-start.39) | collective-permute-done | bytes 196640 | tf_op jit(solution)/shard_map/ppermute | solution.py:27
  166.2 5.4 %collective-permute-start.37 = (bf16[4,96,256]{2,1,0:T(8,128)(2,1)S(1)}, bf16[4,96,256]{2,1,0:T(8,128)(2,1)S(1)}, u32[]{:S(2)}, u32[]{:S(2)}) collective-permute-start(bf16[4,96,256]{2,1,0:T(8,128)(2,1)S(1)} %shard_map.122.refs_4_), channel_id=1, source_target_pairs={{0,2},{1,3},{2,0},{3,1},{4,6},{5,7},{6,4},{7,5},{8,10},{9,11},{10,... | collective-permute-start | bytes 589832 | tf_op jit(solution)/shard_map/ppermute | solution.py:27
  171.6 3.5 %collective-permute-done.38.refs_6_ = bf16[4,96,256]{2,1,0:T(8,128)(2,1)S(1)} collective-permute-done((bf16[4,96,256]{2,1,0:T(8,128)(2,1)S(1)}, bf16[4,96,256]{2,1,0:T(8,128)(2,1)S(1)}, u32[]{:S(2)}, u32[]{:S(2)}) %collective-permute-start.38) | collective-permute-done | bytes 196640 | tf_op jit(solution)/shard_map/ppermute | solution.py:27
  175.1 4.1 %collective-permute-done.37.refs_5_ = bf16[4,96,256]{2,1,0:T(8,128)(2,1)S(1)} collective-permute-done((bf16[4,96,256]{2,1,0:T(8,128)(2,1)S(1)}, bf16[4,96,256]{2,1,0:T(8,128)(2,1)S(1)}, u32[]{:S(2)}, u32[]{:S(2)}) %collective-permute-start.37) | collective-permute-done | bytes 196640 | tf_op jit(solution)/shard_map/ppermute | solution.py:27
  180.9 7.0 %shard_map.123 = (f32[12,96,256]{2,1,0:T(8,128)S(1)}, s16[1168,256]{1,0:T(8,128)(2,1)S(1)}, s16[1168,256]{1,0:T(8,128)(2,1)S(1)}, s16[1168,256]{1,0:T(8,128)(2,1)S(1)}) custom-call(s32[128]{0:T(128)S(1)} %get-tuple-element.151.refs_0_, s32[128]{0:T(128)S(1)} %get-tuple-element.146.refs_1_, s32[1]{0:T(128)S(6)} %select_n.61.refs_2_, ...), custom_call_target="tpu_custom_call" | custom-call | flops 1024 | bytes 1024 | tf_op jit(solution)/shard_map/pallas_call | solution.py:146
  188.0 5.4 %shard_map.124 = (f32[16,96,256]{2,1,0:T(8,128)S(1)}, f32[16,96,256]{2,1,0:T(8,128)S(1)}) custom-call(s32[128]{0:T(128)S(1)} %get-tuple-element.147.refs_0_, s32[128]{0:T(128)S(1)} %get-tuple-element.150.refs_1_, s32[1]{0:T(128)S(6)} %select_n.61.refs_2_, bf16[128,256,256]{2,1,0:T(8,128)(2,1)} %bitcast.54, bf16[12,96,256]{2,1,0:T(8,128)(2,1)S(1)} %shard_map.121.refs_4_, ...), custom_call_target="tpu_custom_call" | custom-call | flops 1024 | bytes 1024 | tf_op jit(solution)/shard_map/pallas_call | solution.py:146
  195.3 9.2 %collective-permute-start.46 = (s16[1168,256]{1,0:T(8,128)(2,1)S(1)}, s16[1168,256]{1,0:T(8,128)(2,1)S(1)}, u32[]{:S(2)}, u32[]{:S(2)}) collective-permute-start(s16[1168,256]{1,0:T(8,128)(2,1)S(1)} %get-tuple-element.140), channel_id=1, source_target_pairs={{0,16},{8,24},{16,0},{24,8},{1,17},{9,25},{17,1},{25,9},{2,18},{10... | collective-permute-start | bytes 1794056 | tf_op jit(solution)/shard_map/ppermute | solution.py:27
  210.3 19.8 %collective-permute-done.46.refs_1_ = s16[1168,256]{1,0:T(8,128)(2,1)S(1)} collective-permute-done((s16[1168,256]{1,0:T(8,128)(2,1)S(1)}, s16[1168,256]{1,0:T(8,128)(2,1)S(1)}, u32[]{:S(2)}, u32[]{:S(2)}) %collective-permute-start.46) | collective-permute-done | bytes 598048 | tf_op jit(solution)/shard_map/ppermute | solution.py:27
  (109 shorter events, 50.0 us)
Async XLA Ops:
  5.1 22.5 %collective-permute-start.1 = (bf16[12,96,256]{2,1,0:T(8,128)(2,1)S(1)}, bf16[12,96,256]{2,1,0:T(8,128)(2,1)S(1)}, u32[]{:S(2)}, u32[]{:S(2)}) collective-permute-start(bf16[12,96,256]{2,1,0:T(8,128)(2,1)S(1)} %convert_bitcast_fusion.refs_4_), channel_id=1, source_target_pairs={{0,16},{8,24},{16,0},{24,8},{1,17},{9,25},{17,1},{25,9},{2,18},{10... | collective-permute-start | bytes 1769480 | tf_op jit(solution)/shard_map/ppermute | solution.py:27
  6.7 20.9 %collective-permute-start = (bf16[12,96,256]{2,1,0:T(8,128)(2,1)S(1)}, bf16[12,96,256]{2,1,0:T(8,128)(2,1)S(1)}, u32[]{:S(2)}, u32[]{:S(2)}) collective-permute-start(bf16[12,96,256]{2,1,0:T(8,128)(2,1)S(1)} %convert_bitcast_fusion.refs_4_), channel_id=1, source_target_pairs={{0,8},{8,0},{16,24},{24,16},{1,9},{9,1},{17,25},{25,17},{2,10},{10... | collective-permute-start | bytes 1769480 | tf_op jit(solution)/shard_map/ppermute | solution.py:27
  8.2 26.4 %collective-permute-start.2 = (bf16[12,96,256]{2,1,0:T(8,128)(2,1)S(1)}, bf16[12,96,256]{2,1,0:T(8,128)(2,1)S(1)}, u32[]{:S(2)}, u32[]{:S(2)}) collective-permute-start(bf16[12,96,256]{2,1,0:T(8,128)(2,1)S(1)} %convert_bitcast_fusion.refs_4_), channel_id=1, source_target_pairs={{0,24},{8,16},{16,8},{24,0},{1,25},{9,17},{17,9},{25,1},{2,26},{10... | collective-permute-start | bytes 1769480 | tf_op jit(solution)/shard_map/ppermute | solution.py:27
  41.8 36.0 %collective-permute-start.12 = (s16[1168,256]{1,0:T(8,128)(2,1)S(1)}, s16[1168,256]{1,0:T(8,128)(2,1)S(1)}, u32[]{:S(2)}, u32[]{:S(2)}) collective-permute-start(s16[1168,256]{1,0:T(8,128)(2,1)S(1)} %get-tuple-element.92), channel_id=1, source_target_pairs={{0,16},{8,24},{16,0},{24,8},{1,17},{9,25},{17,1},{25,9},{2,18},{10... | collective-permute-start | bytes 1794056 | tf_op jit(solution)/shard_map/ppermute | solution.py:27
  52.2 26.3 %collective-permute-start.13 = (s16[1168,256]{1,0:T(8,128)(2,1)S(1)}, s16[1168,256]{1,0:T(8,128)(2,1)S(1)}, u32[]{:S(2)}, u32[]{:S(2)}) collective-permute-start(s16[1168,256]{1,0:T(8,128)(2,1)S(1)} %get-tuple-element.93), channel_id=1, source_target_pairs={{0,24},{8,16},{16,8},{24,0},{1,25},{9,17},{17,9},{25,1},{2,26},{10... | collective-permute-start | bytes 1794056 | tf_op jit(solution)/shard_map/ppermute | solution.py:27
  52.6 28.3 %collective-permute-start.14 = (s16[400,256]{1,0:T(8,128)(2,1)S(1)}, s16[400,256]{1,0:T(8,128)(2,1)S(1)}, u32[]{:S(2)}, u32[]{:S(2)}) collective-permute-start(s16[400,256]{1,0:T(8,128)(2,1)S(1)} %get-tuple-element.95), channel_id=1, source_target_pairs={{0,2},{1,3},{2,0},{3,1},{4,6},{5,7},{6,4},{7,5},{8,10},{9,11},{10,... | collective-permute-start | bytes 614408 | tf_op jit(solution)/shard_map/ppermute | solution.py:27
  52.7 28.2 %collective-permute-start.15 = (s16[400,256]{1,0:T(8,128)(2,1)S(1)}, s16[400,256]{1,0:T(8,128)(2,1)S(1)}, u32[]{:S(2)}, u32[]{:S(2)}) collective-permute-start(s16[400,256]{1,0:T(8,128)(2,1)S(1)} %get-tuple-element.96), channel_id=1, source_target_pairs={{0,4},{1,5},{2,6},{3,7},{4,0},{5,1},{6,2},{7,3},{8,12},{9,13},{10,... | collective-permute-start | bytes 614408 | tf_op jit(solution)/shard_map/ppermute | solution.py:27
  56.4 24.5 %collective-permute-start.16 = (s16[400,256]{1,0:T(8,128)(2,1)S(1)}, s16[400,256]{1,0:T(8,128)(2,1)S(1)}, u32[]{:S(2)}, u32[]{:S(2)}) collective-permute-start(s16[400,256]{1,0:T(8,128)(2,1)S(1)} %get-tuple-element.97), channel_id=1, source_target_pairs={{0,6},{1,7},{2,4},{3,5},{4,2},{5,3},{6,0},{7,1},{8,14},{9,15},{10,... | collective-permute-start | bytes 614408 | tf_op jit(solution)/shard_map/ppermute | solution.py:27
  79.1 23.0 %collective-permute-start.25 = (bf16[12,96,256]{2,1,0:T(8,128)(2,1)S(1)}, bf16[12,96,256]{2,1,0:T(8,128)(2,1)S(1)}, u32[]{:S(2)}, u32[]{:S(2)}) collective-permute-start(bf16[12,96,256]{2,1,0:T(8,128)(2,1)S(1)} %shard_map.116.refs_4_), channel_id=1, source_target_pairs={{0,16},{8,24},{16,0},{24,8},{1,17},{9,25},{17,1},{25,9},{2,18},{10... | collective-permute-start | bytes 1769480 | tf_op jit(solution)/shard_map/ppermute | solution.py:27
  81.3 21.3 %collective-permute-start.24 = (bf16[12,96,256]{2,1,0:T(8,128)(2,1)S(1)}, bf16[12,96,256]{2,1,0:T(8,128)(2,1)S(1)}, u32[]{:S(2)}, u32[]{:S(2)}) collective-permute-start(bf16[12,96,256]{2,1,0:T(8,128)(2,1)S(1)} %shard_map.116.refs_4_), channel_id=1, source_target_pairs={{0,8},{8,0},{16,24},{24,16},{1,9},{9,1},{17,25},{25,17},{2,10},{10... | collective-permute-start | bytes 1769480 | tf_op jit(solution)/shard_map/ppermute | solution.py:27
  81.9 28.9 %collective-permute-start.26 = (bf16[12,96,256]{2,1,0:T(8,128)(2,1)S(1)}, bf16[12,96,256]{2,1,0:T(8,128)(2,1)S(1)}, u32[]{:S(2)}, u32[]{:S(2)}) collective-permute-start(bf16[12,96,256]{2,1,0:T(8,128)(2,1)S(1)} %shard_map.116.refs_4_), channel_id=1, source_target_pairs={{0,24},{8,16},{16,8},{24,0},{1,25},{9,17},{17,9},{25,1},{2,26},{10... | collective-permute-start | bytes 1769480 | tf_op jit(solution)/shard_map/ppermute | solution.py:27
  118.1 35.1 %collective-permute-start.29 = (s16[1168,256]{1,0:T(8,128)(2,1)S(1)}, s16[1168,256]{1,0:T(8,128)(2,1)S(1)}, u32[]{:S(2)}, u32[]{:S(2)}) collective-permute-start(s16[1168,256]{1,0:T(8,128)(2,1)S(1)} %get-tuple-element.116), channel_id=1, source_target_pairs={{0,16},{8,24},{16,0},{24,8},{1,17},{9,25},{17,1},{25,9},{2,18},{10... | collective-permute-start | bytes 1794056 | tf_op jit(solution)/shard_map/ppermute | solution.py:27
  127.6 26.9 %collective-permute-start.30 = (s16[1168,256]{1,0:T(8,128)(2,1)S(1)}, s16[1168,256]{1,0:T(8,128)(2,1)S(1)}, u32[]{:S(2)}, u32[]{:S(2)}) collective-permute-start(s16[1168,256]{1,0:T(8,128)(2,1)S(1)} %get-tuple-element.117), channel_id=1, source_target_pairs={{0,24},{8,16},{16,8},{24,0},{1,25},{9,17},{17,9},{25,1},{2,26},{10... | collective-permute-start | bytes 1794056 | tf_op jit(solution)/shard_map/ppermute | solution.py:27
  128.6 27.7 %collective-permute-start.34 = (s16[400,256]{1,0:T(8,128)(2,1)S(1)}, s16[400,256]{1,0:T(8,128)(2,1)S(1)}, u32[]{:S(2)}, u32[]{:S(2)}) collective-permute-start(s16[400,256]{1,0:T(8,128)(2,1)S(1)} %get-tuple-element.119), channel_id=1, source_target_pairs={{0,2},{1,3},{2,0},{3,1},{4,6},{5,7},{6,4},{7,5},{8,10},{9,11},{10,... | collective-permute-start | bytes 614408 | tf_op jit(solution)/shard_map/ppermute | solution.py:27
  128.6 27.6 %collective-permute-start.35 = (s16[400,256]{1,0:T(8,128)(2,1)S(1)}, s16[400,256]{1,0:T(8,128)(2,1)S(1)}, u32[]{:S(2)}, u32[]{:S(2)}) collective-permute-start(s16[400,256]{1,0:T(8,128)(2,1)S(1)} %get-tuple-element.120), channel_id=1, source_target_pairs={{0,4},{1,5},{2,6},{3,7},{4,0},{5,1},{6,2},{7,3},{8,12},{9,13},{10,... | collective-permute-start | bytes 614408 | tf_op jit(solution)/shard_map/ppermute | solution.py:27
  132.7 23.6 %collective-permute-start.36 = (s16[400,256]{1,0:T(8,128)(2,1)S(1)}, s16[400,256]{1,0:T(8,128)(2,1)S(1)}, u32[]{:S(2)}, u32[]{:S(2)}) collective-permute-start(s16[400,256]{1,0:T(8,128)(2,1)S(1)} %get-tuple-element.121), channel_id=1, source_target_pairs={{0,6},{1,7},{2,4},{3,5},{4,2},{5,3},{6,0},{7,1},{8,14},{9,15},{10,... | collective-permute-start | bytes 614408 | tf_op jit(solution)/shard_map/ppermute | solution.py:27
  155.0 24.2 %collective-permute-start.32 = (bf16[12,96,256]{2,1,0:T(8,128)(2,1)S(1)}, bf16[12,96,256]{2,1,0:T(8,128)(2,1)S(1)}, u32[]{:S(2)}, u32[]{:S(2)}) collective-permute-start(bf16[12,96,256]{2,1,0:T(8,128)(2,1)S(1)} %shard_map.121.refs_4_), channel_id=1, source_target_pairs={{0,16},{8,24},{16,0},{24,8},{1,17},{9,25},{17,1},{25,9},{2,18},{10... | collective-permute-start | bytes 1769480 | tf_op jit(solution)/shard_map/ppermute | solution.py:27
  156.6 23.1 %collective-permute-start.31 = (bf16[12,96,256]{2,1,0:T(8,128)(2,1)S(1)}, bf16[12,96,256]{2,1,0:T(8,128)(2,1)S(1)}, u32[]{:S(2)}, u32[]{:S(2)}) collective-permute-start(bf16[12,96,256]{2,1,0:T(8,128)(2,1)S(1)} %shard_map.121.refs_4_), channel_id=1, source_target_pairs={{0,8},{8,0},{16,24},{24,16},{1,9},{9,1},{17,25},{25,17},{2,10},{10... | collective-permute-start | bytes 1769480 | tf_op jit(solution)/shard_map/ppermute | solution.py:27
  157.9 30.1 %collective-permute-start.33 = (bf16[12,96,256]{2,1,0:T(8,128)(2,1)S(1)}, bf16[12,96,256]{2,1,0:T(8,128)(2,1)S(1)}, u32[]{:S(2)}, u32[]{:S(2)}) collective-permute-start(bf16[12,96,256]{2,1,0:T(8,128)(2,1)S(1)} %shard_map.121.refs_4_), channel_id=1, source_target_pairs={{0,24},{8,16},{16,8},{24,0},{1,25},{9,17},{17,9},{25,1},{2,26},{10... | collective-permute-start | bytes 1769480 | tf_op jit(solution)/shard_map/ppermute | solution.py:27
  195.3 34.8 %collective-permute-start.46 = (s16[1168,256]{1,0:T(8,128)(2,1)S(1)}, s16[1168,256]{1,0:T(8,128)(2,1)S(1)}, u32[]{:S(2)}, u32[]{:S(2)}) collective-permute-start(s16[1168,256]{1,0:T(8,128)(2,1)S(1)} %get-tuple-element.140), channel_id=1, source_target_pairs={{0,16},{8,24},{16,0},{24,8},{1,17},{9,25},{17,1},{25,9},{2,18},{10... | collective-permute-start | bytes 1794056 | tf_op jit(solution)/shard_map/ppermute | solution.py:27
  204.6 27.2 %collective-permute-start.47 = (s16[1168,256]{1,0:T(8,128)(2,1)S(1)}, s16[1168,256]{1,0:T(8,128)(2,1)S(1)}, u32[]{:S(2)}, u32[]{:S(2)}) collective-permute-start(s16[1168,256]{1,0:T(8,128)(2,1)S(1)} %get-tuple-element.141), channel_id=1, source_target_pairs={{0,24},{8,16},{16,8},{24,0},{1,25},{9,17},{17,9},{25,1},{2,26},{10... | collective-permute-start | bytes 1794056 | tf_op jit(solution)/shard_map/ppermute | solution.py:27
  205.8 27.5 %collective-permute-start.48 = (s16[400,256]{1,0:T(8,128)(2,1)S(1)}, s16[400,256]{1,0:T(8,128)(2,1)S(1)}, u32[]{:S(2)}, u32[]{:S(2)}) collective-permute-start(s16[400,256]{1,0:T(8,128)(2,1)S(1)} %get-tuple-element.143), channel_id=1, source_target_pairs={{0,2},{1,3},{2,0},{3,1},{4,6},{5,7},{6,4},{7,5},{8,10},{9,11},{10,... | collective-permute-start | bytes 614408 | tf_op jit(solution)/shard_map/ppermute | solution.py:27
  205.9 27.4 %collective-permute-start.49 = (s16[400,256]{1,0:T(8,128)(2,1)S(1)}, s16[400,256]{1,0:T(8,128)(2,1)S(1)}, u32[]{:S(2)}, u32[]{:S(2)}) collective-permute-start(s16[400,256]{1,0:T(8,128)(2,1)S(1)} %get-tuple-element.144), channel_id=1, source_target_pairs={{0,4},{1,5},{2,6},{3,7},{4,0},{5,1},{6,2},{7,3},{8,12},{9,13},{10,... | collective-permute-start | bytes 614408 | tf_op jit(solution)/shard_map/ppermute | solution.py:27
  209.8 23.5 %collective-permute-start.50 = (s16[400,256]{1,0:T(8,128)(2,1)S(1)}, s16[400,256]{1,0:T(8,128)(2,1)S(1)}, u32[]{:S(2)}, u32[]{:S(2)}) collective-permute-start(s16[400,256]{1,0:T(8,128)(2,1)S(1)} %get-tuple-element.145), channel_id=1, source_target_pairs={{0,6},{1,7},{2,4},{3,5},{4,2},{5,3},{6,0},{7,1},{8,14},{9,15},{10,... | collective-permute-start | bytes 614408 | tf_op jit(solution)/shard_map/ppermute | solution.py:27
  (33 other events, 325.0 us)

commit v3 on v2

--- a/solution.py
+++ b/solution.py
@@ -14,6 +14,8 @@
 LEVELS = 32000.0
 HIGHEST = 126.0
 TAIL = 16
+TIES = 3
+FORWARD = True
 SMALLEST = 1e-33
 
 
@@ -57,23 +59,25 @@
     return -(-size // TAIL) * TAIL
 
 
-def drag_body(piece_count, group, transposed, whole_outs, coded_sizes, *refs):
-    coded_outs = len(coded_sizes)
-    ids_in, ids_out, group_count, tiles = refs[:4]
-    pieces = refs[4 : 4 + piece_count]
-    at = 4 + piece_count
-    wholes = refs[at : at + whole_outs]
-    coded = refs[at + whole_outs : at + whole_outs + coded_outs]
-    vectors, totals, held, piece_sems, tile_sems, out_sems = refs[at + whole_outs + coded_outs :]
-    span = pieces[0].shape[0]
-    loads = [
-        pltpu.make_async_copy(
-            pieces[index], vectors.at[pl.ds(index * span, span)], piece_sems.at[index]
-        )
-        for index in range(piece_count)
-    ]
-    for load in loads:
-        load.start()
+def drags_body(group, counts, *refs):
+    elec_pieces, phon_pieces, elec_parts, phon_parts = counts
+    elec_in, elec_out, phon_in, phon_out, group_count, tiles = refs[:6]
+    refs = refs[6:]
+    sources, refs = refs[: elec_pieces + phon_pieces], refs[elec_pieces + phon_pieces :]
+    halves, refs = refs[:elec_parts], refs[elec_parts:]
+    whole, coded, refs = refs[0], refs[1:phon_parts], refs[phon_parts:]
+    elec, phon, elec_totals, phon_totals, held, source_sems, tile_sems, out_sems = refs
+    loads = []
+    for target, pieces in ((elec, sources[:elec_pieces]), (phon, sources[elec_pieces:])):
+        first = 0
+        for piece in pieces:
+            span = piece.shape[0]
+            loads.append(
+                pltpu.make_async_copy(
+                    piece, target.at[pl.ds(first, span)], source_sems.at[len(loads)]
+                )
+            )
+            first += span
     groups = group_count[0]
 
     def fetch(index):
@@ -88,7 +92,10 @@
         def _():
             fetch(ahead).start()
 
-    totals[...] = jnp.zeros_like(totals)
+    for load in loads:
+        load.start()
+    elec_totals[...] = jnp.zeros_like(elec_totals)
+    phon_totals[...] = jnp.zeros_like(phon_totals)
     for load in loads:
         load.wait()
 
@@ -101,43 +108,90 @@
         slot = lax.rem(index, DEPTH)
         for inner in range(group):
             place = index * group + inner
-            product = lax.dot_general(
-                vectors[ids_in[place]],
-                held[slot, inner],
-                (((1,), (1 if transposed else 0,)), ((), ())),
+            tile = held[slot, inner]
+            to_phon = lax.dot_general(
+                elec[elec_in[place]], tile, (((1,), (0,)), ((), ())),
                 preferred_element_type=jnp.float32,
             )
-            target = ids_out[place]
-            totals[target] = totals[target] + product
+            to_elec = lax.dot_general(
+                phon[phon_in[place]], tile, (((1,), (1,)), ((), ())),
+                preferred_element_type=jnp.float32,
+            )
+            target = phon_out[place]
+            phon_totals[target] = phon_totals[target] + to_phon
+            target = elec_out[place]
+            elec_totals[target] = elec_totals[target] + to_elec
         return carry
 
     lax.fori_loop(0, groups, one_group, 0)
-    stores = []
-    first = 0
-    for index in range(whole_outs):
-        size = wholes[index].shape[0]
+    stores, first = [], 0
+    for half in halves:
+        size = half.shape[0]
         stores.append(
             pltpu.make_async_copy(
-                totals.at[pl.ds(first, size)], wholes[index], out_sems.at[index]
+                elec_totals.at[pl.ds(first, size)], half, out_sems.at[len(stores)]
             )
         )
         first += size
+    span = whole.shape[0]
+    stores.append(
+        pltpu.make_async_copy(phon_totals.at[pl.ds(0, span)], whole, out_sems.at[len(stores)])
+    )
     for store in stores:
         store.start()
-    for index in range(coded_outs):
-        size = coded_sizes[index]
-        encode_piece(lambda block, first=first: totals[first + block], size, coded[index])
-        first += size
+    for index, piece in enumerate(coded):
+        first = (index + 1) * span
+        encode_piece(lambda block, first=first: phon_totals[first + block], span, piece)
     for store in stores:
         store.wait()
 
 
+def drags(ids, tile_set, group, elec_pieces, phon_pieces, elec_parts, phon_parts):
+    _, rows, lanes = elec_pieces[0].shape
+    side = tile_set.shape[-1]
+    elec_blocks = sum(piece.shape[0] for piece in elec_pieces)
+    phon_blocks = sum(piece.shape[0] for piece in phon_pieces)
+    half, span = elec_blocks // elec_parts, phon_blocks // phon_parts
+    any_space = pl.BlockSpec(memory_space=pl.ANY)
+    smem = pl.BlockSpec(memory_space=pltpu.SMEM)
+    vmem = pl.BlockSpec(memory_space=pltpu.VMEM)
+    pieces = list(elec_pieces) + list(phon_pieces)
+    outs = pl.pallas_call(
+        functools.partial(
+            drags_body, group, (len(elec_pieces), len(phon_pieces), elec_parts, phon_parts)
+        ),
+        out_shape=[jax.ShapeDtypeStruct((half, rows, lanes), jnp.float32)] * elec_parts
+        + [jax.ShapeDtypeStruct((span, rows, lanes), jnp.float32)]
+        + [coded_shape(span, rows, lanes)] * (phon_parts - 1),
+        in_specs=[smem] * 5 + [any_space] * (1 + len(pieces)),
+        out_specs=[any_space] * (elec_parts + 1) + [vmem] * (phon_parts - 1),
+        scratch_shapes=[
+            pltpu.VMEM((elec_blocks, rows, lanes), jnp.bfloat16),
+            pltpu.VMEM((phon_blocks, rows, lanes), jnp.bfloat16),
+            pltpu.VMEM((elec_blocks + 1, rows, lanes), jnp.float32),
+            pltpu.VMEM((phon_blocks + 1, rows, lanes), jnp.float32),
+            pltpu.VMEM((DEPTH, group, side, side), jnp.bfloat16),
+            pltpu.SemaphoreType.DMA((len(pieces),)),
+            pltpu.SemaphoreType.DMA((DEPTH,)),
+            pltpu.SemaphoreType.DMA((elec_parts + 1,)),
+        ],
+        compiler_params=pltpu.CompilerParams(vmem_limit_bytes=40 * 1024 * 1024),
+        cost_estimate=pl.CostEstimate(
+            flops=4 * tile_set.shape[0] * rows * side * side,
+            bytes_accessed=2 * tile_set.shape[0] * side * side * 2,
+            transcendentals=0,
+        ),
+    )(*ids, tile_set, *pieces)
+    return outs[:elec_parts], outs[elec_parts], outs[elec_parts + 1 :]
+
+
 def coded_shape(size, rows, lanes):
     return jax.ShapeDtypeStruct((size * rows + tail_rows(size), lanes), jnp.int16)
 
 
 def drag(ids_in, ids_out, group_count, tile_set, group, pieces, transposed, whole_sizes, coded_sizes):
-    span, rows, lanes = pieces[0].shape
+    _, rows, lanes = pieces[0].shape
+    blocks_in = sum(piece.shape[0] for piece in pieces)
     blocks_out = sum(whole_sizes) + sum(coded_sizes)
     any_space = pl.BlockSpec(memory_space=pl.ANY)
     smem = pl.BlockSpec(memory_space=pltpu.SMEM)
@@ -152,7 +206,7 @@
         in_specs=[smem, smem, smem, any_space] + [any_space] * len(pieces),
         out_specs=[any_space] * len(whole_sizes) + [vmem] * len(coded_sizes),
         scratch_shapes=[
-            pltpu.VMEM((span * len(pieces), rows, lanes), jnp.bfloat16),
+            pltpu.VMEM((blocks_in, rows, lanes), jnp.bfloat16),
             pltpu.VMEM((blocks_out + 1, rows, lanes), jnp.float32),
             pltpu.VMEM((DEPTH, group, side, side), jnp.bfloat16),
             pltpu.SemaphoreType.DMA((len(pieces),)),
@@ -160,7 +214,11 @@
             pltpu.SemaphoreType.DMA((max(len(whole_sizes), 1),)),
         ],
         compiler_params=pltpu.CompilerParams(vmem_limit_bytes=40 * 1024 * 1024),
-        cost_estimate=small_cost(),
+        cost_estimate=pl.CostEstimate(
+            flops=2 * tile_set.shape[0] * rows * side * side,
+            bytes_accessed=2 * tile_set.shape[0] * side * side * 2,
+            transcendentals=0,
+        ),
     )(ids_in, ids_out, group_count, tile_set, *pieces)
 
 
@@ -265,6 +323,9 @@
     elec_out = jnp.where(live, elec_out, elec_blocks)
     group_count = (tile_count[0] + (group - 1)) // group
 
+    def after(values, first):
+        return list(lax.optimization_barrier((list(values), list(first)))[0])
+
     def over_el(values):
         return [
             send(value, "el", n_el, partner(n_el, step + 1)) for step, value in enumerate(values)
@@ -281,36 +342,37 @@
         return send(value, "ph", n_ph, lambda place: place ^ 1)
 
     def spread_phon(value):
-        return [value] + over_el([value] * (n_el - 1))
-
-    def spread_elec(value):
+        half = phon_span // 2
+        if FORWARD and n_el == 4 and half:
+            near, far = over_el([value] * 2)
+            halves = after([far[:half], near[half:]], [near, far])
+            passed = [
+                send(piece, "el", n_el, partner(n_el, step + 1)) for step, piece in enumerate(halves)
+            ]
+            return [value, near, far, *passed], halves
+        pieces = [value] + over_el([value] * (n_el - 1))
+        return pieces, pieces[1:2]
+
+    def spread_elec(value, first):
         same_core = [value] + over_z([value] * (n_z - 1))
         if cores == 1:
             return same_core
-        return same_core + [over_core(piece) for piece in same_core]
-
-    def after(values, first):
-        return list(lax.optimization_barrier((list(values), list(first)))[0])
-
+        others = after(same_core[1:], first)
+        return same_core + [over_core(piece) for piece in [value] + others]
+
+    ids = (elec_in, elec_out, phon_in, phon_out, group_count)
     elec_now, phon_now = elec_dev.astype(jnp.bfloat16), phon_dev[0].astype(jnp.bfloat16)
     for sweep in range(ITERS):
         dtype = jnp.bfloat16 if sweep + 1 < ITERS else jnp.float32
-        phon_pieces, elec_pieces = spread_phon(phon_now), spread_elec(elec_now)
-        elec_pieces = after(elec_pieces, phon_pieces[1:3])
-        phon_own, *phon_coded = drag(
-            elec_in, phon_out, group_count, tile_set, group, elec_pieces, False,
-            [phon_span], [phon_span] * (n_el - 1),
-        )
-        phon_pieces = after(phon_pieces, [phon_own])
-        half = elec_blocks // cores
-        halves = drag(
-            phon_in, elec_out, group_count, tile_set, group, phon_pieces, True, [half] * cores, []
+        phon_pieces, passed = spread_phon(phon_now)
+        elec_pieces = spread_elec(elec_now, passed)
+        halves, phon_own, phon_coded = drags(
+            ids, tile_set, group, elec_pieces, phon_pieces, cores, n_el
         )
         theirs = over_core(halves[1]) if cores == 2 else jnp.zeros_like(halves[0])
         elec_own, *elec_coded = pair_sum(halves[0], theirs, n_z - 1)
-        phon_coded = over_el(phon_coded)
-        elec_coded = over_z(elec_coded)
-        (phon_own,) = after([phon_own], [elec_own])
+        phon_coded, elec_coded = over_el(phon_coded), over_z(elec_coded)
+        (phon_own,) = after([phon_own], [elec_own, *elec_coded[:TIES]])
         phon_now = renew(phon_source[0], phon_own, phon_coded, phon_rate[0], dtype)
         (elec_own,) = after([elec_own], [phon_now])
         elec_now = renew(elec_source, elec_own, elec_coded, elec_rate, dtype)

time: 235 us -> 215 us (0.915)
  the two profiles are of different devices: /device:TPU:24 before, /device:TPU:0 now
where the time goes in v3:
time: 215 us
  waiting for transfers between devices  107 us (50%)
  starting transfers between devices  79.1 us (37%)
  Pallas kernels  23.9 us (11%)
    ppermute x54, waiting for transfers between devices, send(): lax.ppermute(value, axis, [(place, place_of(place)) for place in range(si...  107 us
    ppermute x54, starting transfers between devices, send(): lax.ppermute(value, axis, [(place, place_of(place)) for place in range(si...  79.1 us
    pallas_call x3, Pallas kernels, drags(): pl.pallas_call(functools.partial(drags_body, group, (len(elec_pieces), le...  18.7 us
  transfers between devices with their start and end apart: 54, of which 39 were waited for; matrix products, arithmetic and copies ran while one was open for 1% of the time, Pallas kernels for 1%

profile of v3, /device:TPU:0, one launch (start us, length us, event | category | flops | bytes accessed | tf_op | source)
XLA Modules:
  0.0 214.9 jit_solution(2189041474359194798)
XLA Ops:
  6.6 3.7 %collective-permute-start.2 = (bf16[4,96,256]{2,1,0:T(8,128)(2,1)S(1)}, bf16[4,96,256]{2,1,0:T(8,128)(2,1)S(1)}, u32[]{:S(2)}, u32[]{:S(2)}) collective-permute-start(bf16[4,96,256]{2,1,0:T(8,128)(2,1)S(1)} %convert_element_type.9.refs_6_), channel_id=1, source_target_pairs={{0,6},{1,7},{2,4},{3,5},{4,2},{5,3},{6,0},{7,1},{8,14},{9,15},{10,... | collective-permute-start | bytes 589832 | tf_op jit(solution)/shard_map/ppermute | solution.py:29
  11.1 7.3 %collective-permute-done.5.refs_15_ = bf16[12,96,256]{2,1,0:T(8,128)(2,1)S(1)} collective-permute-done((bf16[12,96,256]{2,1,0:T(8,128)(2,1)S(1)}, bf16[12,96,256]{2,1,0:T(8,128)(2,1)S(1)}, u32[]{:S(2)}, u32[]{:S(2)}) %collective-permute-start.5) | collective-permute-done | bytes 589856 | tf_op jit(solution)/shard_map/ppermute | solution.py:29
  30.9 6.2 %shard_map.113 = (f32[16,96,256]{2,1,0:T(8,128)S(1)}, f32[16,96,256]{2,1,0:T(8,128)S(1)}, f32[12,96,256]{2,1,0:T(8,128)S(1)}, s16[1168,256]{1,0:T(8,128)(2,1)S(1...) custom-call(s32[128]{0:T(128)S(1)} %get-tuple-element.109.refs_0_, s32[128]{0:T(128)S(1)} %get-tuple-element.108.refs_1_, ...), custom_call_target="tpu_custom_call" | custom-call | flops 3221225472 | bytes 33554432 | tf_op jit(solution)/shard_map/pallas_call | solution.py:159
  38.3 9.1 %collective-permute-start.16 = (s16[1168,256]{1,0:T(8,128)(2,1)S(1)}, s16[1168,256]{1,0:T(8,128)(2,1)S(1)}, u32[]{:S(2)}, u32[]{:S(2)}) collective-permute-start(s16[1168,256]{1,0:T(8,128)(2,1)S(1)} %get-tuple-element.67), channel_id=1, source_target_pairs={{0,16},{8,24},{16,0},{24,8},{1,17},{9,25},{17,1},{25,9},{2,18},{10... | collective-permute-start | bytes 1794056 | tf_op jit(solution)/shard_map/ppermute | solution.py:29
  49.3 3.4 %collective-permute-start.13 = (s16[400,256]{1,0:T(8,128)(2,1)S(1)}, s16[400,256]{1,0:T(8,128)(2,1)S(1)}, u32[]{:S(2)}, u32[]{:S(2)}) collective-permute-start(s16[400,256]{1,0:T(8,128)(2,1)S(1)} %get-tuple-element.63), channel_id=1, source_target_pairs={{0,4},{1,5},{2,6},{3,7},{4,0},{5,1},{6,2},{7,3},{8,12},{9,13},{10,... | collective-permute-start | bytes 614408 | tf_op jit(solution)/shard_map/ppermute | solution.py:29
  52.6 7.3 %collective-permute-done.12.refs_0_ = s16[400,256]{1,0:T(8,128)(2,1)S(1)} collective-permute-done((s16[400,256]{1,0:T(8,128)(2,1)S(1)}, s16[400,256]{1,0:T(8,128)(2,1)S(1)}, u32[]{:S(2)}, u32[]{:S(2)}) %collective-permute-start.12) | collective-permute-done | bytes 204832 | tf_op jit(solution)/shard_map/ppermute | solution.py:29
  62.2 5.4 %collective-permute-done.14.refs_2_ = s16[400,256]{1,0:T(8,128)(2,1)S(1)} collective-permute-done((s16[400,256]{1,0:T(8,128)(2,1)S(1)}, s16[400,256]{1,0:T(8,128)(2,1)S(1)}, u32[]{:S(2)}, u32[]{:S(2)}) %collective-permute-start.14) | collective-permute-done | bytes 204832 | tf_op jit(solution)/shard_map/ppermute | solution.py:29
  67.6 5.7 %collective-permute-done.16.refs_1_ = s16[1168,256]{1,0:T(8,128)(2,1)S(1)} collective-permute-done((s16[1168,256]{1,0:T(8,128)(2,1)S(1)}, s16[1168,256]{1,0:T(8,128)(2,1)S(1)}, u32[]{:S(2)}, u32[]{:S(2)}) %collective-permute-start.16) | collective-permute-done | bytes 598048 | tf_op jit(solution)/shard_map/ppermute | solution.py:29
  82.8 7.5 %collective-permute-done.23.refs_15_ = bf16[12,96,256]{2,1,0:T(8,128)(2,1)S(1)} collective-permute-done((bf16[12,96,256]{2,1,0:T(8,128)(2,1)S(1)}, bf16[12,96,256]{2,1,0:T(8,128)(2,1)S(1)}, u32[]{:S(2)}, u32[]{:S(2)}) %collective-permute-start.23) | collective-permute-done | bytes 589856 | tf_op jit(solution)/shard_map/ppermute | solution.py:29
  92.9 3.4 %collective-permute-done.19.refs_8_ = bf16[4,96,256]{2,1,0:T(8,128)(2,1)S(1)} collective-permute-done((bf16[4,96,256]{2,1,0:T(8,128)(2,1)S(1)}, bf16[4,96,256]{2,1,0:T(8,128)(2,1)S(1)}, u32[]{:S(2)}, u32[]{:S(2)}) %collective-permute-start.19) | collective-permute-done | bytes 196640 | tf_op jit(solution)/shard_map/ppermute | solution.py:29
  100.2 6.2 %shard_map.117 = (f32[16,96,256]{2,1,0:T(8,128)S(1)}, f32[16,96,256]{2,1,0:T(8,128)S(1)}, f32[12,96,256]{2,1,0:T(8,128)S(1)}, s16[1168,256]{1,0:T(8,128)(2,1)S(1...) custom-call(s32[128]{0:T(128)S(1)} %get-tuple-element.109.refs_0_, s32[128]{0:T(128)S(1)} %get-tuple-element.108.refs_1_, ...), custom_call_target="tpu_custom_call" | custom-call | flops 3221225472 | bytes 33554432 | tf_op jit(solution)/shard_map/pallas_call | solution.py:159
  108.6 7.4 %collective-permute-start.34 = (s16[1168,256]{1,0:T(8,128)(2,1)S(1)}, s16[1168,256]{1,0:T(8,128)(2,1)S(1)}, u32[]{:S(2)}, u32[]{:S(2)}) collective-permute-start(s16[1168,256]{1,0:T(8,128)(2,1)S(1)} %get-tuple-element.84), channel_id=1, source_target_pairs={{0,16},{8,24},{16,0},{24,8},{1,17},{9,25},{17,1},{25,9},{2,18},{10... | collective-permute-start | bytes 1794056 | tf_op jit(solution)/shard_map/ppermute | solution.py:29
  117.9 3.3 %collective-permute-start.31 = (s16[400,256]{1,0:T(8,128)(2,1)S(1)}, s16[400,256]{1,0:T(8,128)(2,1)S(1)}, u32[]{:S(2)}, u32[]{:S(2)}) collective-permute-start(s16[400,256]{1,0:T(8,128)(2,1)S(1)} %get-tuple-element.80), channel_id=1, source_target_pairs={{0,4},{1,5},{2,6},{3,7},{4,0},{5,1},{6,2},{7,3},{8,12},{9,13},{10,... | collective-permute-start | bytes 614408 | tf_op jit(solution)/shard_map/ppermute | solution.py:29
  121.2 7.3 %collective-permute-done.30.refs_0_ = s16[400,256]{1,0:T(8,128)(2,1)S(1)} collective-permute-done((s16[400,256]{1,0:T(8,128)(2,1)S(1)}, s16[400,256]{1,0:T(8,128)(2,1)S(1)}, u32[]{:S(2)}, u32[]{:S(2)}) %collective-permute-start.30) | collective-permute-done | bytes 204832 | tf_op jit(solution)/shard_map/ppermute | solution.py:29
  130.8 5.4 %collective-permute-done.32.refs_2_ = s16[400,256]{1,0:T(8,128)(2,1)S(1)} collective-permute-done((s16[400,256]{1,0:T(8,128)(2,1)S(1)}, s16[400,256]{1,0:T(8,128)(2,1)S(1)}, u32[]{:S(2)}, u32[]{:S(2)}) %collective-permute-start.32) | collective-permute-done | bytes 204832 | tf_op jit(solution)/shard_map/ppermute | solution.py:29
  136.1 5.7 %collective-permute-done.34.refs_1_ = s16[1168,256]{1,0:T(8,128)(2,1)S(1)} collective-permute-done((s16[1168,256]{1,0:T(8,128)(2,1)S(1)}, s16[1168,256]{1,0:T(8,128)(2,1)S(1)}, u32[]{:S(2)}, u32[]{:S(2)}) %collective-permute-start.34) | collective-permute-done | bytes 598048 | tf_op jit(solution)/shard_map/ppermute | solution.py:29
  151.4 7.5 %collective-permute-done.41.refs_15_ = bf16[12,96,256]{2,1,0:T(8,128)(2,1)S(1)} collective-permute-done((bf16[12,96,256]{2,1,0:T(8,128)(2,1)S(1)}, bf16[12,96,256]{2,1,0:T(8,128)(2,1)S(1)}, u32[]{:S(2)}, u32[]{:S(2)}) %collective-permute-start.41) | collective-permute-done | bytes 589856 | tf_op jit(solution)/shard_map/ppermute | solution.py:29
  161.4 3.4 %collective-permute-done.37.refs_8_ = bf16[4,96,256]{2,1,0:T(8,128)(2,1)S(1)} collective-permute-done((bf16[4,96,256]{2,1,0:T(8,128)(2,1)S(1)}, bf16[4,96,256]{2,1,0:T(8,128)(2,1)S(1)}, u32[]{:S(2)}, u32[]{:S(2)}) %collective-permute-start.37) | collective-permute-done | bytes 196640 | tf_op jit(solution)/shard_map/ppermute | solution.py:29
  168.8 6.2 %shard_map.121 = (f32[16,96,256]{2,1,0:T(8,128)S(1)}, f32[16,96,256]{2,1,0:T(8,128)S(1)}, f32[12,96,256]{2,1,0:T(8,128)S(1)}, s16[1168,256]{1,0:T(8,128)(2,1)S(1...) custom-call(s32[128]{0:T(128)S(1)} %get-tuple-element.109.refs_0_, s32[128]{0:T(128)S(1)} %get-tuple-element.108.refs_1_, ...), custom_call_target="tpu_custom_call" | custom-call | flops 3221225472 | bytes 33554432 | tf_op jit(solution)/shard_map/pallas_call | solution.py:159
  177.2 7.3 %collective-permute-start.52 = (s16[1168,256]{1,0:T(8,128)(2,1)S(1)}, s16[1168,256]{1,0:T(8,128)(2,1)S(1)}, u32[]{:S(2)}, u32[]{:S(2)}) collective-permute-start(s16[1168,256]{1,0:T(8,128)(2,1)S(1)} %get-tuple-element.101), channel_id=1, source_target_pairs={{0,16},{8,24},{16,0},{24,8},{1,17},{9,25},{17,1},{25,9},{2,18},{10... | collective-permute-start | bytes 1794056 | tf_op jit(solution)/shard_map/ppermute | solution.py:29
  186.5 3.3 %collective-permute-start.49 = (s16[400,256]{1,0:T(8,128)(2,1)S(1)}, s16[400,256]{1,0:T(8,128)(2,1)S(1)}, u32[]{:S(2)}, u32[]{:S(2)}) collective-permute-start(s16[400,256]{1,0:T(8,128)(2,1)S(1)} %get-tuple-element.97), channel_id=1, source_target_pairs={{0,4},{1,5},{2,6},{3,7},{4,0},{5,1},{6,2},{7,3},{8,12},{9,13},{10,... | collective-permute-start | bytes 614408 | tf_op jit(solution)/shard_map/ppermute | solution.py:29
  189.8 7.3 %collective-permute-done.48.refs_0_ = s16[400,256]{1,0:T(8,128)(2,1)S(1)} collective-permute-done((s16[400,256]{1,0:T(8,128)(2,1)S(1)}, s16[400,256]{1,0:T(8,128)(2,1)S(1)}, u32[]{:S(2)}, u32[]{:S(2)}) %collective-permute-start.48) | collective-permute-done | bytes 204832 | tf_op jit(solution)/shard_map/ppermute | solution.py:29
  199.3 5.4 %collective-permute-done.50.refs_2_ = s16[400,256]{1,0:T(8,128)(2,1)S(1)} collective-permute-done((s16[400,256]{1,0:T(8,128)(2,1)S(1)}, s16[400,256]{1,0:T(8,128)(2,1)S(1)}, u32[]{:S(2)}, u32[]{:S(2)}) %collective-permute-start.50) | collective-permute-done | bytes 204832 | tf_op jit(solution)/shard_map/ppermute | solution.py:29
  204.7 5.7 %collective-permute-done.52.refs_1_ = s16[1168,256]{1,0:T(8,128)(2,1)S(1)} collective-permute-done((s16[1168,256]{1,0:T(8,128)(2,1)S(1)}, s16[1168,256]{1,0:T(8,128)(2,1)S(1)}, u32[]{:S(2)}, u32[]{:S(2)}) %collective-permute-start.52) | collective-permute-done | bytes 598048 | tf_op jit(solution)/shard_map/ppermute | solution.py:29
  (120 shorter events, 72.8 us)
Async XLA Ops:
  2.0 16.3 %collective-permute-start.5 = (bf16[12,96,256]{2,1,0:T(8,128)(2,1)S(1)}, bf16[12,96,256]{2,1,0:T(8,128)(2,1)S(1)}, u32[]{:S(2)}, u32[]{:S(2)}) collective-permute-start(bf16[12,96,256]{2,1,0:T(8,128)(2,1)S(1)} %convert_bitcast_fusion.refs_14_), channel_id=1, source_target_pairs={{0,8},{8,0},{16,24},{24,16},{1,9},{9,1},{17,25},{25,17},{2,10},{10... | collective-permute-start | bytes 1769480 | tf_op jit(solution)/shard_map/ppermute | solution.py:29
  5.1 14.8 %collective-permute-start.4 = (bf16[12,96,256]{2,1,0:T(8,128)(2,1)S(1)}, bf16[12,96,256]{2,1,0:T(8,128)(2,1)S(1)}, u32[]{:S(2)}, u32[]{:S(2)}) collective-permute-start(bf16[12,96,256]{2,1,0:T(8,128)(2,1)S(1)} %convert_bitcast_fusion.refs_14_), channel_id=1, source_target_pairs={{0,16},{8,24},{16,0},{24,8},{1,17},{9,25},{17,1},{25,9},{2,18},{10... | collective-permute-start | bytes 1769480 | tf_op jit(solution)/shard_map/ppermute | solution.py:29
  6.6 15.0 %collective-permute-start.2 = (bf16[4,96,256]{2,1,0:T(8,128)(2,1)S(1)}, bf16[4,96,256]{2,1,0:T(8,128)(2,1)S(1)}, u32[]{:S(2)}, u32[]{:S(2)}) collective-permute-start(bf16[4,96,256]{2,1,0:T(8,128)(2,1)S(1)} %convert_element_type.9.refs_6_), channel_id=1, source_target_pairs={{0,6},{1,7},{2,4},{3,5},{4,2},{5,3},{6,0},{7,1},{8,14},{9,15},{10,... | collective-permute-start | bytes 589832 | tf_op jit(solution)/shard_map/ppermute | solution.py:29
  10.3 16.1 %collective-permute-start.1 = (bf16[4,96,256]{2,1,0:T(8,128)(2,1)S(1)}, bf16[4,96,256]{2,1,0:T(8,128)(2,1)S(1)}, u32[]{:S(2)}, u32[]{:S(2)}) collective-permute-start(bf16[4,96,256]{2,1,0:T(8,128)(2,1)S(1)} %convert_element_type.9.refs_6_), channel_id=1, source_target_pairs={{0,4},{1,5},{2,6},{3,7},{4,0},{5,1},{6,2},{7,3},{8,12},{9,13},{10,... | collective-permute-start | bytes 589832 | tf_op jit(solution)/shard_map/ppermute | solution.py:29
  10.3 16.1 %collective-permute-start = (bf16[4,96,256]{2,1,0:T(8,128)(2,1)S(1)}, bf16[4,96,256]{2,1,0:T(8,128)(2,1)S(1)}, u32[]{:S(2)}, u32[]{:S(2)}) collective-permute-start(bf16[4,96,256]{2,1,0:T(8,128)(2,1)S(1)} %convert_element_type.9.refs_6_), channel_id=1, source_target_pairs={{0,2},{1,3},{2,0},{3,1},{4,6},{5,7},{6,4},{7,5},{8,10},{9,11},{10,... | collective-permute-start | bytes 589832 | tf_op jit(solution)/shard_map/ppermute | solution.py:29
  37.3 30.2 %collective-permute-start.15 = (s16[1168,256]{1,0:T(8,128)(2,1)S(1)}, s16[1168,256]{1,0:T(8,128)(2,1)S(1)}, u32[]{:S(2)}, u32[]{:S(2)}) collective-permute-start(s16[1168,256]{1,0:T(8,128)(2,1)S(1)} %get-tuple-element.66), channel_id=1, source_target_pairs={{0,8},{8,0},{16,24},{24,16},{1,9},{9,1},{17,25},{25,17},{2,10},{10... | collective-permute-start | bytes 1794056 | tf_op jit(solution)/shard_map/ppermute | solution.py:29
  38.3 35.0 %collective-permute-start.16 = (s16[1168,256]{1,0:T(8,128)(2,1)S(1)}, s16[1168,256]{1,0:T(8,128)(2,1)S(1)}, u32[]{:S(2)}, u32[]{:S(2)}) collective-permute-start(s16[1168,256]{1,0:T(8,128)(2,1)S(1)} %get-tuple-element.67), channel_id=1, source_target_pairs={{0,16},{8,24},{16,0},{24,8},{1,17},{9,25},{17,1},{25,9},{2,18},{10... | collective-permute-start | bytes 1794056 | tf_op jit(solution)/shard_map/ppermute | solution.py:29
  47.4 27.7 %collective-permute-start.17 = (s16[1168,256]{1,0:T(8,128)(2,1)S(1)}, s16[1168,256]{1,0:T(8,128)(2,1)S(1)}, u32[]{:S(2)}, u32[]{:S(2)}) collective-permute-start(s16[1168,256]{1,0:T(8,128)(2,1)S(1)} %get-tuple-element.68), channel_id=1, source_target_pairs={{0,24},{8,16},{16,8},{24,0},{1,25},{9,17},{17,9},{25,1},{2,26},{10... | collective-permute-start | bytes 1794056 | tf_op jit(solution)/shard_map/ppermute | solution.py:29
  75.7 14.5 %collective-permute-start.23 = (bf16[12,96,256]{2,1,0:T(8,128)(2,1)S(1)}, bf16[12,96,256]{2,1,0:T(8,128)(2,1)S(1)}, u32[]{:S(2)}, u32[]{:S(2)}) collective-permute-start(bf16[12,96,256]{2,1,0:T(8,128)(2,1)S(1)} %shard_map.115.refs_14_), channel_id=1, source_target_pairs={{0,8},{8,0},{16,24},{24,16},{1,9},{9,1},{17,25},{25,17},{2,10},{10... | collective-permute-start | bytes 1769480 | tf_op jit(solution)/shard_map/ppermute | solution.py:29
  76.4 14.3 %collective-permute-start.22 = (bf16[12,96,256]{2,1,0:T(8,128)(2,1)S(1)}, bf16[12,96,256]{2,1,0:T(8,128)(2,1)S(1)}, u32[]{:S(2)}, u32[]{:S(2)}) collective-permute-start(bf16[12,96,256]{2,1,0:T(8,128)(2,1)S(1)} %shard_map.115.refs_14_), channel_id=1, source_target_pairs={{0,16},{8,24},{16,0},{24,8},{1,17},{9,25},{17,1},{25,9},{2,18},{10... | collective-permute-start | bytes 1769480 | tf_op jit(solution)/shard_map/ppermute | solution.py:29
  78.4 13.8 %collective-permute-start.20 = (bf16[4,96,256]{2,1,0:T(8,128)(2,1)S(1)}, bf16[4,96,256]{2,1,0:T(8,128)(2,1)S(1)}, u32[]{:S(2)}, u32[]{:S(2)}) collective-permute-start(bf16[4,96,256]{2,1,0:T(8,128)(2,1)S(1)} %shard_map.116.refs_6_), channel_id=1, source_target_pairs={{0,6},{1,7},{2,4},{3,5},{4,2},{5,3},{6,0},{7,1},{8,14},{9,15},{10,... | collective-permute-start | bytes 589832 | tf_op jit(solution)/shard_map/ppermute | solution.py:29
  80.1 16.1 %collective-permute-start.19 = (bf16[4,96,256]{2,1,0:T(8,128)(2,1)S(1)}, bf16[4,96,256]{2,1,0:T(8,128)(2,1)S(1)}, u32[]{:S(2)}, u32[]{:S(2)}) collective-permute-start(bf16[4,96,256]{2,1,0:T(8,128)(2,1)S(1)} %shard_map.116.refs_6_), channel_id=1, source_target_pairs={{0,4},{1,5},{2,6},{3,7},{4,0},{5,1},{6,2},{7,3},{8,12},{9,13},{10,... | collective-permute-start | bytes 589832 | tf_op jit(solution)/shard_map/ppermute | solution.py:29
  80.1 16.1 %collective-permute-start.18 = (bf16[4,96,256]{2,1,0:T(8,128)(2,1)S(1)}, bf16[4,96,256]{2,1,0:T(8,128)(2,1)S(1)}, u32[]{:S(2)}, u32[]{:S(2)}) collective-permute-start(bf16[4,96,256]{2,1,0:T(8,128)(2,1)S(1)} %shard_map.116.refs_6_), channel_id=1, source_target_pairs={{0,2},{1,3},{2,0},{3,1},{4,6},{5,7},{6,4},{7,5},{8,10},{9,11},{10,... | collective-permute-start | bytes 589832 | tf_op jit(solution)/shard_map/ppermute | solution.py:29
  106.5 29.6 %collective-permute-start.33 = (s16[1168,256]{1,0:T(8,128)(2,1)S(1)}, s16[1168,256]{1,0:T(8,128)(2,1)S(1)}, u32[]{:S(2)}, u32[]{:S(2)}) collective-permute-start(s16[1168,256]{1,0:T(8,128)(2,1)S(1)} %get-tuple-element.83), channel_id=1, source_target_pairs={{0,8},{8,0},{16,24},{24,16},{1,9},{9,1},{17,25},{25,17},{2,10},{10... | collective-permute-start | bytes 1794056 | tf_op jit(solution)/shard_map/ppermute | solution.py:29
  108.6 33.2 %collective-permute-start.34 = (s16[1168,256]{1,0:T(8,128)(2,1)S(1)}, s16[1168,256]{1,0:T(8,128)(2,1)S(1)}, u32[]{:S(2)}, u32[]{:S(2)}) collective-permute-start(s16[1168,256]{1,0:T(8,128)(2,1)S(1)} %get-tuple-element.84), channel_id=1, source_target_pairs={{0,16},{8,24},{16,0},{24,8},{1,17},{9,25},{17,1},{25,9},{2,18},{10... | collective-permute-start | bytes 1794056 | tf_op jit(solution)/shard_map/ppermute | solution.py:29
  116.0 27.7 %collective-permute-start.35 = (s16[1168,256]{1,0:T(8,128)(2,1)S(1)}, s16[1168,256]{1,0:T(8,128)(2,1)S(1)}, u32[]{:S(2)}, u32[]{:S(2)}) collective-permute-start(s16[1168,256]{1,0:T(8,128)(2,1)S(1)} %get-tuple-element.85), channel_id=1, source_target_pairs={{0,24},{8,16},{16,8},{24,0},{1,25},{9,17},{17,9},{25,1},{2,26},{10... | collective-permute-start | bytes 1794056 | tf_op jit(solution)/shard_map/ppermute | solution.py:29
  144.3 14.5 %collective-permute-start.41 = (bf16[12,96,256]{2,1,0:T(8,128)(2,1)S(1)}, bf16[12,96,256]{2,1,0:T(8,128)(2,1)S(1)}, u32[]{:S(2)}, u32[]{:S(2)}) collective-permute-start(bf16[12,96,256]{2,1,0:T(8,128)(2,1)S(1)} %shard_map.119.refs_14_), channel_id=1, source_target_pairs={{0,8},{8,0},{16,24},{24,16},{1,9},{9,1},{17,25},{25,17},{2,10},{10... | collective-permute-start | bytes 1769480 | tf_op jit(solution)/shard_map/ppermute | solution.py:29
  145.0 14.3 %collective-permute-start.40 = (bf16[12,96,256]{2,1,0:T(8,128)(2,1)S(1)}, bf16[12,96,256]{2,1,0:T(8,128)(2,1)S(1)}, u32[]{:S(2)}, u32[]{:S(2)}) collective-permute-start(bf16[12,96,256]{2,1,0:T(8,128)(2,1)S(1)} %shard_map.119.refs_14_), channel_id=1, source_target_pairs={{0,16},{8,24},{16,0},{24,8},{1,17},{9,25},{17,1},{25,9},{2,18},{10... | collective-permute-start | bytes 1769480 | tf_op jit(solution)/shard_map/ppermute | solution.py:29
  146.9 13.8 %collective-permute-start.38 = (bf16[4,96,256]{2,1,0:T(8,128)(2,1)S(1)}, bf16[4,96,256]{2,1,0:T(8,128)(2,1)S(1)}, u32[]{:S(2)}, u32[]{:S(2)}) collective-permute-start(bf16[4,96,256]{2,1,0:T(8,128)(2,1)S(1)} %shard_map.120.refs_6_), channel_id=1, source_target_pairs={{0,6},{1,7},{2,4},{3,5},{4,2},{5,3},{6,0},{7,1},{8,14},{9,15},{10,... | collective-permute-start | bytes 589832 | tf_op jit(solution)/shard_map/ppermute | solution.py:29
  148.5 16.3 %collective-permute-start.37 = (bf16[4,96,256]{2,1,0:T(8,128)(2,1)S(1)}, bf16[4,96,256]{2,1,0:T(8,128)(2,1)S(1)}, u32[]{:S(2)}, u32[]{:S(2)}) collective-permute-start(bf16[4,96,256]{2,1,0:T(8,128)(2,1)S(1)} %shard_map.120.refs_6_), channel_id=1, source_target_pairs={{0,4},{1,5},{2,6},{3,7},{4,0},{5,1},{6,2},{7,3},{8,12},{9,13},{10,... | collective-permute-start | bytes 589832 | tf_op jit(solution)/shard_map/ppermute | solution.py:29
  148.5 16.3 %collective-permute-start.36 = (bf16[4,96,256]{2,1,0:T(8,128)(2,1)S(1)}, bf16[4,96,256]{2,1,0:T(8,128)(2,1)S(1)}, u32[]{:S(2)}, u32[]{:S(2)}) collective-permute-start(bf16[4,96,256]{2,1,0:T(8,128)(2,1)S(1)} %shard_map.120.refs_6_), channel_id=1, source_target_pairs={{0,2},{1,3},{2,0},{3,1},{4,6},{5,7},{6,4},{7,5},{8,10},{9,11},{10,... | collective-permute-start | bytes 589832 | tf_op jit(solution)/shard_map/ppermute | solution.py:29
  175.1 29.6 %collective-permute-start.51 = (s16[1168,256]{1,0:T(8,128)(2,1)S(1)}, s16[1168,256]{1,0:T(8,128)(2,1)S(1)}, u32[]{:S(2)}, u32[]{:S(2)}) collective-permute-start(s16[1168,256]{1,0:T(8,128)(2,1)S(1)} %get-tuple-element.100), channel_id=1, source_target_pairs={{0,8},{8,0},{16,24},{24,16},{1,9},{9,1},{17,25},{25,17},{2,10},{10... | collective-permute-start | bytes 1794056 | tf_op jit(solution)/shard_map/ppermute | solution.py:29
  177.2 33.2 %collective-permute-start.52 = (s16[1168,256]{1,0:T(8,128)(2,1)S(1)}, s16[1168,256]{1,0:T(8,128)(2,1)S(1)}, u32[]{:S(2)}, u32[]{:S(2)}) collective-permute-start(s16[1168,256]{1,0:T(8,128)(2,1)S(1)} %get-tuple-element.101), channel_id=1, source_target_pairs={{0,16},{8,24},{16,0},{24,8},{1,17},{9,25},{17,1},{25,9},{2,18},{10... | collective-permute-start | bytes 1794056 | tf_op jit(solution)/shard_map/ppermute | solution.py:29
  184.6 27.7 %collective-permute-start.53 = (s16[1168,256]{1,0:T(8,128)(2,1)S(1)}, s16[1168,256]{1,0:T(8,128)(2,1)S(1)}, u32[]{:S(2)}, u32[]{:S(2)}) collective-permute-start(s16[1168,256]{1,0:T(8,128)(2,1)S(1)} %get-tuple-element.102), channel_id=1, source_target_pairs={{0,24},{8,16},{16,8},{24,0},{1,25},{9,17},{17,9},{25,1},{2,26},{10... | collective-permute-start | bytes 1794056 | tf_op jit(solution)/shard_map/ppermute | solution.py:29
  (37 other events, 318.7 us)

commit v4 on v3

--- a/solution.py
+++ b/solution.py
@@ -15,7 +15,8 @@
 HIGHEST = 126.0
 TAIL = 16
 TIES = 3
-FORWARD = True
+EARLY = 2
+RELAY = True
 SMALLEST = 1e-33
 
 
@@ -59,13 +60,14 @@
     return -(-size // TAIL) * TAIL
 
 
-def drags_body(group, counts, *refs):
-    elec_pieces, phon_pieces, elec_parts, phon_parts = counts
+def drags_body(group, counts, kept, *refs):
+    elec_pieces, phon_pieces = counts
+    elec_kept, phon_kept, plan = kept
     elec_in, elec_out, phon_in, phon_out, group_count, tiles = refs[:6]
     refs = refs[6:]
     sources, refs = refs[: elec_pieces + phon_pieces], refs[elec_pieces + phon_pieces :]
-    halves, refs = refs[:elec_parts], refs[elec_parts:]
-    whole, coded, refs = refs[0], refs[1:phon_parts], refs[phon_parts:]
+    whole, refs = refs[: len(elec_kept) + len(phon_kept)], refs[len(elec_kept) + len(phon_kept) :]
+    coded, refs = refs[: len(plan)], refs[len(plan) :]
     elec, phon, elec_totals, phon_totals, held, source_sems, tile_sems, out_sems = refs
     loads = []
     for target, pieces in ((elec, sources[:elec_pieces]), (phon, sources[elec_pieces:])):
@@ -124,47 +126,40 @@
         return carry
 
     lax.fori_loop(0, groups, one_group, 0)
-    stores, first = [], 0
-    for half in halves:
-        size = half.shape[0]
-        stores.append(
-            pltpu.make_async_copy(
-                elec_totals.at[pl.ds(first, size)], half, out_sems.at[len(stores)]
-            )
+    places = [(elec_totals, span) for span in elec_kept] + [(phon_totals, span) for span in phon_kept]
+    stores = [
+        pltpu.make_async_copy(
+            totals.at[pl.ds(first, end - first)], whole[index], out_sems.at[index]
         )
-        first += size
-    span = whole.shape[0]
-    stores.append(
-        pltpu.make_async_copy(phon_totals.at[pl.ds(0, span)], whole, out_sems.at[len(stores)])
-    )
+        for index, (totals, (first, end)) in enumerate(places)
+    ]
     for store in stores:
         store.start()
-    for index, piece in enumerate(coded):
-        first = (index + 1) * span
-        encode_piece(lambda block, first=first: phon_totals[first + block], span, piece)
+    for blocks, piece in zip(plan, coded):
+        encode_piece(lambda index, blocks=blocks: phon_totals[blocks[index]], len(blocks), piece)
     for store in stores:
         store.wait()
 
 
-def drags(ids, tile_set, group, elec_pieces, phon_pieces, elec_parts, phon_parts):
+def drags(ids, tile_set, group, elec_pieces, phon_pieces, kept):
+    elec_kept, phon_kept, plan = kept
     _, rows, lanes = elec_pieces[0].shape
     side = tile_set.shape[-1]
     elec_blocks = sum(piece.shape[0] for piece in elec_pieces)
     phon_blocks = sum(piece.shape[0] for piece in phon_pieces)
-    half, span = elec_blocks // elec_parts, phon_blocks // phon_parts
     any_space = pl.BlockSpec(memory_space=pl.ANY)
     smem = pl.BlockSpec(memory_space=pltpu.SMEM)
     vmem = pl.BlockSpec(memory_space=pltpu.VMEM)
     pieces = list(elec_pieces) + list(phon_pieces)
+    whole = list(elec_kept) + list(phon_kept)
     outs = pl.pallas_call(
-        functools.partial(
-            drags_body, group, (len(elec_pieces), len(phon_pieces), elec_parts, phon_parts)
-        ),
-        out_shape=[jax.ShapeDtypeStruct((half, rows, lanes), jnp.float32)] * elec_parts
-        + [jax.ShapeDtypeStruct((span, rows, lanes), jnp.float32)]
-        + [coded_shape(span, rows, lanes)] * (phon_parts - 1),
+        functools.partial(drags_body, group, (len(elec_pieces), len(phon_pieces)), kept),
+        out_shape=[
+            jax.ShapeDtypeStruct((end - first, rows, lanes), jnp.float32) for first, end in whole
+        ]
+        + [coded_shape(len(blocks), rows, lanes) for blocks in plan],
         in_specs=[smem] * 5 + [any_space] * (1 + len(pieces)),
-        out_specs=[any_space] * (elec_parts + 1) + [vmem] * (phon_parts - 1),
+        out_specs=[any_space] * len(whole) + [vmem] * len(plan),
         scratch_shapes=[
             pltpu.VMEM((elec_blocks, rows, lanes), jnp.bfloat16),
             pltpu.VMEM((phon_blocks, rows, lanes), jnp.bfloat16),
@@ -173,7 +168,7 @@
             pltpu.VMEM((DEPTH, group, side, side), jnp.bfloat16),
             pltpu.SemaphoreType.DMA((len(pieces),)),
             pltpu.SemaphoreType.DMA((DEPTH,)),
-            pltpu.SemaphoreType.DMA((elec_parts + 1,)),
+            pltpu.SemaphoreType.DMA((len(whole),)),
         ],
         compiler_params=pltpu.CompilerParams(vmem_limit_bytes=40 * 1024 * 1024),
         cost_estimate=pl.CostEstimate(
@@ -182,7 +177,7 @@
             transcendentals=0,
         ),
     )(*ids, tile_set, *pieces)
-    return outs[:elec_parts], outs[elec_parts], outs[elec_parts + 1 :]
+    return outs[: len(elec_kept)], outs[len(elec_kept) : len(whole)], outs[len(whole) :]
 
 
 def coded_shape(size, rows, lanes):
@@ -231,7 +226,7 @@
 
 
 def pair_sum(mine, theirs, piece_count):
-    blocks, rows, lanes = mine.shape
+    blocks, rows, lanes = theirs.shape
     span = blocks // (piece_count + 1)
     vmem = pl.BlockSpec(memory_space=pltpu.VMEM)
     return pl.pallas_call(
@@ -249,29 +244,62 @@
     return pl.CostEstimate(flops=COST, bytes_accessed=COST, transcendentals=0)
 
 
-def renew_body(source, own, rate, *refs):
+def decode(piece, index, scales, rows):
+    values = piece[pl.ds(index * rows, rows), :].astype(jnp.int32).astype(jnp.float32)
+    return values * scales[index]
+
+
+def piece_size(piece, rows):
+    return next(size for size in range(piece.shape[0] // rows + 1) if size * rows + tail_rows(size) == piece.shape[0])
+
+
+def renew_body(terms, source, own, rate, *refs):
     coded, result = refs[:-1], refs[-1]
-    size, rows, _ = own.shape
-    scales = [scales_of(piece, size, rows) for piece in coded]
-    for index in range(size):
+    _, rows, _ = result.shape
+    scales = [scales_of(piece, piece_size(piece, rows), rows) for piece in coded]
+    for index, parts in enumerate(terms):
         total = own[index]
-        for piece, scale in zip(coded, scales):
-            values = piece[pl.ds(index * rows, rows), :].astype(jnp.int32).astype(jnp.float32)
-            total = total + values * scale[index]
+        for piece, place in parts:
+            total = total + decode(coded[piece], place, scales[piece], rows)
         fresh = (source[index] + total) / rate[pl.ds(index, 1), :]
         result[index] = fresh.astype(result.dtype)
 
 
-def renew(source, own, coded, rate, dtype):
+def renew(source, own, coded, terms, rate, dtype):
     vmem = pl.BlockSpec(memory_space=pltpu.VMEM)
     return pl.pallas_call(
-        renew_body,
-        out_shape=jax.ShapeDtypeStruct(own.shape, dtype),
+        functools.partial(renew_body, terms),
+        out_shape=jax.ShapeDtypeStruct(source.shape, dtype),
         in_specs=[vmem] * (3 + len(coded)),
         out_specs=vmem,
         compiler_params=pltpu.CompilerParams(vmem_limit_bytes=32 * 1024 * 1024),
         cost_estimate=small_cost(),
     )(source, own, rate, *coded)
+
+
+def combine_body(plan, totals, *refs):
+    taken, given = refs[: len(plan)], refs[len(plan) :]
+    _, rows, _ = totals.shape
+    for blocks, source, target in zip(plan, taken, given):
+        scales = scales_of(source, piece_size(source, rows), rows)
+        encode_piece(
+            lambda index, blocks=blocks, source=source, scales=scales: totals[blocks[index]]
+            + decode(source, index, scales, rows),
+            len(blocks), target,
+        )
+
+
+def combine(totals, taken, plan):
+    _, rows, lanes = totals.shape
+    vmem = pl.BlockSpec(memory_space=pltpu.VMEM)
+    return pl.pallas_call(
+        functools.partial(combine_body, plan),
+        out_shape=[coded_shape(len(blocks), rows, lanes) for blocks in plan],
+        in_specs=[vmem] * (1 + len(taken)),
+        out_specs=[vmem] * len(plan),
+        compiler_params=pltpu.CompilerParams(vmem_limit_bytes=32 * 1024 * 1024),
+        cost_estimate=small_cost(),
+    )(totals, *taken)
 
 
 def local(
@@ -343,7 +371,7 @@
 
     def spread_phon(value):
         half = phon_span // 2
-        if FORWARD and n_el == 4 and half:
+        if RELAY and n_el == 4 and half:
             near, far = over_el([value] * 2)
             halves = after([far[:half], near[half:]], [near, far])
             passed = [
@@ -360,22 +388,49 @@
         others = after(same_core[1:], first)
         return same_core + [over_core(piece) for piece in [value] + others]
 
+    elec_terms = [[(step, index) for step in range(n_z - 1)] for index in range(elec_span)]
+    half = phon_span // 2
+    relay = RELAY and n_el == 4 and phon_span % 2 == 0
+    near, far, both = phon_span, 2 * phon_span, 3 * phon_span
+    if relay:
+        plan = [
+            [start + index for start in (both, near) for index in range(half)],
+            [start + index for start in (both, far) for index in range(half, phon_span)],
+        ]
+        combined = [list(range(half)), list(range(half, phon_span))]
+        phon_terms = [[(0, half + index), (3, index)] for index in range(half)]
+        phon_terms += [[(1, half + index), (2, index)] for index in range(half)]
+    else:
+        plan = [
+            list(range((step + 1) * phon_span, (step + 2) * phon_span)) for step in range(n_el - 1)
+        ]
+        phon_terms = [[(step, index) for step in range(n_el - 1)] for index in range(phon_span)]
+    middle = elec_blocks // 2
+    kept = (
+        [(0, middle), (middle, elec_blocks)],
+        [(0, phon_span)] + [(near + half, far + half)] * relay,
+        plan,
+    )
     ids = (elec_in, elec_out, phon_in, phon_out, group_count)
     elec_now, phon_now = elec_dev.astype(jnp.bfloat16), phon_dev[0].astype(jnp.bfloat16)
     for sweep in range(ITERS):
         dtype = jnp.bfloat16 if sweep + 1 < ITERS else jnp.float32
         phon_pieces, passed = spread_phon(phon_now)
         elec_pieces = spread_elec(elec_now, passed)
-        halves, phon_own, phon_coded = drags(
-            ids, tile_set, group, elec_pieces, phon_pieces, cores, n_el
+        (elec_own, given), phon_own, phon_coded = drags(
+            ids, tile_set, group, elec_pieces, phon_pieces, kept
         )
-        theirs = over_core(halves[1]) if cores == 2 else jnp.zeros_like(halves[0])
-        elec_own, *elec_coded = pair_sum(halves[0], theirs, n_z - 1)
-        phon_coded, elec_coded = over_el(phon_coded), over_z(elec_coded)
-        (phon_own,) = after([phon_own], [elec_own, *elec_coded[:TIES]])
-        phon_now = renew(phon_source[0], phon_own, phon_coded, phon_rate[0], dtype)
+        theirs = over_core(given)
+        elec_own, *elec_coded = pair_sum(elec_own, theirs, n_z - 1)
+        elec_coded = over_z(elec_coded)
+        phon_coded = over_el(phon_coded)
+        if relay:
+            taken = after(phon_coded[::-1], [elec_own, *elec_coded[:EARLY]])
+            phon_coded += over_el(combine(phon_own[1], taken, combined))
+        (phon_kept,) = after(phon_own[:1], [elec_own, *elec_coded[:TIES]])
+        phon_now = renew(phon_source[0], phon_kept, phon_coded, phon_terms, phon_rate[0], dtype)
         (elec_own,) = after([elec_own], [phon_now])
-        elec_now = renew(elec_source, elec_own, elec_coded, elec_rate, dtype)
+        elec_now = renew(elec_source, elec_own, elec_coded, elec_terms, elec_rate, dtype)
     return (elec_now, phon_now[None])
 
 

time: 215 us -> 208 us (0.967)
  waiting for transfers between devices: 107 us -> 89.7 us
  starting transfers between devices: 79.1 us -> 87.3 us
    ppermute x54 -> x57, waiting for transfers between devices: 107 us -> 89.7 us  [send(): lax.ppermute(value, axis, [(place, place_of(place)) for place in range(si...]
    ppermute x54 -> x57, starting transfers between devices: 79.1 us -> 87.3 us  [send(): lax.ppermute(value, axis, [(place, place_of(place)) for place in range(si...]
    pallas_call x6 -> x9, Pallas kernels: 4.19 us -> 4.82 us  [the longest x6 3.68 us: renew(): pl.pallas_call(functools.partial(renew_body, terms), out_shape=jax.ShapeD...]
  transfers between devices with their start and end apart: 54 -> 57, of which waited for: 39 -> 40; matrix products, arithmetic and copies ran while one was open for 1% -> 1% of each run, Pallas kernels for 1% -> 1%
where the time goes in v4:
time: 208 us; the launch traced here: 207 us
  waiting for transfers between devices  89.7 us (43%)
  starting transfers between devices  87.3 us (42%)
  Pallas kernels  25.1 us (12%)
    ppermute x57, waiting for transfers between devices, send(): lax.ppermute(value, axis, [(place, place_of(place)) for place in range(si...  89.7 us
    ppermute x57, starting transfers between devices, send(): lax.ppermute(value, axis, [(place, place_of(place)) for place in range(si...  87.3 us
    pallas_call x3, Pallas kernels, drags(): pl.pallas_call(functools.partial(drags_body, group, (len(elec_pieces), le...  19.3 us
  transfers between devices with their start and end apart: 57, of which 40 were waited for; matrix products, arithmetic and copies ran while one was open for 1% of the time, Pallas kernels for 1%

profile of v4, /device:TPU:0, one launch (start us, length us, event | category | flops | bytes accessed | tf_op | source)
XLA Modules:
  0.0 206.7 jit_solution(4973370879981283603)
XLA Ops:
  6.6 3.7 %collective-permute-start.2 = (bf16[4,96,256]{2,1,0:T(8,128)(2,1)S(1)}, bf16[4,96,256]{2,1,0:T(8,128)(2,1)S(1)}, u32[]{:S(2)}, u32[]{:S(2)}) collective-permute-start(bf16[4,96,256]{2,1,0:T(8,128)(2,1)S(1)} %convert_element_type.9.refs_6_), channel_id=1, source_target_pairs={{0,6},{1,7},{2,4},{3,5},{4,2},{5,3},{6,0},{7,1},{8,14},{9,15},{10,... | collective-permute-start | bytes 589832 | tf_op jit(solution)/shard_map/ppermute | solution.py:30
  11.1 7.3 %collective-permute-done.5.refs_15_ = bf16[12,96,256]{2,1,0:T(8,128)(2,1)S(1)} collective-permute-done((bf16[12,96,256]{2,1,0:T(8,128)(2,1)S(1)}, bf16[12,96,256]{2,1,0:T(8,128)(2,1)S(1)}, u32[]{:S(2)}, u32[]{:S(2)}) %collective-permute-start.5) | collective-permute-done | bytes 589856 | tf_op jit(solution)/shard_map/ppermute | solution.py:30
  30.9 6.4 %shard_map.113 = (f32[16,96,256]{2,1,0:T(8,128)S(1)}, f32[16,96,256]{2,1,0:T(8,128)S(1)}, f32[12,96,256]{2,1,0:T(8,128)S(1)}, f32[12,96,256]{2,1,0:T(8,128)S(1)}...) custom-call(s32[128]{0:T(128)S(1)} %get-tuple-element.133.refs_0_, s32[128]{0:T(128)S(1)} %get-tuple-element.132.refs_1_, ...), custom_call_target="tpu_custom_call" | custom-call | flops 3221225472 | bytes 33554432 | tf_op jit(solution)/shard_map/pallas_call | solution.py:155
  43.5 3.9 %collective-permute-start.12 = (s16[400,256]{1,0:T(8,128)(2,1)S(1)}, s16[400,256]{1,0:T(8,128)(2,1)S(1)}, u32[]{:S(2)}, u32[]{:S(2)}) collective-permute-start(s16[400,256]{1,0:T(8,128)(2,1)S(1)} %get-tuple-element.74), channel_id=1, source_target_pairs={{0,2},{1,3},{2,0},{3,1},{4,6},{5,7},{6,4},{7,5},{8,10},{9,11},{10,... | collective-permute-start | bytes 614408 | tf_op jit(solution)/shard_map/ppermute | solution.py:30
  47.4 4.4 %collective-permute-start.13 = (s16[400,256]{1,0:T(8,128)(2,1)S(1)}, s16[400,256]{1,0:T(8,128)(2,1)S(1)}, u32[]{:S(2)}, u32[]{:S(2)}) collective-permute-start(s16[400,256]{1,0:T(8,128)(2,1)S(1)} %get-tuple-element.75), channel_id=1, source_target_pairs={{0,4},{1,5},{2,6},{3,7},{4,0},{5,1},{6,2},{7,3},{8,12},{9,13},{10,... | collective-permute-start | bytes 614408 | tf_op jit(solution)/shard_map/ppermute | solution.py:30
  51.8 3.8 %collective-permute-done.15.refs_1_.refs_0_ = s16[1168,256]{1,0:T(8,128)(2,1)S(1)} collective-permute-done((s16[1168,256]{1,0:T(8,128)(2,1)S(1)}, s16[1168,256]{1,0:T(8,128)(2,1)S(1)}, u32[]{:S(2)}, u32[]{:S(2)}) %collective-permute-start.15) | collective-permute-done | bytes 598048 | tf_op jit(solution)/shard_map/ppermute | solution.py:30
  56.6 4.8 %collective-permute-done.13.refs_1_ = s16[400,256]{1,0:T(8,128)(2,1)S(1)} collective-permute-done((s16[400,256]{1,0:T(8,128)(2,1)S(1)}, s16[400,256]{1,0:T(8,128)(2,1)S(1)}, u32[]{:S(2)}, u32[]{:S(2)}) %collective-permute-start.13) | collective-permute-done | bytes 204832 | tf_op jit(solution)/shard_map/ppermute | solution.py:30
  67.5 5.2 %collective-permute-done.14.refs_2_ = s16[400,256]{1,0:T(8,128)(2,1)S(1)} collective-permute-done((s16[400,256]{1,0:T(8,128)(2,1)S(1)}, s16[400,256]{1,0:T(8,128)(2,1)S(1)}, u32[]{:S(2)}, u32[]{:S(2)}) %collective-permute-start.14) | collective-permute-done | bytes 204832 | tf_op jit(solution)/shard_map/ppermute | solution.py:30
  75.8 3.6 %collective-permute-start.21 = (bf16[4,96,256]{2,1,0:T(8,128)(2,1)S(1)}, bf16[4,96,256]{2,1,0:T(8,128)(2,1)S(1)}, u32[]{:S(2)}, u32[]{:S(2)}) collective-permute-start(bf16[4,96,256]{2,1,0:T(8,128)(2,1)S(1)} %shard_map.117.refs_6_), channel_id=1, source_target_pairs={{0,6},{1,7},{2,4},{3,5},{4,2},{5,3},{6,0},{7,1},{8,14},{9,15},{10,... | collective-permute-start | bytes 589832 | tf_op jit(solution)/shard_map/ppermute | solution.py:30
  80.5 5.3 %collective-permute-done.24.refs_15_ = bf16[12,96,256]{2,1,0:T(8,128)(2,1)S(1)} collective-permute-done((bf16[12,96,256]{2,1,0:T(8,128)(2,1)S(1)}, bf16[12,96,256]{2,1,0:T(8,128)(2,1)S(1)}, u32[]{:S(2)}, u32[]{:S(2)}) %collective-permute-start.24) | collective-permute-done | bytes 589856 | tf_op jit(solution)/shard_map/ppermute | solution.py:30
  89.0 5.6 %collective-permute-done.20.refs_8_ = bf16[4,96,256]{2,1,0:T(8,128)(2,1)S(1)} collective-permute-done((bf16[4,96,256]{2,1,0:T(8,128)(2,1)S(1)}, bf16[4,96,256]{2,1,0:T(8,128)(2,1)S(1)}, u32[]{:S(2)}, u32[]{:S(2)}) %collective-permute-start.20) | collective-permute-done | bytes 196640 | tf_op jit(solution)/shard_map/ppermute | solution.py:30
  96.9 6.4 %shard_map.118 = (f32[16,96,256]{2,1,0:T(8,128)S(1)}, f32[16,96,256]{2,1,0:T(8,128)S(1)}, f32[12,96,256]{2,1,0:T(8,128)S(1)}, f32[12,96,256]{2,1,0:T(8,128)S(1)}...) custom-call(s32[128]{0:T(128)S(1)} %get-tuple-element.133.refs_0_, s32[128]{0:T(128)S(1)} %get-tuple-element.132.refs_1_, ...), custom_call_target="tpu_custom_call" | custom-call | flops 3221225472 | bytes 33554432 | tf_op jit(solution)/shard_map/pallas_call | solution.py:155
  109.9 5.8 %collective-permute-start.31 = (s16[400,256]{1,0:T(8,128)(2,1)S(1)}, s16[400,256]{1,0:T(8,128)(2,1)S(1)}, u32[]{:S(2)}, u32[]{:S(2)}) collective-permute-start(s16[400,256]{1,0:T(8,128)(2,1)S(1)} %get-tuple-element.95), channel_id=1, source_target_pairs={{0,2},{1,3},{2,0},{3,1},{4,6},{5,7},{6,4},{7,5},{8,10},{9,11},{10,... | collective-permute-start | bytes 614408 | tf_op jit(solution)/shard_map/ppermute | solution.py:30
  117.5 4.5 %collective-permute-done.34.refs_1_.refs_0_ = s16[1168,256]{1,0:T(8,128)(2,1)S(1)} collective-permute-done((s16[1168,256]{1,0:T(8,128)(2,1)S(1)}, s16[1168,256]{1,0:T(8,128)(2,1)S(1)}, u32[]{:S(2)}, u32[]{:S(2)}) %collective-permute-start.34) | collective-permute-done | bytes 598048 | tf_op jit(solution)/shard_map/ppermute | solution.py:30
  124.4 3.4 %collective-permute-done.32.refs_1_ = s16[400,256]{1,0:T(8,128)(2,1)S(1)} collective-permute-done((s16[400,256]{1,0:T(8,128)(2,1)S(1)}, s16[400,256]{1,0:T(8,128)(2,1)S(1)}, u32[]{:S(2)}, u32[]{:S(2)}) %collective-permute-start.32) | collective-permute-done | bytes 204832 | tf_op jit(solution)/shard_map/ppermute | solution.py:30
  133.3 5.1 %collective-permute-done.33.refs_2_ = s16[400,256]{1,0:T(8,128)(2,1)S(1)} collective-permute-done((s16[400,256]{1,0:T(8,128)(2,1)S(1)}, s16[400,256]{1,0:T(8,128)(2,1)S(1)}, u32[]{:S(2)}, u32[]{:S(2)}) %collective-permute-start.33) | collective-permute-done | bytes 204832 | tf_op jit(solution)/shard_map/ppermute | solution.py:30
  141.5 3.6 %collective-permute-start.40 = (bf16[4,96,256]{2,1,0:T(8,128)(2,1)S(1)}, bf16[4,96,256]{2,1,0:T(8,128)(2,1)S(1)}, u32[]{:S(2)}, u32[]{:S(2)}) collective-permute-start(bf16[4,96,256]{2,1,0:T(8,128)(2,1)S(1)} %shard_map.122.refs_6_), channel_id=1, source_target_pairs={{0,6},{1,7},{2,4},{3,5},{4,2},{5,3},{6,0},{7,1},{8,14},{9,15},{10,... | collective-permute-start | bytes 589832 | tf_op jit(solution)/shard_map/ppermute | solution.py:30
  146.2 5.4 %collective-permute-done.43.refs_15_ = bf16[12,96,256]{2,1,0:T(8,128)(2,1)S(1)} collective-permute-done((bf16[12,96,256]{2,1,0:T(8,128)(2,1)S(1)}, bf16[12,96,256]{2,1,0:T(8,128)(2,1)S(1)}, u32[]{:S(2)}, u32[]{:S(2)}) %collective-permute-start.43) | collective-permute-done | bytes 589856 | tf_op jit(solution)/shard_map/ppermute | solution.py:30
  154.7 5.6 %collective-permute-done.39.refs_8_ = bf16[4,96,256]{2,1,0:T(8,128)(2,1)S(1)} collective-permute-done((bf16[4,96,256]{2,1,0:T(8,128)(2,1)S(1)}, bf16[4,96,256]{2,1,0:T(8,128)(2,1)S(1)}, u32[]{:S(2)}, u32[]{:S(2)}) %collective-permute-start.39) | collective-permute-done | bytes 196640 | tf_op jit(solution)/shard_map/ppermute | solution.py:30
  162.6 6.5 %shard_map.123 = (f32[16,96,256]{2,1,0:T(8,128)S(1)}, f32[16,96,256]{2,1,0:T(8,128)S(1)}, f32[12,96,256]{2,1,0:T(8,128)S(1)}, f32[12,96,256]{2,1,0:T(8,128)S(1)}...) custom-call(s32[128]{0:T(128)S(1)} %get-tuple-element.133.refs_0_, s32[128]{0:T(128)S(1)} %get-tuple-element.132.refs_1_, ...), custom_call_target="tpu_custom_call" | custom-call | flops 3221225472 | bytes 33554432 | tf_op jit(solution)/shard_map/pallas_call | solution.py:155
  175.8 5.8 %collective-permute-start.50 = (s16[400,256]{1,0:T(8,128)(2,1)S(1)}, s16[400,256]{1,0:T(8,128)(2,1)S(1)}, u32[]{:S(2)}, u32[]{:S(2)}) collective-permute-start(s16[400,256]{1,0:T(8,128)(2,1)S(1)} %get-tuple-element.116), channel_id=1, source_target_pairs={{0,2},{1,3},{2,0},{3,1},{4,6},{5,7},{6,4},{7,5},{8,10},{9,11},{10,... | collective-permute-start | bytes 614408 | tf_op jit(solution)/shard_map/ppermute | solution.py:30
  183.4 4.5 %collective-permute-done.53.refs_1_.refs_0_ = s16[1168,256]{1,0:T(8,128)(2,1)S(1)} collective-permute-done((s16[1168,256]{1,0:T(8,128)(2,1)S(1)}, s16[1168,256]{1,0:T(8,128)(2,1)S(1)}, u32[]{:S(2)}, u32[]{:S(2)}) %collective-permute-start.53) | collective-permute-done | bytes 598048 | tf_op jit(solution)/shard_map/ppermute | solution.py:30
  190.3 3.4 %collective-permute-done.51.refs_1_ = s16[400,256]{1,0:T(8,128)(2,1)S(1)} collective-permute-done((s16[400,256]{1,0:T(8,128)(2,1)S(1)}, s16[400,256]{1,0:T(8,128)(2,1)S(1)}, u32[]{:S(2)}, u32[]{:S(2)}) %collective-permute-start.51) | collective-permute-done | bytes 204832 | tf_op jit(solution)/shard_map/ppermute | solution.py:30
  199.2 5.1 %collective-permute-done.52.refs_2_ = s16[400,256]{1,0:T(8,128)(2,1)S(1)} collective-permute-done((s16[400,256]{1,0:T(8,128)(2,1)S(1)}, s16[400,256]{1,0:T(8,128)(2,1)S(1)}, u32[]{:S(2)}, u32[]{:S(2)}) %collective-permute-start.52) | collective-permute-done | bytes 204832 | tf_op jit(solution)/shard_map/ppermute | solution.py:30
  (129 shorter events, 86.3 us)
Async XLA Ops:
  2.0 16.3 %collective-permute-start.5 = (bf16[12,96,256]{2,1,0:T(8,128)(2,1)S(1)}, bf16[12,96,256]{2,1,0:T(8,128)(2,1)S(1)}, u32[]{:S(2)}, u32[]{:S(2)}) collective-permute-start(bf16[12,96,256]{2,1,0:T(8,128)(2,1)S(1)} %convert_bitcast_fusion.refs_14_), channel_id=1, source_target_pairs={{0,8},{8,0},{16,24},{24,16},{1,9},{9,1},{17,25},{25,17},{2,10},{10... | collective-permute-start | bytes 1769480 | tf_op jit(solution)/shard_map/ppermute | solution.py:30
  5.1 14.8 %collective-permute-start.4 = (bf16[12,96,256]{2,1,0:T(8,128)(2,1)S(1)}, bf16[12,96,256]{2,1,0:T(8,128)(2,1)S(1)}, u32[]{:S(2)}, u32[]{:S(2)}) collective-permute-start(bf16[12,96,256]{2,1,0:T(8,128)(2,1)S(1)} %convert_bitcast_fusion.refs_14_), channel_id=1, source_target_pairs={{0,16},{8,24},{16,0},{24,8},{1,17},{9,25},{17,1},{25,9},{2,18},{10... | collective-permute-start | bytes 1769480 | tf_op jit(solution)/shard_map/ppermute | solution.py:30
  6.6 15.0 %collective-permute-start.2 = (bf16[4,96,256]{2,1,0:T(8,128)(2,1)S(1)}, bf16[4,96,256]{2,1,0:T(8,128)(2,1)S(1)}, u32[]{:S(2)}, u32[]{:S(2)}) collective-permute-start(bf16[4,96,256]{2,1,0:T(8,128)(2,1)S(1)} %convert_element_type.9.refs_6_), channel_id=1, source_target_pairs={{0,6},{1,7},{2,4},{3,5},{4,2},{5,3},{6,0},{7,1},{8,14},{9,15},{10,... | collective-permute-start | bytes 589832 | tf_op jit(solution)/shard_map/ppermute | solution.py:30
  10.3 16.1 %collective-permute-start.1 = (bf16[4,96,256]{2,1,0:T(8,128)(2,1)S(1)}, bf16[4,96,256]{2,1,0:T(8,128)(2,1)S(1)}, u32[]{:S(2)}, u32[]{:S(2)}) collective-permute-start(bf16[4,96,256]{2,1,0:T(8,128)(2,1)S(1)} %convert_element_type.9.refs_6_), channel_id=1, source_target_pairs={{0,4},{1,5},{2,6},{3,7},{4,0},{5,1},{6,2},{7,3},{8,12},{9,13},{10,... | collective-permute-start | bytes 589832 | tf_op jit(solution)/shard_map/ppermute | solution.py:30
  10.3 16.1 %collective-permute-start = (bf16[4,96,256]{2,1,0:T(8,128)(2,1)S(1)}, bf16[4,96,256]{2,1,0:T(8,128)(2,1)S(1)}, u32[]{:S(2)}, u32[]{:S(2)}) collective-permute-start(bf16[4,96,256]{2,1,0:T(8,128)(2,1)S(1)} %convert_element_type.9.refs_6_), channel_id=1, source_target_pairs={{0,2},{1,3},{2,0},{3,1},{4,6},{5,7},{6,4},{7,5},{8,10},{9,11},{10,... | collective-permute-start | bytes 589832 | tf_op jit(solution)/shard_map/ppermute | solution.py:30
  40.1 15.5 %collective-permute-start.15 = (s16[1168,256]{1,0:T(8,128)(2,1)S(1)}, s16[1168,256]{1,0:T(8,128)(2,1)S(1)}, u32[]{:S(2)}, u32[]{:S(2)}) collective-permute-start(s16[1168,256]{1,0:T(8,128)(2,1)S(1)} %get-tuple-element.78), channel_id=1, source_target_pairs={{0,8},{8,0},{16,24},{24,16},{1,9},{9,1},{17,25},{25,17},{2,10},{10... | collective-permute-start | bytes 1794056 | tf_op jit(solution)/shard_map/ppermute | solution.py:30
  40.1 16.2 %collective-permute-start.16 = (s16[1168,256]{1,0:T(8,128)(2,1)S(1)}, s16[1168,256]{1,0:T(8,128)(2,1)S(1)}, u32[]{:S(2)}, u32[]{:S(2)}) collective-permute-start(s16[1168,256]{1,0:T(8,128)(2,1)S(1)} %get-tuple-element.79), channel_id=1, source_target_pairs={{0,16},{8,24},{16,0},{24,8},{1,17},{9,25},{17,1},{25,9},{2,18},{10... | collective-permute-start | bytes 1794056 | tf_op jit(solution)/shard_map/ppermute | solution.py:30
  43.5 13.1 %collective-permute-start.12 = (s16[400,256]{1,0:T(8,128)(2,1)S(1)}, s16[400,256]{1,0:T(8,128)(2,1)S(1)}, u32[]{:S(2)}, u32[]{:S(2)}) collective-permute-start(s16[400,256]{1,0:T(8,128)(2,1)S(1)} %get-tuple-element.74), channel_id=1, source_target_pairs={{0,2},{1,3},{2,0},{3,1},{4,6},{5,7},{6,4},{7,5},{8,10},{9,11},{10,... | collective-permute-start | bytes 614408 | tf_op jit(solution)/shard_map/ppermute | solution.py:30
  47.4 14.0 %collective-permute-start.13 = (s16[400,256]{1,0:T(8,128)(2,1)S(1)}, s16[400,256]{1,0:T(8,128)(2,1)S(1)}, u32[]{:S(2)}, u32[]{:S(2)}) collective-permute-start(s16[400,256]{1,0:T(8,128)(2,1)S(1)} %get-tuple-element.75), channel_id=1, source_target_pairs={{0,4},{1,5},{2,6},{3,7},{4,0},{5,1},{6,2},{7,3},{8,12},{9,13},{10,... | collective-permute-start | bytes 614408 | tf_op jit(solution)/shard_map/ppermute | solution.py:30
  73.2 12.6 %collective-permute-start.24 = (bf16[12,96,256]{2,1,0:T(8,128)(2,1)S(1)}, bf16[12,96,256]{2,1,0:T(8,128)(2,1)S(1)}, u32[]{:S(2)}, u32[]{:S(2)}) collective-permute-start(bf16[12,96,256]{2,1,0:T(8,128)(2,1)S(1)} %shard_map.116.refs_14_), channel_id=1, source_target_pairs={{0,8},{8,0},{16,24},{24,16},{1,9},{9,1},{17,25},{25,17},{2,10},{10... | collective-permute-start | bytes 1769480 | tf_op jit(solution)/shard_map/ppermute | solution.py:30
  74.1 13.2 %collective-permute-start.23 = (bf16[12,96,256]{2,1,0:T(8,128)(2,1)S(1)}, bf16[12,96,256]{2,1,0:T(8,128)(2,1)S(1)}, u32[]{:S(2)}, u32[]{:S(2)}) collective-permute-start(bf16[12,96,256]{2,1,0:T(8,128)(2,1)S(1)} %shard_map.116.refs_14_), channel_id=1, source_target_pairs={{0,16},{8,24},{16,0},{24,8},{1,17},{9,25},{17,1},{25,9},{2,18},{10... | collective-permute-start | bytes 1769480 | tf_op jit(solution)/shard_map/ppermute | solution.py:30
  79.4 15.2 %collective-permute-start.20 = (bf16[4,96,256]{2,1,0:T(8,128)(2,1)S(1)}, bf16[4,96,256]{2,1,0:T(8,128)(2,1)S(1)}, u32[]{:S(2)}, u32[]{:S(2)}) collective-permute-start(bf16[4,96,256]{2,1,0:T(8,128)(2,1)S(1)} %shard_map.117.refs_6_), channel_id=1, source_target_pairs={{0,4},{1,5},{2,6},{3,7},{4,0},{5,1},{6,2},{7,3},{8,12},{9,13},{10,... | collective-permute-start | bytes 589832 | tf_op jit(solution)/shard_map/ppermute | solution.py:30
  80.5 14.0 %collective-permute-start.19 = (bf16[4,96,256]{2,1,0:T(8,128)(2,1)S(1)}, bf16[4,96,256]{2,1,0:T(8,128)(2,1)S(1)}, u32[]{:S(2)}, u32[]{:S(2)}) collective-permute-start(bf16[4,96,256]{2,1,0:T(8,128)(2,1)S(1)} %shard_map.117.refs_6_), channel_id=1, source_target_pairs={{0,2},{1,3},{2,0},{3,1},{4,6},{5,7},{6,4},{7,5},{8,10},{9,11},{10,... | collective-permute-start | bytes 589832 | tf_op jit(solution)/shard_map/ppermute | solution.py:30
  106.5 15.5 %collective-permute-start.34 = (s16[1168,256]{1,0:T(8,128)(2,1)S(1)}, s16[1168,256]{1,0:T(8,128)(2,1)S(1)}, u32[]{:S(2)}, u32[]{:S(2)}) collective-permute-start(s16[1168,256]{1,0:T(8,128)(2,1)S(1)} %get-tuple-element.99), channel_id=1, source_target_pairs={{0,8},{8,0},{16,24},{24,16},{1,9},{9,1},{17,25},{25,17},{2,10},{10... | collective-permute-start | bytes 1794056 | tf_op jit(solution)/shard_map/ppermute | solution.py:30
  106.7 15.9 %collective-permute-start.35 = (s16[1168,256]{1,0:T(8,128)(2,1)S(1)}, s16[1168,256]{1,0:T(8,128)(2,1)S(1)}, u32[]{:S(2)}, u32[]{:S(2)}) collective-permute-start(s16[1168,256]{1,0:T(8,128)(2,1)S(1)} %get-tuple-element.100), channel_id=1, source_target_pairs={{0,16},{8,24},{16,0},{24,8},{1,17},{9,25},{17,1},{25,9},{2,18},{10... | collective-permute-start | bytes 1794056 | tf_op jit(solution)/shard_map/ppermute | solution.py:30
  109.9 14.6 %collective-permute-start.31 = (s16[400,256]{1,0:T(8,128)(2,1)S(1)}, s16[400,256]{1,0:T(8,128)(2,1)S(1)}, u32[]{:S(2)}, u32[]{:S(2)}) collective-permute-start(s16[400,256]{1,0:T(8,128)(2,1)S(1)} %get-tuple-element.95), channel_id=1, source_target_pairs={{0,2},{1,3},{2,0},{3,1},{4,6},{5,7},{6,4},{7,5},{8,10},{9,11},{10,... | collective-permute-start | bytes 614408 | tf_op jit(solution)/shard_map/ppermute | solution.py:30
  115.7 12.2 %collective-permute-start.32 = (s16[400,256]{1,0:T(8,128)(2,1)S(1)}, s16[400,256]{1,0:T(8,128)(2,1)S(1)}, u32[]{:S(2)}, u32[]{:S(2)}) collective-permute-start(s16[400,256]{1,0:T(8,128)(2,1)S(1)} %get-tuple-element.96), channel_id=1, source_target_pairs={{0,4},{1,5},{2,6},{3,7},{4,0},{5,1},{6,2},{7,3},{8,12},{9,13},{10,... | collective-permute-start | bytes 614408 | tf_op jit(solution)/shard_map/ppermute | solution.py:30
  138.9 12.7 %collective-permute-start.43 = (bf16[12,96,256]{2,1,0:T(8,128)(2,1)S(1)}, bf16[12,96,256]{2,1,0:T(8,128)(2,1)S(1)}, u32[]{:S(2)}, u32[]{:S(2)}) collective-permute-start(bf16[12,96,256]{2,1,0:T(8,128)(2,1)S(1)} %shard_map.121.refs_14_), channel_id=1, source_target_pairs={{0,8},{8,0},{16,24},{24,16},{1,9},{9,1},{17,25},{25,17},{2,10},{10... | collective-permute-start | bytes 1769480 | tf_op jit(solution)/shard_map/ppermute | solution.py:30
  139.8 13.2 %collective-permute-start.42 = (bf16[12,96,256]{2,1,0:T(8,128)(2,1)S(1)}, bf16[12,96,256]{2,1,0:T(8,128)(2,1)S(1)}, u32[]{:S(2)}, u32[]{:S(2)}) collective-permute-start(bf16[12,96,256]{2,1,0:T(8,128)(2,1)S(1)} %shard_map.121.refs_14_), channel_id=1, source_target_pairs={{0,16},{8,24},{16,0},{24,8},{1,17},{9,25},{17,1},{25,9},{2,18},{10... | collective-permute-start | bytes 1769480 | tf_op jit(solution)/shard_map/ppermute | solution.py:30
  145.1 15.2 %collective-permute-start.39 = (bf16[4,96,256]{2,1,0:T(8,128)(2,1)S(1)}, bf16[4,96,256]{2,1,0:T(8,128)(2,1)S(1)}, u32[]{:S(2)}, u32[]{:S(2)}) collective-permute-start(bf16[4,96,256]{2,1,0:T(8,128)(2,1)S(1)} %shard_map.122.refs_6_), channel_id=1, source_target_pairs={{0,4},{1,5},{2,6},{3,7},{4,0},{5,1},{6,2},{7,3},{8,12},{9,13},{10,... | collective-permute-start | bytes 589832 | tf_op jit(solution)/shard_map/ppermute | solution.py:30
  146.2 14.1 %collective-permute-start.38 = (bf16[4,96,256]{2,1,0:T(8,128)(2,1)S(1)}, bf16[4,96,256]{2,1,0:T(8,128)(2,1)S(1)}, u32[]{:S(2)}, u32[]{:S(2)}) collective-permute-start(bf16[4,96,256]{2,1,0:T(8,128)(2,1)S(1)} %shard_map.122.refs_6_), channel_id=1, source_target_pairs={{0,2},{1,3},{2,0},{3,1},{4,6},{5,7},{6,4},{7,5},{8,10},{9,11},{10,... | collective-permute-start | bytes 589832 | tf_op jit(solution)/shard_map/ppermute | solution.py:30
  172.4 15.5 %collective-permute-start.53 = (s16[1168,256]{1,0:T(8,128)(2,1)S(1)}, s16[1168,256]{1,0:T(8,128)(2,1)S(1)}, u32[]{:S(2)}, u32[]{:S(2)}) collective-permute-start(s16[1168,256]{1,0:T(8,128)(2,1)S(1)} %get-tuple-element.120), channel_id=1, source_target_pairs={{0,8},{8,0},{16,24},{24,16},{1,9},{9,1},{17,25},{25,17},{2,10},{10... | collective-permute-start | bytes 1794056 | tf_op jit(solution)/shard_map/ppermute | solution.py:30
  172.6 15.9 %collective-permute-start.54 = (s16[1168,256]{1,0:T(8,128)(2,1)S(1)}, s16[1168,256]{1,0:T(8,128)(2,1)S(1)}, u32[]{:S(2)}, u32[]{:S(2)}) collective-permute-start(s16[1168,256]{1,0:T(8,128)(2,1)S(1)} %get-tuple-element.121), channel_id=1, source_target_pairs={{0,16},{8,24},{16,0},{24,8},{1,17},{9,25},{17,1},{25,9},{2,18},{10... | collective-permute-start | bytes 1794056 | tf_op jit(solution)/shard_map/ppermute | solution.py:30
  175.8 14.5 %collective-permute-start.50 = (s16[400,256]{1,0:T(8,128)(2,1)S(1)}, s16[400,256]{1,0:T(8,128)(2,1)S(1)}, u32[]{:S(2)}, u32[]{:S(2)}) collective-permute-start(s16[400,256]{1,0:T(8,128)(2,1)S(1)} %get-tuple-element.116), channel_id=1, source_target_pairs={{0,2},{1,3},{2,0},{3,1},{4,6},{5,7},{6,4},{7,5},{8,10},{9,11},{10,... | collective-permute-start | bytes 614408 | tf_op jit(solution)/shard_map/ppermute | solution.py:30
  (40 other events, 345.3 us)

commit v5 on v4

--- a/solution.py
+++ b/solution.py
@@ -9,7 +9,7 @@
 from jax.sharding import PartitionSpec as P
 
 ITERS = 3
-DEPTH = 4
+DEPTH = 3
 COST = 1024
 LEVELS = 32000.0
 HIGHEST = 126.0
@@ -68,18 +68,7 @@
     sources, refs = refs[: elec_pieces + phon_pieces], refs[elec_pieces + phon_pieces :]
     whole, refs = refs[: len(elec_kept) + len(phon_kept)], refs[len(elec_kept) + len(phon_kept) :]
     coded, refs = refs[: len(plan)], refs[len(plan) :]
-    elec, phon, elec_totals, phon_totals, held, source_sems, tile_sems, out_sems = refs
-    loads = []
-    for target, pieces in ((elec, sources[:elec_pieces]), (phon, sources[elec_pieces:])):
-        first = 0
-        for piece in pieces:
-            span = piece.shape[0]
-            loads.append(
-                pltpu.make_async_copy(
-                    piece, target.at[pl.ds(first, span)], source_sems.at[len(loads)]
-                )
-            )
-            first += span
+    elec, phon, elec_totals, phon_totals, held, tile_sems, out_sems = refs
     groups = group_count[0]
 
     def fetch(index):
@@ -94,12 +83,14 @@
         def _():
             fetch(ahead).start()
 
-    for load in loads:
-        load.start()
+    for target, pieces in ((elec, sources[:elec_pieces]), (phon, sources[elec_pieces:])):
+        first = 0
+        for piece in pieces:
+            span = piece.shape[0]
+            target[pl.ds(first, span)] = piece[...]
+            first += span
     elec_totals[...] = jnp.zeros_like(elec_totals)
     phon_totals[...] = jnp.zeros_like(phon_totals)
-    for load in loads:
-        load.wait()
 
     def one_group(index, carry):
         @pl.when(index + DEPTH - 1 < groups)
@@ -158,7 +149,7 @@
             jax.ShapeDtypeStruct((end - first, rows, lanes), jnp.float32) for first, end in whole
         ]
         + [coded_shape(len(blocks), rows, lanes) for blocks in plan],
-        in_specs=[smem] * 5 + [any_space] * (1 + len(pieces)),
+        in_specs=[smem] * 5 + [any_space] + [vmem] * len(pieces),
         out_specs=[any_space] * len(whole) + [vmem] * len(plan),
         scratch_shapes=[
             pltpu.VMEM((elec_blocks, rows, lanes), jnp.bfloat16),
@@ -166,7 +157,6 @@
             pltpu.VMEM((elec_blocks + 1, rows, lanes), jnp.float32),
             pltpu.VMEM((phon_blocks + 1, rows, lanes), jnp.float32),
             pltpu.VMEM((DEPTH, group, side, side), jnp.bfloat16),
-            pltpu.SemaphoreType.DMA((len(pieces),)),
             pltpu.SemaphoreType.DMA((DEPTH,)),
             pltpu.SemaphoreType.DMA((len(whole),)),
         ],
@@ -204,7 +194,6 @@
             pltpu.VMEM((blocks_in, rows, lanes), jnp.bfloat16),
             pltpu.VMEM((blocks_out + 1, rows, lanes), jnp.float32),
             pltpu.VMEM((DEPTH, group, side, side), jnp.bfloat16),
-            pltpu.SemaphoreType.DMA((len(pieces),)),
             pltpu.SemaphoreType.DMA((DEPTH,)),
             pltpu.SemaphoreType.DMA((max(len(whole_sizes), 1),)),
         ],
@@ -318,7 +307,7 @@
 ):
     tile_set = tiles[0, 0]
     slots = tile_set.shape[0]
-    group = math.gcd(slots, 8)
+    group = math.gcd(slots, 16)
     elec_span = elec_dev.shape[0]
     phon_span = phon_dev.shape[1]
     elec_blocks = elec_span * n_ph

time: 208 us -> 208 us (level)
  starting transfers between devices: 87.3 us -> 57.1 us
  waiting for transfers between devices: 89.7 us -> 109 us
  Pallas kernels: 25.1 us -> 36.9 us
    ppermute x57, starting transfers between devices: 87.3 us -> 57.1 us  [send(): lax.ppermute(value, axis, [(place, place_of(place)) for place in range(si...]
    ppermute x57, waiting for transfers between devices: 89.7 us -> 109 us  [send(): lax.ppermute(value, axis, [(place, place_of(place)) for place in range(si...]
    pallas_call x3, Pallas kernels: 19.3 us -> 31.1 us  [drags(): pl.pallas_call(functools.partial(drags_body, group, (len(elec_pieces), le...]
  transfers between devices with their start and end apart: 57 -> 57, of which waited for: 40 -> 35; matrix products, arithmetic and copies ran while one was open for 1% -> 1% of each run, Pallas kernels for 1% -> 1%
where the time goes in v5:
time: 208 us
  waiting for transfers between devices  109 us (52%)
  starting transfers between devices  57.1 us (27%)
  Pallas kernels  36.9 us (18%)
    ppermute x57, waiting for transfers between devices, send(): lax.ppermute(value, axis, [(place, place_of(place)) for place in range(si...  109 us
    ppermute x57, starting transfers between devices, send(): lax.ppermute(value, axis, [(place, place_of(place)) for place in range(si...  57.1 us
    pallas_call x3, Pallas kernels, drags(): pl.pallas_call(functools.partial(drags_body, group, (len(elec_pieces), le...  31.1 us
  transfers between devices with their start and end apart: 57, of which 35 were waited for; matrix products, arithmetic and copies ran while one was open for 1% of the time, Pallas kernels for 1%

profile of v5, /device:TPU:0, one launch (start us, length us, event | category | flops | bytes accessed | tf_op | source)
XLA Modules:
  0.0 207.7 jit_solution(467483606297927152)
XLA Ops:
  6.6 3.7 %collective-permute-start.2 = (bf16[4,96,256]{2,1,0:T(8,128)(2,1)S(1)}, bf16[4,96,256]{2,1,0:T(8,128)(2,1)S(1)}, u32[]{:S(2)}, u32[]{:S(2)}) collective-permute-start(bf16[4,96,256]{2,1,0:T(8,128)(2,1)S(1)} %convert_element_type.9.refs_6_), channel_id=1, source_target_pairs={{0,6},{1,7},{2,4},{3,5},{4,2},{5,3},{6,0},{7,1},{8,14},{9,15},{10,... | collective-permute-start | bytes 589832 | tf_op jit(solution)/shard_map/ppermute | solution.py:30
  11.1 7.3 %collective-permute-done.5.refs_15_ = bf16[12,96,256]{2,1,0:T(8,128)(2,1)S(1)} collective-permute-done((bf16[12,96,256]{2,1,0:T(8,128)(2,1)S(1)}, bf16[12,96,256]{2,1,0:T(8,128)(2,1)S(1)}, u32[]{:S(2)}, u32[]{:S(2)}) %collective-permute-start.5) | collective-permute-done | bytes 589856 | tf_op jit(solution)/shard_map/ppermute | solution.py:30
  30.9 10.3 %shard_map.113 = (f32[16,96,256]{2,1,0:T(8,128)S(1)}, f32[16,96,256]{2,1,0:T(8,128)S(1)}, f32[12,96,256]{2,1,0:T(8,128)S(1)}, f32[12,96,256]{2,1,0:T(8,128)S(1)}...) custom-call(s32[128]{0:T(128)S(1)} %get-tuple-element.133.refs_0_, s32[128]{0:T(128)S(1)} %get-tuple-element.132.refs_1_, ...), custom_call_target="tpu_custom_call" | custom-call | flops 3221225472 | bytes 33554432 | tf_op jit(solution)/shard_map/pallas_call | solution.py:146
  41.7 3.1 %collective-permute-done.11.theirs = f32[16,96,256]{2,1,0:T(8,128)S(1)} collective-permute-done((f32[16,96,256]{2,1,0:T(8,128)S(1)}, f32[16,96,256]{2,1,0:T(8,128)S(1)}, u32[]{:S(2)}, u32[]{:S(2)}) %collective-permute-start.11) | collective-permute-done | bytes 1572896 | tf_op jit(solution)/shard_map/ppermute | solution.py:30
  48.3 9.0 %collective-permute-done.15.refs_1_.refs_0_ = s16[1168,256]{1,0:T(8,128)(2,1)S(1)} collective-permute-done((s16[1168,256]{1,0:T(8,128)(2,1)S(1)}, s16[1168,256]{1,0:T(8,128)(2,1)S(1)}, u32[]{:S(2)}, u32[]{:S(2)}) %collective-permute-start.15) | collective-permute-done | bytes 598048 | tf_op jit(solution)/shard_map/ppermute | solution.py:30
  65.6 5.8 %collective-permute-done.14.refs_2_ = s16[400,256]{1,0:T(8,128)(2,1)S(1)} collective-permute-done((s16[400,256]{1,0:T(8,128)(2,1)S(1)}, s16[400,256]{1,0:T(8,128)(2,1)S(1)}, u32[]{:S(2)}, u32[]{:S(2)}) %collective-permute-start.14) | collective-permute-done | bytes 204832 | tf_op jit(solution)/shard_map/ppermute | solution.py:30
  74.8 3.6 %collective-permute-start.20 = (bf16[4,96,256]{2,1,0:T(8,128)(2,1)S(1)}, bf16[4,96,256]{2,1,0:T(8,128)(2,1)S(1)}, u32[]{:S(2)}, u32[]{:S(2)}) collective-permute-start(bf16[4,96,256]{2,1,0:T(8,128)(2,1)S(1)} %shard_map.117.refs_6_), channel_id=1, source_target_pairs={{0,4},{1,5},{2,6},{3,7},{4,0},{5,1},{6,2},{7,3},{8,12},{9,13},{10,... | collective-permute-start | bytes 589832 | tf_op jit(solution)/shard_map/ppermute | solution.py:30
  78.7 6.8 %collective-permute-done.24.refs_15_ = bf16[12,96,256]{2,1,0:T(8,128)(2,1)S(1)} collective-permute-done((bf16[12,96,256]{2,1,0:T(8,128)(2,1)S(1)}, bf16[12,96,256]{2,1,0:T(8,128)(2,1)S(1)}, u32[]{:S(2)}, u32[]{:S(2)}) %collective-permute-start.24) | collective-permute-done | bytes 589856 | tf_op jit(solution)/shard_map/ppermute | solution.py:30
  88.0 5.3 %collective-permute-done.20.refs_8_ = bf16[4,96,256]{2,1,0:T(8,128)(2,1)S(1)} collective-permute-done((bf16[4,96,256]{2,1,0:T(8,128)(2,1)S(1)}, bf16[4,96,256]{2,1,0:T(8,128)(2,1)S(1)}, u32[]{:S(2)}, u32[]{:S(2)}) %collective-permute-start.20) | collective-permute-done | bytes 196640 | tf_op jit(solution)/shard_map/ppermute | solution.py:30
  96.1 10.5 %shard_map.118 = (f32[16,96,256]{2,1,0:T(8,128)S(1)}, f32[16,96,256]{2,1,0:T(8,128)S(1)}, f32[12,96,256]{2,1,0:T(8,128)S(1)}, f32[12,96,256]{2,1,0:T(8,128)S(1)}...) custom-call(s32[128]{0:T(128)S(1)} %get-tuple-element.133.refs_0_, s32[128]{0:T(128)S(1)} %get-tuple-element.132.refs_1_, ...), custom_call_target="tpu_custom_call" | custom-call | flops 3221225472 | bytes 33554432 | tf_op jit(solution)/shard_map/pallas_call | solution.py:146
  106.8 3.2 %collective-permute-done.30.theirs = f32[16,96,256]{2,1,0:T(8,128)S(1)} collective-permute-done((f32[16,96,256]{2,1,0:T(8,128)S(1)}, f32[16,96,256]{2,1,0:T(8,128)S(1)}, u32[]{:S(2)}, u32[]{:S(2)}) %collective-permute-start.30) | collective-permute-done | bytes 1572896 | tf_op jit(solution)/shard_map/ppermute | solution.py:30
  110.4 3.9 %collective-permute-start.31 = (s16[400,256]{1,0:T(8,128)(2,1)S(1)}, s16[400,256]{1,0:T(8,128)(2,1)S(1)}, u32[]{:S(2)}, u32[]{:S(2)}) collective-permute-start(s16[400,256]{1,0:T(8,128)(2,1)S(1)} %get-tuple-element.95), channel_id=1, source_target_pairs={{0,2},{1,3},{2,0},{3,1},{4,6},{5,7},{6,4},{7,5},{8,10},{9,11},{10,... | collective-permute-start | bytes 614408 | tf_op jit(solution)/shard_map/ppermute | solution.py:30
  114.3 8.3 %collective-permute-done.34.refs_1_.refs_0_ = s16[1168,256]{1,0:T(8,128)(2,1)S(1)} collective-permute-done((s16[1168,256]{1,0:T(8,128)(2,1)S(1)}, s16[1168,256]{1,0:T(8,128)(2,1)S(1)}, u32[]{:S(2)}, u32[]{:S(2)}) %collective-permute-start.34) | collective-permute-done | bytes 598048 | tf_op jit(solution)/shard_map/ppermute | solution.py:30
  122.6 3.8 %collective-permute-done.32.refs_1_ = s16[400,256]{1,0:T(8,128)(2,1)S(1)} collective-permute-done((s16[400,256]{1,0:T(8,128)(2,1)S(1)}, s16[400,256]{1,0:T(8,128)(2,1)S(1)}, u32[]{:S(2)}, u32[]{:S(2)}) %collective-permute-start.32) | collective-permute-done | bytes 204832 | tf_op jit(solution)/shard_map/ppermute | solution.py:30
  126.8 3.2 %collective-permute-start.36 = (s16[592,256]{1,0:T(8,128)(2,1)S(1)}, s16[592,256]{1,0:T(8,128)(2,1)S(1)}, u32[]{:S(2)}, u32[]{:S(2)}) collective-permute-start(s16[592,256]{1,0:T(8,128)(2,1)S(1)} %get-tuple-element.104), channel_id=1, source_target_pairs={{0,8},{8,0},{16,24},{24,16},{1,9},{9,1},{17,25},{25,17},{2,10},{10... | collective-permute-start | bytes 909320 | tf_op jit(solution)/shard_map/ppermute | solution.py:30
  130.0 8.6 %collective-permute-done.33.refs_2_ = s16[400,256]{1,0:T(8,128)(2,1)S(1)} collective-permute-done((s16[400,256]{1,0:T(8,128)(2,1)S(1)}, s16[400,256]{1,0:T(8,128)(2,1)S(1)}, u32[]{:S(2)}, u32[]{:S(2)}) %collective-permute-start.33) | collective-permute-done | bytes 204832 | tf_op jit(solution)/shard_map/ppermute | solution.py:30
  141.8 4.6 %collective-permute-start.39 = (bf16[4,96,256]{2,1,0:T(8,128)(2,1)S(1)}, bf16[4,96,256]{2,1,0:T(8,128)(2,1)S(1)}, u32[]{:S(2)}, u32[]{:S(2)}) collective-permute-start(bf16[4,96,256]{2,1,0:T(8,128)(2,1)S(1)} %shard_map.122.refs_6_), channel_id=1, source_target_pairs={{0,4},{1,5},{2,6},{3,7},{4,0},{5,1},{6,2},{7,3},{8,12},{9,13},{10,... | collective-permute-start | bytes 589832 | tf_op jit(solution)/shard_map/ppermute | solution.py:30
  146.4 7.0 %collective-permute-done.43.refs_15_ = bf16[12,96,256]{2,1,0:T(8,128)(2,1)S(1)} collective-permute-done((bf16[12,96,256]{2,1,0:T(8,128)(2,1)S(1)}, bf16[12,96,256]{2,1,0:T(8,128)(2,1)S(1)}, u32[]{:S(2)}, u32[]{:S(2)}) %collective-permute-start.43) | collective-permute-done | bytes 589856 | tf_op jit(solution)/shard_map/ppermute | solution.py:30
  156.5 4.6 %collective-permute-done.39.refs_8_ = bf16[4,96,256]{2,1,0:T(8,128)(2,1)S(1)} collective-permute-done((bf16[4,96,256]{2,1,0:T(8,128)(2,1)S(1)}, bf16[4,96,256]{2,1,0:T(8,128)(2,1)S(1)}, u32[]{:S(2)}, u32[]{:S(2)}) %collective-permute-start.39) | collective-permute-done | bytes 196640 | tf_op jit(solution)/shard_map/ppermute | solution.py:30
  163.4 10.3 %shard_map.123 = (f32[16,96,256]{2,1,0:T(8,128)S(1)}, f32[16,96,256]{2,1,0:T(8,128)S(1)}, f32[12,96,256]{2,1,0:T(8,128)S(1)}, f32[12,96,256]{2,1,0:T(8,128)S(1)}...) custom-call(s32[128]{0:T(128)S(1)} %get-tuple-element.133.refs_0_, s32[128]{0:T(128)S(1)} %get-tuple-element.132.refs_1_, ...), custom_call_target="tpu_custom_call" | custom-call | flops 3221225472 | bytes 33554432 | tf_op jit(solution)/shard_map/pallas_call | solution.py:146
  177.5 3.4 %collective-permute-start.50 = (s16[400,256]{1,0:T(8,128)(2,1)S(1)}, s16[400,256]{1,0:T(8,128)(2,1)S(1)}, u32[]{:S(2)}, u32[]{:S(2)}) collective-permute-start(s16[400,256]{1,0:T(8,128)(2,1)S(1)} %get-tuple-element.116), channel_id=1, source_target_pairs={{0,2},{1,3},{2,0},{3,1},{4,6},{5,7},{6,4},{7,5},{8,10},{9,11},{10,... | collective-permute-start | bytes 614408 | tf_op jit(solution)/shard_map/ppermute | solution.py:30
  181.4 8.2 %collective-permute-done.53.refs_1_.refs_0_ = s16[1168,256]{1,0:T(8,128)(2,1)S(1)} collective-permute-done((s16[1168,256]{1,0:T(8,128)(2,1)S(1)}, s16[1168,256]{1,0:T(8,128)(2,1)S(1)}, u32[]{:S(2)}, u32[]{:S(2)}) %collective-permute-start.53) | collective-permute-done | bytes 598048 | tf_op jit(solution)/shard_map/ppermute | solution.py:30
  189.7 3.4 %collective-permute-done.51.refs_1_ = s16[400,256]{1,0:T(8,128)(2,1)S(1)} collective-permute-done((s16[400,256]{1,0:T(8,128)(2,1)S(1)}, s16[400,256]{1,0:T(8,128)(2,1)S(1)}, u32[]{:S(2)}, u32[]{:S(2)}) %collective-permute-start.51) | collective-permute-done | bytes 204832 | tf_op jit(solution)/shard_map/ppermute | solution.py:30
  198.7 6.6 %collective-permute-done.52.refs_2_ = s16[400,256]{1,0:T(8,128)(2,1)S(1)} collective-permute-done((s16[400,256]{1,0:T(8,128)(2,1)S(1)}, s16[400,256]{1,0:T(8,128)(2,1)S(1)}, u32[]{:S(2)}, u32[]{:S(2)}) %collective-permute-start.52) | collective-permute-done | bytes 204832 | tf_op jit(solution)/shard_map/ppermute | solution.py:30
  (129 shorter events, 61.8 us)
Async XLA Ops:
  2.0 16.3 %collective-permute-start.5 = (bf16[12,96,256]{2,1,0:T(8,128)(2,1)S(1)}, bf16[12,96,256]{2,1,0:T(8,128)(2,1)S(1)}, u32[]{:S(2)}, u32[]{:S(2)}) collective-permute-start(bf16[12,96,256]{2,1,0:T(8,128)(2,1)S(1)} %convert_bitcast_fusion.refs_14_), channel_id=1, source_target_pairs={{0,8},{8,0},{16,24},{24,16},{1,9},{9,1},{17,25},{25,17},{2,10},{10... | collective-permute-start | bytes 1769480 | tf_op jit(solution)/shard_map/ppermute | solution.py:30
  5.1 14.8 %collective-permute-start.4 = (bf16[12,96,256]{2,1,0:T(8,128)(2,1)S(1)}, bf16[12,96,256]{2,1,0:T(8,128)(2,1)S(1)}, u32[]{:S(2)}, u32[]{:S(2)}) collective-permute-start(bf16[12,96,256]{2,1,0:T(8,128)(2,1)S(1)} %convert_bitcast_fusion.refs_14_), channel_id=1, source_target_pairs={{0,16},{8,24},{16,0},{24,8},{1,17},{9,25},{17,1},{25,9},{2,18},{10... | collective-permute-start | bytes 1769480 | tf_op jit(solution)/shard_map/ppermute | solution.py:30
  6.6 15.0 %collective-permute-start.2 = (bf16[4,96,256]{2,1,0:T(8,128)(2,1)S(1)}, bf16[4,96,256]{2,1,0:T(8,128)(2,1)S(1)}, u32[]{:S(2)}, u32[]{:S(2)}) collective-permute-start(bf16[4,96,256]{2,1,0:T(8,128)(2,1)S(1)} %convert_element_type.9.refs_6_), channel_id=1, source_target_pairs={{0,6},{1,7},{2,4},{3,5},{4,2},{5,3},{6,0},{7,1},{8,14},{9,15},{10,... | collective-permute-start | bytes 589832 | tf_op jit(solution)/shard_map/ppermute | solution.py:30
  10.3 16.1 %collective-permute-start.1 = (bf16[4,96,256]{2,1,0:T(8,128)(2,1)S(1)}, bf16[4,96,256]{2,1,0:T(8,128)(2,1)S(1)}, u32[]{:S(2)}, u32[]{:S(2)}) collective-permute-start(bf16[4,96,256]{2,1,0:T(8,128)(2,1)S(1)} %convert_element_type.9.refs_6_), channel_id=1, source_target_pairs={{0,4},{1,5},{2,6},{3,7},{4,0},{5,1},{6,2},{7,3},{8,12},{9,13},{10,... | collective-permute-start | bytes 589832 | tf_op jit(solution)/shard_map/ppermute | solution.py:30
  10.3 16.1 %collective-permute-start = (bf16[4,96,256]{2,1,0:T(8,128)(2,1)S(1)}, bf16[4,96,256]{2,1,0:T(8,128)(2,1)S(1)}, u32[]{:S(2)}, u32[]{:S(2)}) collective-permute-start(bf16[4,96,256]{2,1,0:T(8,128)(2,1)S(1)} %convert_element_type.9.refs_6_), channel_id=1, source_target_pairs={{0,2},{1,3},{2,0},{3,1},{4,6},{5,7},{6,4},{7,5},{8,10},{9,11},{10,... | collective-permute-start | bytes 589832 | tf_op jit(solution)/shard_map/ppermute | solution.py:30
  41.3 15.9 %collective-permute-start.15 = (s16[1168,256]{1,0:T(8,128)(2,1)S(1)}, s16[1168,256]{1,0:T(8,128)(2,1)S(1)}, u32[]{:S(2)}, u32[]{:S(2)}) collective-permute-start(s16[1168,256]{1,0:T(8,128)(2,1)S(1)} %get-tuple-element.78), channel_id=1, source_target_pairs={{0,8},{8,0},{16,24},{24,16},{1,9},{9,1},{17,25},{25,17},{2,10},{10... | collective-permute-start | bytes 1794056 | tf_op jit(solution)/shard_map/ppermute | solution.py:30
  41.4 15.8 %collective-permute-start.16 = (s16[1168,256]{1,0:T(8,128)(2,1)S(1)}, s16[1168,256]{1,0:T(8,128)(2,1)S(1)}, u32[]{:S(2)}, u32[]{:S(2)}) collective-permute-start(s16[1168,256]{1,0:T(8,128)(2,1)S(1)} %get-tuple-element.79), channel_id=1, source_target_pairs={{0,16},{8,24},{16,0},{24,8},{1,17},{9,25},{17,1},{25,9},{2,18},{10... | collective-permute-start | bytes 1794056 | tf_op jit(solution)/shard_map/ppermute | solution.py:30
  45.1 12.2 %collective-permute-start.12 = (s16[400,256]{1,0:T(8,128)(2,1)S(1)}, s16[400,256]{1,0:T(8,128)(2,1)S(1)}, u32[]{:S(2)}, u32[]{:S(2)}) collective-permute-start(s16[400,256]{1,0:T(8,128)(2,1)S(1)} %get-tuple-element.74), channel_id=1, source_target_pairs={{0,2},{1,3},{2,0},{3,1},{4,6},{5,7},{6,4},{7,5},{8,10},{9,11},{10,... | collective-permute-start | bytes 614408 | tf_op jit(solution)/shard_map/ppermute | solution.py:30
  71.8 13.6 %collective-permute-start.24 = (bf16[12,96,256]{2,1,0:T(8,128)(2,1)S(1)}, bf16[12,96,256]{2,1,0:T(8,128)(2,1)S(1)}, u32[]{:S(2)}, u32[]{:S(2)}) collective-permute-start(bf16[12,96,256]{2,1,0:T(8,128)(2,1)S(1)} %shard_map.116.refs_14_), channel_id=1, source_target_pairs={{0,8},{8,0},{16,24},{24,16},{1,9},{9,1},{17,25},{25,17},{2,10},{10... | collective-permute-start | bytes 1769480 | tf_op jit(solution)/shard_map/ppermute | solution.py:30
  73.5 13.0 %collective-permute-start.23 = (bf16[12,96,256]{2,1,0:T(8,128)(2,1)S(1)}, bf16[12,96,256]{2,1,0:T(8,128)(2,1)S(1)}, u32[]{:S(2)}, u32[]{:S(2)}) collective-permute-start(bf16[12,96,256]{2,1,0:T(8,128)(2,1)S(1)} %shard_map.116.refs_14_), channel_id=1, source_target_pairs={{0,16},{8,24},{16,0},{24,8},{1,17},{9,25},{17,1},{25,9},{2,18},{10... | collective-permute-start | bytes 1769480 | tf_op jit(solution)/shard_map/ppermute | solution.py:30
  74.2 13.1 %collective-permute-start.21 = (bf16[4,96,256]{2,1,0:T(8,128)(2,1)S(1)}, bf16[4,96,256]{2,1,0:T(8,128)(2,1)S(1)}, u32[]{:S(2)}, u32[]{:S(2)}) collective-permute-start(bf16[4,96,256]{2,1,0:T(8,128)(2,1)S(1)} %shard_map.117.refs_6_), channel_id=1, source_target_pairs={{0,6},{1,7},{2,4},{3,5},{4,2},{5,3},{6,0},{7,1},{8,14},{9,15},{10,... | collective-permute-start | bytes 589832 | tf_op jit(solution)/shard_map/ppermute | solution.py:30
  74.8 18.5 %collective-permute-start.20 = (bf16[4,96,256]{2,1,0:T(8,128)(2,1)S(1)}, bf16[4,96,256]{2,1,0:T(8,128)(2,1)S(1)}, u32[]{:S(2)}, u32[]{:S(2)}) collective-permute-start(bf16[4,96,256]{2,1,0:T(8,128)(2,1)S(1)} %shard_map.117.refs_6_), channel_id=1, source_target_pairs={{0,4},{1,5},{2,6},{3,7},{4,0},{5,1},{6,2},{7,3},{8,12},{9,13},{10,... | collective-permute-start | bytes 589832 | tf_op jit(solution)/shard_map/ppermute | solution.py:30
  78.4 14.9 %collective-permute-start.19 = (bf16[4,96,256]{2,1,0:T(8,128)(2,1)S(1)}, bf16[4,96,256]{2,1,0:T(8,128)(2,1)S(1)}, u32[]{:S(2)}, u32[]{:S(2)}) collective-permute-start(bf16[4,96,256]{2,1,0:T(8,128)(2,1)S(1)} %shard_map.117.refs_6_), channel_id=1, source_target_pairs={{0,2},{1,3},{2,0},{3,1},{4,6},{5,7},{6,4},{7,5},{8,10},{9,11},{10,... | collective-permute-start | bytes 589832 | tf_op jit(solution)/shard_map/ppermute | solution.py:30
  106.7 15.9 %collective-permute-start.34 = (s16[1168,256]{1,0:T(8,128)(2,1)S(1)}, s16[1168,256]{1,0:T(8,128)(2,1)S(1)}, u32[]{:S(2)}, u32[]{:S(2)}) collective-permute-start(s16[1168,256]{1,0:T(8,128)(2,1)S(1)} %get-tuple-element.99), channel_id=1, source_target_pairs={{0,8},{8,0},{16,24},{24,16},{1,9},{9,1},{17,25},{25,17},{2,10},{10... | collective-permute-start | bytes 1794056 | tf_op jit(solution)/shard_map/ppermute | solution.py:30
  106.7 15.8 %collective-permute-start.35 = (s16[1168,256]{1,0:T(8,128)(2,1)S(1)}, s16[1168,256]{1,0:T(8,128)(2,1)S(1)}, u32[]{:S(2)}, u32[]{:S(2)}) collective-permute-start(s16[1168,256]{1,0:T(8,128)(2,1)S(1)} %get-tuple-element.100), channel_id=1, source_target_pairs={{0,16},{8,24},{16,0},{24,8},{1,17},{9,25},{17,1},{25,9},{2,18},{10... | collective-permute-start | bytes 1794056 | tf_op jit(solution)/shard_map/ppermute | solution.py:30
  110.4 12.2 %collective-permute-start.31 = (s16[400,256]{1,0:T(8,128)(2,1)S(1)}, s16[400,256]{1,0:T(8,128)(2,1)S(1)}, u32[]{:S(2)}, u32[]{:S(2)}) collective-permute-start(s16[400,256]{1,0:T(8,128)(2,1)S(1)} %get-tuple-element.95), channel_id=1, source_target_pairs={{0,2},{1,3},{2,0},{3,1},{4,6},{5,7},{6,4},{7,5},{8,10},{9,11},{10,... | collective-permute-start | bytes 614408 | tf_op jit(solution)/shard_map/ppermute | solution.py:30
  139.3 14.1 %collective-permute-start.43 = (bf16[12,96,256]{2,1,0:T(8,128)(2,1)S(1)}, bf16[12,96,256]{2,1,0:T(8,128)(2,1)S(1)}, u32[]{:S(2)}, u32[]{:S(2)}) collective-permute-start(bf16[12,96,256]{2,1,0:T(8,128)(2,1)S(1)} %shard_map.121.refs_14_), channel_id=1, source_target_pairs={{0,8},{8,0},{16,24},{24,16},{1,9},{9,1},{17,25},{25,17},{2,10},{10... | collective-permute-start | bytes 1769480 | tf_op jit(solution)/shard_map/ppermute | solution.py:30
  139.9 13.9 %collective-permute-start.42 = (bf16[12,96,256]{2,1,0:T(8,128)(2,1)S(1)}, bf16[12,96,256]{2,1,0:T(8,128)(2,1)S(1)}, u32[]{:S(2)}, u32[]{:S(2)}) collective-permute-start(bf16[12,96,256]{2,1,0:T(8,128)(2,1)S(1)} %shard_map.121.refs_14_), channel_id=1, source_target_pairs={{0,16},{8,24},{16,0},{24,8},{1,17},{9,25},{17,1},{25,9},{2,18},{10... | collective-permute-start | bytes 1769480 | tf_op jit(solution)/shard_map/ppermute | solution.py:30
  141.5 13.8 %collective-permute-start.40 = (bf16[4,96,256]{2,1,0:T(8,128)(2,1)S(1)}, bf16[4,96,256]{2,1,0:T(8,128)(2,1)S(1)}, u32[]{:S(2)}, u32[]{:S(2)}) collective-permute-start(bf16[4,96,256]{2,1,0:T(8,128)(2,1)S(1)} %shard_map.122.refs_6_), channel_id=1, source_target_pairs={{0,6},{1,7},{2,4},{3,5},{4,2},{5,3},{6,0},{7,1},{8,14},{9,15},{10,... | collective-permute-start | bytes 589832 | tf_op jit(solution)/shard_map/ppermute | solution.py:30
  141.8 19.2 %collective-permute-start.39 = (bf16[4,96,256]{2,1,0:T(8,128)(2,1)S(1)}, bf16[4,96,256]{2,1,0:T(8,128)(2,1)S(1)}, u32[]{:S(2)}, u32[]{:S(2)}) collective-permute-start(bf16[4,96,256]{2,1,0:T(8,128)(2,1)S(1)} %shard_map.122.refs_6_), channel_id=1, source_target_pairs={{0,4},{1,5},{2,6},{3,7},{4,0},{5,1},{6,2},{7,3},{8,12},{9,13},{10,... | collective-permute-start | bytes 589832 | tf_op jit(solution)/shard_map/ppermute | solution.py:30
  146.4 14.7 %collective-permute-start.38 = (bf16[4,96,256]{2,1,0:T(8,128)(2,1)S(1)}, bf16[4,96,256]{2,1,0:T(8,128)(2,1)S(1)}, u32[]{:S(2)}, u32[]{:S(2)}) collective-permute-start(bf16[4,96,256]{2,1,0:T(8,128)(2,1)S(1)} %shard_map.122.refs_6_), channel_id=1, source_target_pairs={{0,2},{1,3},{2,0},{3,1},{4,6},{5,7},{6,4},{7,5},{8,10},{9,11},{10,... | collective-permute-start | bytes 589832 | tf_op jit(solution)/shard_map/ppermute | solution.py:30
  173.8 15.9 %collective-permute-start.53 = (s16[1168,256]{1,0:T(8,128)(2,1)S(1)}, s16[1168,256]{1,0:T(8,128)(2,1)S(1)}, u32[]{:S(2)}, u32[]{:S(2)}) collective-permute-start(s16[1168,256]{1,0:T(8,128)(2,1)S(1)} %get-tuple-element.120), channel_id=1, source_target_pairs={{0,8},{8,0},{16,24},{24,16},{1,9},{9,1},{17,25},{25,17},{2,10},{10... | collective-permute-start | bytes 1794056 | tf_op jit(solution)/shard_map/ppermute | solution.py:30
  173.8 15.8 %collective-permute-start.54 = (s16[1168,256]{1,0:T(8,128)(2,1)S(1)}, s16[1168,256]{1,0:T(8,128)(2,1)S(1)}, u32[]{:S(2)}, u32[]{:S(2)}) collective-permute-start(s16[1168,256]{1,0:T(8,128)(2,1)S(1)} %get-tuple-element.121), channel_id=1, source_target_pairs={{0,16},{8,24},{16,0},{24,8},{1,17},{9,25},{17,1},{25,9},{2,18},{10... | collective-permute-start | bytes 1794056 | tf_op jit(solution)/shard_map/ppermute | solution.py:30
  177.5 12.2 %collective-permute-start.50 = (s16[400,256]{1,0:T(8,128)(2,1)S(1)}, s16[400,256]{1,0:T(8,128)(2,1)S(1)}, u32[]{:S(2)}, u32[]{:S(2)}) collective-permute-start(s16[400,256]{1,0:T(8,128)(2,1)S(1)} %get-tuple-element.116), channel_id=1, source_target_pairs={{0,2},{1,3},{2,0},{3,1},{4,6},{5,7},{6,4},{7,5},{8,10},{9,11},{10,... | collective-permute-start | bytes 614408 | tf_op jit(solution)/shard_map/ppermute | solution.py:30
  (40 other events, 337.1 us)

commit v6 on v5

--- a/solution.py
+++ b/solution.py
@@ -291,6 +291,27 @@
     )(totals, *taken)
 
 
+def split_body(near, far, first, second):
+    half = first.shape[0]
+    first[...] = far[pl.ds(0, half)]
+    second[...] = near[pl.ds(half, second.shape[0])]
+
+
+def split(near, far, half):
+    blocks, rows, lanes = near.shape
+    vmem = pl.BlockSpec(memory_space=pltpu.VMEM)
+    return pl.pallas_call(
+        split_body,
+        out_shape=[
+            jax.ShapeDtypeStruct((size, rows, lanes), near.dtype) for size in (half, blocks - half)
+        ],
+        in_specs=[vmem] * 2,
+        out_specs=[vmem] * 2,
+        compiler_params=pltpu.CompilerParams(vmem_limit_bytes=32 * 1024 * 1024),
+        cost_estimate=small_cost(),
+    )(near, far)
+
+
 def local(
     n_el,
     n_ph,
@@ -362,7 +383,7 @@
         half = phon_span // 2
         if RELAY and n_el == 4 and half:
             near, far = over_el([value] * 2)
-            halves = after([far[:half], near[half:]], [near, far])
+            halves = split(near, far, half)
             passed = [
                 send(piece, "el", n_el, partner(n_el, step + 1)) for step, piece in enumerate(halves)
             ]

time: 208 us -> 204 us (0.981); the launches traced: 208 us -> 206 us
  starting transfers between devices: 57.1 us -> 71.7 us
  waiting for transfers between devices: 109 us -> 100 us
  Pallas kernels: 36.9 us -> 30.8 us
    ppermute x57, starting transfers between devices: 57.1 us -> 71.7 us  [send(): lax.ppermute(value, axis, [(place, place_of(place)) for place in range(si...]
    ppermute x57, waiting for transfers between devices: 109 us -> 100 us  [send(): lax.ppermute(value, axis, [(place, place_of(place)) for place in range(si...]
    pallas_call x3, Pallas kernels: 31.1 us -> 24 us  [drags(): pl.pallas_call(functools.partial(drags_body, group, (len(elec_pieces), le...]
  transfers between devices with their start and end apart: 57 -> 57, of which waited for: 35 -> 34; matrix products, arithmetic and copies ran while one was open for 1% -> 0% of each run, Pallas kernels for 1% -> 1%
where the time goes in v6:
time: 204 us; the launch traced here: 206 us
  waiting for transfers between devices  100 us (49%)
  starting transfers between devices  71.7 us (35%)
  Pallas kernels  30.8 us (15%)
    ppermute x57, waiting for transfers between devices, send(): lax.ppermute(value, axis, [(place, place_of(place)) for place in range(si...  100 us
    ppermute x57, starting transfers between devices, send(): lax.ppermute(value, axis, [(place, place_of(place)) for place in range(si...  71.7 us
    pallas_call x3, Pallas kernels, drags(): pl.pallas_call(functools.partial(drags_body, group, (len(elec_pieces), le...  24 us
  transfers between devices with their start and end apart: 57, of which 34 were waited for; matrix products, arithmetic and copies ran while one was open for 0% of the time, Pallas kernels for 1%

profile of v6, /device:TPU:0, one launch (start us, length us, event | category | flops | bytes accessed | tf_op | source)
XLA Modules:
  0.0 205.9 jit_solution(14360235816025282420)
XLA Ops:
  6.6 3.7 %collective-permute-start.2 = (bf16[4,96,256]{2,1,0:T(8,128)(2,1)S(1)}, bf16[4,96,256]{2,1,0:T(8,128)(2,1)S(1)}, u32[]{:S(2)}, u32[]{:S(2)}) collective-permute-start(bf16[4,96,256]{2,1,0:T(8,128)(2,1)S(1)} %convert_element_type.9.refs_6_), channel_id=1, source_target_pairs={{0,6},{1,7},{2,4},{3,5},{4,2},{5,3},{6,0},{7,1},{8,14},{9,15},{10,... | collective-permute-start | bytes 589832 | tf_op jit(solution)/shard_map/ppermute | solution.py:30
  11.1 7.4 %collective-permute-done.5.far.refs_16_ = bf16[12,96,256]{2,1,0:T(8,128)(2,1)S(1)} collective-permute-done((bf16[12,96,256]{2,1,0:T(8,128)(2,1)S(1)}, bf16[12,96,256]{2,1,0:T(8,128)(2,1)S(1)}, u32[]{:S(2)}, u32[]{:S(2)}) %collective-permute-start.5) | collective-permute-done | bytes 589856 | tf_op jit(solution)/shard_map/ppermute | solution.py:30
  30.3 8.0 %shard_map.114 = (f32[16,96,256]{2,1,0:T(8,128)S(1)}, f32[16,96,256]{2,1,0:T(8,128)S(1)}, f32[12,96,256]{2,1,0:T(8,128)S(1)}, f32[12,96,256]{2,1,0:T(8,128)S(1)}...) custom-call(s32[128]{0:T(128)S(1)} %get-tuple-element.133.refs_0_, s32[128]{0:T(128)S(1)} %get-tuple-element.132.refs_1_, ...), custom_call_target="tpu_custom_call" | custom-call | flops 3221225472 | bytes 33554432 | tf_op jit(solution)/shard_map/pallas_call | solution.py:146
  38.4 5.1 %collective-permute-start.15 = (s16[1168,256]{1,0:T(8,128)(2,1)S(1)}, s16[1168,256]{1,0:T(8,128)(2,1)S(1)}, u32[]{:S(2)}, u32[]{:S(2)}) collective-permute-start(s16[1168,256]{1,0:T(8,128)(2,1)S(1)} %get-tuple-element.78), channel_id=1, source_target_pairs={{0,8},{8,0},{16,24},{24,16},{1,9},{9,1},{17,25},{25,17},{2,10},{10... | collective-permute-start | bytes 1794056 | tf_op jit(solution)/shard_map/ppermute | solution.py:30
  47.7 9.8 %collective-permute-done.15.refs_1_.refs_0_ = s16[1168,256]{1,0:T(8,128)(2,1)S(1)} collective-permute-done((s16[1168,256]{1,0:T(8,128)(2,1)S(1)}, s16[1168,256]{1,0:T(8,128)(2,1)S(1)}, u32[]{:S(2)}, u32[]{:S(2)}) %collective-permute-start.15) | collective-permute-done | bytes 598048 | tf_op jit(solution)/shard_map/ppermute | solution.py:30
  63.1 7.6 %collective-permute-done.14.refs_2_ = s16[400,256]{1,0:T(8,128)(2,1)S(1)} collective-permute-done((s16[400,256]{1,0:T(8,128)(2,1)S(1)}, s16[400,256]{1,0:T(8,128)(2,1)S(1)}, u32[]{:S(2)}, u32[]{:S(2)}) %collective-permute-start.14) | collective-permute-done | bytes 204832 | tf_op jit(solution)/shard_map/ppermute | solution.py:30
  73.5 4.4 %collective-permute-start.20 = (bf16[4,96,256]{2,1,0:T(8,128)(2,1)S(1)}, bf16[4,96,256]{2,1,0:T(8,128)(2,1)S(1)}, u32[]{:S(2)}, u32[]{:S(2)}) collective-permute-start(bf16[4,96,256]{2,1,0:T(8,128)(2,1)S(1)} %shard_map.118.refs_6_), channel_id=1, source_target_pairs={{0,4},{1,5},{2,6},{3,7},{4,0},{5,1},{6,2},{7,3},{8,12},{9,13},{10,... | collective-permute-start | bytes 589832 | tf_op jit(solution)/shard_map/ppermute | solution.py:30
  77.8 6.0 %collective-permute-done.24.far.refs_16_ = bf16[12,96,256]{2,1,0:T(8,128)(2,1)S(1)} collective-permute-done((bf16[12,96,256]{2,1,0:T(8,128)(2,1)S(1)}, bf16[12,96,256]{2,1,0:T(8,128)(2,1)S(1)}, u32[]{:S(2)}, u32[]{:S(2)}) %collective-permute-start.24) | collective-permute-done | bytes 589856 | tf_op jit(solution)/shard_map/ppermute | solution.py:30
  86.1 5.9 %collective-permute-done.20.refs_8_ = bf16[4,96,256]{2,1,0:T(8,128)(2,1)S(1)} collective-permute-done((bf16[4,96,256]{2,1,0:T(8,128)(2,1)S(1)}, bf16[4,96,256]{2,1,0:T(8,128)(2,1)S(1)}, u32[]{:S(2)}, u32[]{:S(2)}) %collective-permute-start.20) | collective-permute-done | bytes 196640 | tf_op jit(solution)/shard_map/ppermute | solution.py:30
  94.1 8.1 %shard_map.120 = (f32[16,96,256]{2,1,0:T(8,128)S(1)}, f32[16,96,256]{2,1,0:T(8,128)S(1)}, f32[12,96,256]{2,1,0:T(8,128)S(1)}, f32[12,96,256]{2,1,0:T(8,128)S(1)}...) custom-call(s32[128]{0:T(128)S(1)} %get-tuple-element.133.refs_0_, s32[128]{0:T(128)S(1)} %get-tuple-element.132.refs_1_, ...), custom_call_target="tpu_custom_call" | custom-call | flops 3221225472 | bytes 33554432 | tf_op jit(solution)/shard_map/pallas_call | solution.py:146
  102.3 5.9 %collective-permute-start.34 = (s16[1168,256]{1,0:T(8,128)(2,1)S(1)}, s16[1168,256]{1,0:T(8,128)(2,1)S(1)}, u32[]{:S(2)}, u32[]{:S(2)}) collective-permute-start(s16[1168,256]{1,0:T(8,128)(2,1)S(1)} %get-tuple-element.99), channel_id=1, source_target_pairs={{0,8},{8,0},{16,24},{24,16},{1,9},{9,1},{17,25},{25,17},{2,10},{10... | collective-permute-start | bytes 1794056 | tf_op jit(solution)/shard_map/ppermute | solution.py:30
  108.5 5.3 %collective-permute-start.31 = (s16[400,256]{1,0:T(8,128)(2,1)S(1)}, s16[400,256]{1,0:T(8,128)(2,1)S(1)}, u32[]{:S(2)}, u32[]{:S(2)}) collective-permute-start(s16[400,256]{1,0:T(8,128)(2,1)S(1)} %get-tuple-element.95), channel_id=1, source_target_pairs={{0,2},{1,3},{2,0},{3,1},{4,6},{5,7},{6,4},{7,5},{8,10},{9,11},{10,... | collective-permute-start | bytes 614408 | tf_op jit(solution)/shard_map/ppermute | solution.py:30
  113.8 8.4 %collective-permute-done.34.refs_1_.refs_0_ = s16[1168,256]{1,0:T(8,128)(2,1)S(1)} collective-permute-done((s16[1168,256]{1,0:T(8,128)(2,1)S(1)}, s16[1168,256]{1,0:T(8,128)(2,1)S(1)}, u32[]{:S(2)}, u32[]{:S(2)}) %collective-permute-start.34) | collective-permute-done | bytes 598048 | tf_op jit(solution)/shard_map/ppermute | solution.py:30
  126.2 3.4 %collective-permute-start.37 = (s16[592,256]{1,0:T(8,128)(2,1)S(1)}, s16[592,256]{1,0:T(8,128)(2,1)S(1)}, u32[]{:S(2)}, u32[]{:S(2)}) collective-permute-start(s16[592,256]{1,0:T(8,128)(2,1)S(1)} %get-tuple-element.105), channel_id=1, source_target_pairs={{0,16},{8,24},{16,0},{24,8},{1,17},{9,25},{17,1},{25,9},{2,18},{10... | collective-permute-start | bytes 909320 | tf_op jit(solution)/shard_map/ppermute | solution.py:30
  129.8 7.7 %collective-permute-done.33.refs_2_ = s16[400,256]{1,0:T(8,128)(2,1)S(1)} collective-permute-done((s16[400,256]{1,0:T(8,128)(2,1)S(1)}, s16[400,256]{1,0:T(8,128)(2,1)S(1)}, u32[]{:S(2)}, u32[]{:S(2)}) %collective-permute-start.33) | collective-permute-done | bytes 204832 | tf_op jit(solution)/shard_map/ppermute | solution.py:30
  140.6 3.9 %collective-permute-start.39 = (bf16[4,96,256]{2,1,0:T(8,128)(2,1)S(1)}, bf16[4,96,256]{2,1,0:T(8,128)(2,1)S(1)}, u32[]{:S(2)}, u32[]{:S(2)}) collective-permute-start(bf16[4,96,256]{2,1,0:T(8,128)(2,1)S(1)} %shard_map.124.refs_6_), channel_id=1, source_target_pairs={{0,4},{1,5},{2,6},{3,7},{4,0},{5,1},{6,2},{7,3},{8,12},{9,13},{10,... | collective-permute-start | bytes 589832 | tf_op jit(solution)/shard_map/ppermute | solution.py:30
  144.4 7.0 %collective-permute-done.43.far.refs_16_ = bf16[12,96,256]{2,1,0:T(8,128)(2,1)S(1)} collective-permute-done((bf16[12,96,256]{2,1,0:T(8,128)(2,1)S(1)}, bf16[12,96,256]{2,1,0:T(8,128)(2,1)S(1)}, u32[]{:S(2)}, u32[]{:S(2)}) %collective-permute-start.43) | collective-permute-done | bytes 589856 | tf_op jit(solution)/shard_map/ppermute | solution.py:30
  153.9 4.6 %collective-permute-done.39.refs_8_ = bf16[4,96,256]{2,1,0:T(8,128)(2,1)S(1)} collective-permute-done((bf16[4,96,256]{2,1,0:T(8,128)(2,1)S(1)}, bf16[4,96,256]{2,1,0:T(8,128)(2,1)S(1)}, u32[]{:S(2)}, u32[]{:S(2)}) %collective-permute-start.39) | collective-permute-done | bytes 196640 | tf_op jit(solution)/shard_map/ppermute | solution.py:30
  161.3 7.9 %shard_map.126 = (f32[16,96,256]{2,1,0:T(8,128)S(1)}, f32[16,96,256]{2,1,0:T(8,128)S(1)}, f32[12,96,256]{2,1,0:T(8,128)S(1)}, f32[12,96,256]{2,1,0:T(8,128)S(1)}...) custom-call(s32[128]{0:T(128)S(1)} %get-tuple-element.133.refs_0_, s32[128]{0:T(128)S(1)} %get-tuple-element.132.refs_1_, ...), custom_call_target="tpu_custom_call" | custom-call | flops 3221225472 | bytes 33554432 | tf_op jit(solution)/shard_map/pallas_call | solution.py:146
  169.3 6.1 %collective-permute-start.53 = (s16[1168,256]{1,0:T(8,128)(2,1)S(1)}, s16[1168,256]{1,0:T(8,128)(2,1)S(1)}, u32[]{:S(2)}, u32[]{:S(2)}) collective-permute-start(s16[1168,256]{1,0:T(8,128)(2,1)S(1)} %get-tuple-element.120), channel_id=1, source_target_pairs={{0,8},{8,0},{16,24},{24,16},{1,9},{9,1},{17,25},{25,17},{2,10},{10... | collective-permute-start | bytes 1794056 | tf_op jit(solution)/shard_map/ppermute | solution.py:30
  175.8 4.0 %collective-permute-start.50 = (s16[400,256]{1,0:T(8,128)(2,1)S(1)}, s16[400,256]{1,0:T(8,128)(2,1)S(1)}, u32[]{:S(2)}, u32[]{:S(2)}) collective-permute-start(s16[400,256]{1,0:T(8,128)(2,1)S(1)} %get-tuple-element.116), channel_id=1, source_target_pairs={{0,2},{1,3},{2,0},{3,1},{4,6},{5,7},{6,4},{7,5},{8,10},{9,11},{10,... | collective-permute-start | bytes 614408 | tf_op jit(solution)/shard_map/ppermute | solution.py:30
  180.4 9.2 %collective-permute-done.53.refs_1_.refs_0_ = s16[1168,256]{1,0:T(8,128)(2,1)S(1)} collective-permute-done((s16[1168,256]{1,0:T(8,128)(2,1)S(1)}, s16[1168,256]{1,0:T(8,128)(2,1)S(1)}, u32[]{:S(2)}, u32[]{:S(2)}) %collective-permute-start.53) | collective-permute-done | bytes 598048 | tf_op jit(solution)/shard_map/ppermute | solution.py:30
  192.2 3.4 %collective-permute-start.56 = (s16[592,256]{1,0:T(8,128)(2,1)S(1)}, s16[592,256]{1,0:T(8,128)(2,1)S(1)}, u32[]{:S(2)}, u32[]{:S(2)}) collective-permute-start(s16[592,256]{1,0:T(8,128)(2,1)S(1)} %get-tuple-element.126), channel_id=1, source_target_pairs={{0,16},{8,24},{16,0},{24,8},{1,17},{9,25},{17,1},{25,9},{2,18},{10... | collective-permute-start | bytes 909320 | tf_op jit(solution)/shard_map/ppermute | solution.py:30
  196.3 7.1 %collective-permute-done.52.refs_2_ = s16[400,256]{1,0:T(8,128)(2,1)S(1)} collective-permute-done((s16[400,256]{1,0:T(8,128)(2,1)S(1)}, s16[400,256]{1,0:T(8,128)(2,1)S(1)}, u32[]{:S(2)}, u32[]{:S(2)}) %collective-permute-start.52) | collective-permute-done | bytes 204832 | tf_op jit(solution)/shard_map/ppermute | solution.py:30
  (126 shorter events, 54.4 us)
Async XLA Ops:
  2.0 16.4 %collective-permute-start.5 = (bf16[12,96,256]{2,1,0:T(8,128)(2,1)S(1)}, bf16[12,96,256]{2,1,0:T(8,128)(2,1)S(1)}, u32[]{:S(2)}, u32[]{:S(2)}) collective-permute-start(bf16[12,96,256]{2,1,0:T(8,128)(2,1)S(1)} %convert_bitcast_fusion.refs_14_), channel_id=1, source_target_pairs={{0,16},{8,24},{16,0},{24,8},{1,17},{9,25},{17,1},{25,9},{2,18},{10... | collective-permute-start | bytes 1769480 | tf_op jit(solution)/shard_map/ppermute | solution.py:30
  5.1 14.8 %collective-permute-start.4 = (bf16[12,96,256]{2,1,0:T(8,128)(2,1)S(1)}, bf16[12,96,256]{2,1,0:T(8,128)(2,1)S(1)}, u32[]{:S(2)}, u32[]{:S(2)}) collective-permute-start(bf16[12,96,256]{2,1,0:T(8,128)(2,1)S(1)} %convert_bitcast_fusion.refs_14_), channel_id=1, source_target_pairs={{0,8},{8,0},{16,24},{24,16},{1,9},{9,1},{17,25},{25,17},{2,10},{10... | collective-permute-start | bytes 1769480 | tf_op jit(solution)/shard_map/ppermute | solution.py:30
  6.6 15.6 %collective-permute-start.2 = (bf16[4,96,256]{2,1,0:T(8,128)(2,1)S(1)}, bf16[4,96,256]{2,1,0:T(8,128)(2,1)S(1)}, u32[]{:S(2)}, u32[]{:S(2)}) collective-permute-start(bf16[4,96,256]{2,1,0:T(8,128)(2,1)S(1)} %convert_element_type.9.refs_6_), channel_id=1, source_target_pairs={{0,6},{1,7},{2,4},{3,5},{4,2},{5,3},{6,0},{7,1},{8,14},{9,15},{10,... | collective-permute-start | bytes 589832 | tf_op jit(solution)/shard_map/ppermute | solution.py:30
  10.3 16.1 %collective-permute-start.1 = (bf16[4,96,256]{2,1,0:T(8,128)(2,1)S(1)}, bf16[4,96,256]{2,1,0:T(8,128)(2,1)S(1)}, u32[]{:S(2)}, u32[]{:S(2)}) collective-permute-start(bf16[4,96,256]{2,1,0:T(8,128)(2,1)S(1)} %convert_element_type.9.refs_6_), channel_id=1, source_target_pairs={{0,4},{1,5},{2,6},{3,7},{4,0},{5,1},{6,2},{7,3},{8,12},{9,13},{10,... | collective-permute-start | bytes 589832 | tf_op jit(solution)/shard_map/ppermute | solution.py:30
  10.3 16.1 %collective-permute-start = (bf16[4,96,256]{2,1,0:T(8,128)(2,1)S(1)}, bf16[4,96,256]{2,1,0:T(8,128)(2,1)S(1)}, u32[]{:S(2)}, u32[]{:S(2)}) collective-permute-start(bf16[4,96,256]{2,1,0:T(8,128)(2,1)S(1)} %convert_element_type.9.refs_6_), channel_id=1, source_target_pairs={{0,2},{1,3},{2,0},{3,1},{4,6},{5,7},{6,4},{7,5},{8,10},{9,11},{10,... | collective-permute-start | bytes 589832 | tf_op jit(solution)/shard_map/ppermute | solution.py:30
  38.4 19.2 %collective-permute-start.15 = (s16[1168,256]{1,0:T(8,128)(2,1)S(1)}, s16[1168,256]{1,0:T(8,128)(2,1)S(1)}, u32[]{:S(2)}, u32[]{:S(2)}) collective-permute-start(s16[1168,256]{1,0:T(8,128)(2,1)S(1)} %get-tuple-element.78), channel_id=1, source_target_pairs={{0,8},{8,0},{16,24},{24,16},{1,9},{9,1},{17,25},{25,17},{2,10},{10... | collective-permute-start | bytes 1794056 | tf_op jit(solution)/shard_map/ppermute | solution.py:30
  43.4 15.6 %collective-permute-start.16 = (s16[1168,256]{1,0:T(8,128)(2,1)S(1)}, s16[1168,256]{1,0:T(8,128)(2,1)S(1)}, u32[]{:S(2)}, u32[]{:S(2)}) collective-permute-start(s16[1168,256]{1,0:T(8,128)(2,1)S(1)} %get-tuple-element.79), channel_id=1, source_target_pairs={{0,16},{8,24},{16,0},{24,8},{1,17},{9,25},{17,1},{25,9},{2,18},{10... | collective-permute-start | bytes 1794056 | tf_op jit(solution)/shard_map/ppermute | solution.py:30
  43.8 15.2 %collective-permute-start.12 = (s16[400,256]{1,0:T(8,128)(2,1)S(1)}, s16[400,256]{1,0:T(8,128)(2,1)S(1)}, u32[]{:S(2)}, u32[]{:S(2)}) collective-permute-start(s16[400,256]{1,0:T(8,128)(2,1)S(1)} %get-tuple-element.74), channel_id=1, source_target_pairs={{0,2},{1,3},{2,0},{3,1},{4,6},{5,7},{6,4},{7,5},{8,10},{9,11},{10,... | collective-permute-start | bytes 614408 | tf_op jit(solution)/shard_map/ppermute | solution.py:30
  71.2 12.7 %collective-permute-start.24 = (bf16[12,96,256]{2,1,0:T(8,128)(2,1)S(1)}, bf16[12,96,256]{2,1,0:T(8,128)(2,1)S(1)}, u32[]{:S(2)}, u32[]{:S(2)}) collective-permute-start(bf16[12,96,256]{2,1,0:T(8,128)(2,1)S(1)} %shard_map.117.refs_14_), channel_id=1, source_target_pairs={{0,16},{8,24},{16,0},{24,8},{1,17},{9,25},{17,1},{25,9},{2,18},{10... | collective-permute-start | bytes 1769480 | tf_op jit(solution)/shard_map/ppermute | solution.py:30
  71.5 12.8 %collective-permute-start.23 = (bf16[12,96,256]{2,1,0:T(8,128)(2,1)S(1)}, bf16[12,96,256]{2,1,0:T(8,128)(2,1)S(1)}, u32[]{:S(2)}, u32[]{:S(2)}) collective-permute-start(bf16[12,96,256]{2,1,0:T(8,128)(2,1)S(1)} %shard_map.117.refs_14_), channel_id=1, source_target_pairs={{0,8},{8,0},{16,24},{24,16},{1,9},{9,1},{17,25},{25,17},{2,10},{10... | collective-permute-start | bytes 1769480 | tf_op jit(solution)/shard_map/ppermute | solution.py:30
  72.1 13.0 %collective-permute-start.21 = (bf16[4,96,256]{2,1,0:T(8,128)(2,1)S(1)}, bf16[4,96,256]{2,1,0:T(8,128)(2,1)S(1)}, u32[]{:S(2)}, u32[]{:S(2)}) collective-permute-start(bf16[4,96,256]{2,1,0:T(8,128)(2,1)S(1)} %shard_map.118.refs_6_), channel_id=1, source_target_pairs={{0,6},{1,7},{2,4},{3,5},{4,2},{5,3},{6,0},{7,1},{8,14},{9,15},{10,... | collective-permute-start | bytes 589832 | tf_op jit(solution)/shard_map/ppermute | solution.py:30
  73.5 18.6 %collective-permute-start.20 = (bf16[4,96,256]{2,1,0:T(8,128)(2,1)S(1)}, bf16[4,96,256]{2,1,0:T(8,128)(2,1)S(1)}, u32[]{:S(2)}, u32[]{:S(2)}) collective-permute-start(bf16[4,96,256]{2,1,0:T(8,128)(2,1)S(1)} %shard_map.118.refs_6_), channel_id=1, source_target_pairs={{0,4},{1,5},{2,6},{3,7},{4,0},{5,1},{6,2},{7,3},{8,12},{9,13},{10,... | collective-permute-start | bytes 589832 | tf_op jit(solution)/shard_map/ppermute | solution.py:30
  77.8 14.2 %collective-permute-start.19 = (bf16[4,96,256]{2,1,0:T(8,128)(2,1)S(1)}, bf16[4,96,256]{2,1,0:T(8,128)(2,1)S(1)}, u32[]{:S(2)}, u32[]{:S(2)}) collective-permute-start(bf16[4,96,256]{2,1,0:T(8,128)(2,1)S(1)} %shard_map.118.refs_6_), channel_id=1, source_target_pairs={{0,2},{1,3},{2,0},{3,1},{4,6},{5,7},{6,4},{7,5},{8,10},{9,11},{10,... | collective-permute-start | bytes 589832 | tf_op jit(solution)/shard_map/ppermute | solution.py:30
  102.3 20.0 %collective-permute-start.34 = (s16[1168,256]{1,0:T(8,128)(2,1)S(1)}, s16[1168,256]{1,0:T(8,128)(2,1)S(1)}, u32[]{:S(2)}, u32[]{:S(2)}) collective-permute-start(s16[1168,256]{1,0:T(8,128)(2,1)S(1)} %get-tuple-element.99), channel_id=1, source_target_pairs={{0,8},{8,0},{16,24},{24,16},{1,9},{9,1},{17,25},{25,17},{2,10},{10... | collective-permute-start | bytes 1794056 | tf_op jit(solution)/shard_map/ppermute | solution.py:30
  108.1 15.6 %collective-permute-start.35 = (s16[1168,256]{1,0:T(8,128)(2,1)S(1)}, s16[1168,256]{1,0:T(8,128)(2,1)S(1)}, u32[]{:S(2)}, u32[]{:S(2)}) collective-permute-start(s16[1168,256]{1,0:T(8,128)(2,1)S(1)} %get-tuple-element.100), channel_id=1, source_target_pairs={{0,16},{8,24},{16,0},{24,8},{1,17},{9,25},{17,1},{25,9},{2,18},{10... | collective-permute-start | bytes 1794056 | tf_op jit(solution)/shard_map/ppermute | solution.py:30
  108.5 15.2 %collective-permute-start.31 = (s16[400,256]{1,0:T(8,128)(2,1)S(1)}, s16[400,256]{1,0:T(8,128)(2,1)S(1)}, u32[]{:S(2)}, u32[]{:S(2)}) collective-permute-start(s16[400,256]{1,0:T(8,128)(2,1)S(1)} %get-tuple-element.95), channel_id=1, source_target_pairs={{0,2},{1,3},{2,0},{3,1},{4,6},{5,7},{6,4},{7,5},{8,10},{9,11},{10,... | collective-permute-start | bytes 614408 | tf_op jit(solution)/shard_map/ppermute | solution.py:30
  138.0 13.4 %collective-permute-start.43 = (bf16[12,96,256]{2,1,0:T(8,128)(2,1)S(1)}, bf16[12,96,256]{2,1,0:T(8,128)(2,1)S(1)}, u32[]{:S(2)}, u32[]{:S(2)}) collective-permute-start(bf16[12,96,256]{2,1,0:T(8,128)(2,1)S(1)} %shard_map.123.refs_14_), channel_id=1, source_target_pairs={{0,16},{8,24},{16,0},{24,8},{1,17},{9,25},{17,1},{25,9},{2,18},{10... | collective-permute-start | bytes 1769480 | tf_op jit(solution)/shard_map/ppermute | solution.py:30
  138.5 13.4 %collective-permute-start.42 = (bf16[12,96,256]{2,1,0:T(8,128)(2,1)S(1)}, bf16[12,96,256]{2,1,0:T(8,128)(2,1)S(1)}, u32[]{:S(2)}, u32[]{:S(2)}) collective-permute-start(bf16[12,96,256]{2,1,0:T(8,128)(2,1)S(1)} %shard_map.123.refs_14_), channel_id=1, source_target_pairs={{0,8},{8,0},{16,24},{24,16},{1,9},{9,1},{17,25},{25,17},{2,10},{10... | collective-permute-start | bytes 1769480 | tf_op jit(solution)/shard_map/ppermute | solution.py:30
  139.1 13.6 %collective-permute-start.40 = (bf16[4,96,256]{2,1,0:T(8,128)(2,1)S(1)}, bf16[4,96,256]{2,1,0:T(8,128)(2,1)S(1)}, u32[]{:S(2)}, u32[]{:S(2)}) collective-permute-start(bf16[4,96,256]{2,1,0:T(8,128)(2,1)S(1)} %shard_map.124.refs_6_), channel_id=1, source_target_pairs={{0,6},{1,7},{2,4},{3,5},{4,2},{5,3},{6,0},{7,1},{8,14},{9,15},{10,... | collective-permute-start | bytes 589832 | tf_op jit(solution)/shard_map/ppermute | solution.py:30
  140.6 18.0 %collective-permute-start.39 = (bf16[4,96,256]{2,1,0:T(8,128)(2,1)S(1)}, bf16[4,96,256]{2,1,0:T(8,128)(2,1)S(1)}, u32[]{:S(2)}, u32[]{:S(2)}) collective-permute-start(bf16[4,96,256]{2,1,0:T(8,128)(2,1)S(1)} %shard_map.124.refs_6_), channel_id=1, source_target_pairs={{0,4},{1,5},{2,6},{3,7},{4,0},{5,1},{6,2},{7,3},{8,12},{9,13},{10,... | collective-permute-start | bytes 589832 | tf_op jit(solution)/shard_map/ppermute | solution.py:30
  144.4 14.1 %collective-permute-start.38 = (bf16[4,96,256]{2,1,0:T(8,128)(2,1)S(1)}, bf16[4,96,256]{2,1,0:T(8,128)(2,1)S(1)}, u32[]{:S(2)}, u32[]{:S(2)}) collective-permute-start(bf16[4,96,256]{2,1,0:T(8,128)(2,1)S(1)} %shard_map.124.refs_6_), channel_id=1, source_target_pairs={{0,2},{1,3},{2,0},{3,1},{4,6},{5,7},{6,4},{7,5},{8,10},{9,11},{10,... | collective-permute-start | bytes 589832 | tf_op jit(solution)/shard_map/ppermute | solution.py:30
  169.3 20.2 %collective-permute-start.53 = (s16[1168,256]{1,0:T(8,128)(2,1)S(1)}, s16[1168,256]{1,0:T(8,128)(2,1)S(1)}, u32[]{:S(2)}, u32[]{:S(2)}) collective-permute-start(s16[1168,256]{1,0:T(8,128)(2,1)S(1)} %get-tuple-element.120), channel_id=1, source_target_pairs={{0,8},{8,0},{16,24},{24,16},{1,9},{9,1},{17,25},{25,17},{2,10},{10... | collective-permute-start | bytes 1794056 | tf_op jit(solution)/shard_map/ppermute | solution.py:30
  175.5 15.6 %collective-permute-start.54 = (s16[1168,256]{1,0:T(8,128)(2,1)S(1)}, s16[1168,256]{1,0:T(8,128)(2,1)S(1)}, u32[]{:S(2)}, u32[]{:S(2)}) collective-permute-start(s16[1168,256]{1,0:T(8,128)(2,1)S(1)} %get-tuple-element.121), channel_id=1, source_target_pairs={{0,16},{8,24},{16,0},{24,8},{1,17},{9,25},{17,1},{25,9},{2,18},{10... | collective-permute-start | bytes 1794056 | tf_op jit(solution)/shard_map/ppermute | solution.py:30
  175.8 15.2 %collective-permute-start.50 = (s16[400,256]{1,0:T(8,128)(2,1)S(1)}, s16[400,256]{1,0:T(8,128)(2,1)S(1)}, u32[]{:S(2)}, u32[]{:S(2)}) collective-permute-start(s16[400,256]{1,0:T(8,128)(2,1)S(1)} %get-tuple-element.116), channel_id=1, source_target_pairs={{0,2},{1,3},{2,0},{3,1},{4,6},{5,7},{6,4},{7,5},{8,10},{9,11},{10,... | collective-permute-start | bytes 614408 | tf_op jit(solution)/shard_map/ppermute | solution.py:30
  (40 other events, 342.4 us)

commit v7 on v6

--- a/solution.py
+++ b/solution.py
@@ -68,7 +68,7 @@
     sources, refs = refs[: elec_pieces + phon_pieces], refs[elec_pieces + phon_pieces :]
     whole, refs = refs[: len(elec_kept) + len(phon_kept)], refs[len(elec_kept) + len(phon_kept) :]
     coded, refs = refs[: len(plan)], refs[len(plan) :]
-    elec, phon, elec_totals, phon_totals, held, tile_sems, out_sems = refs
+    elec, phon, elec_totals, phon_totals, held, tile_sems = refs
     groups = group_count[0]
 
     def fetch(index):
@@ -118,18 +118,10 @@
 
     lax.fori_loop(0, groups, one_group, 0)
     places = [(elec_totals, span) for span in elec_kept] + [(phon_totals, span) for span in phon_kept]
-    stores = [
-        pltpu.make_async_copy(
-            totals.at[pl.ds(first, end - first)], whole[index], out_sems.at[index]
-        )
-        for index, (totals, (first, end)) in enumerate(places)
-    ]
-    for store in stores:
-        store.start()
+    for target, (totals, (first, end)) in zip(whole, places):
+        target[...] = totals[pl.ds(first, end - first)]
     for blocks, piece in zip(plan, coded):
         encode_piece(lambda index, blocks=blocks: phon_totals[blocks[index]], len(blocks), piece)
-    for store in stores:
-        store.wait()
 
 
 def drags(ids, tile_set, group, elec_pieces, phon_pieces, kept):
@@ -150,7 +142,7 @@
         ]
         + [coded_shape(len(blocks), rows, lanes) for blocks in plan],
         in_specs=[smem] * 5 + [any_space] + [vmem] * len(pieces),
-        out_specs=[any_space] * len(whole) + [vmem] * len(plan),
+        out_specs=[vmem] * (len(whole) + len(plan)),
         scratch_shapes=[
             pltpu.VMEM((elec_blocks, rows, lanes), jnp.bfloat16),
             pltpu.VMEM((phon_blocks, rows, lanes), jnp.bfloat16),
@@ -158,7 +150,6 @@
             pltpu.VMEM((phon_blocks + 1, rows, lanes), jnp.float32),
             pltpu.VMEM((DEPTH, group, side, side), jnp.bfloat16),
             pltpu.SemaphoreType.DMA((DEPTH,)),
-            pltpu.SemaphoreType.DMA((len(whole),)),
         ],
         compiler_params=pltpu.CompilerParams(vmem_limit_bytes=40 * 1024 * 1024),
         cost_estimate=pl.CostEstimate(

time: 204 us -> 204 us (level)
  starting transfers between devices: 71.7 us -> 94.5 us
  waiting for transfers between devices: 100 us -> 84 us
  Pallas kernels: 30.8 us -> 22.6 us
    ppermute x57, starting transfers between devices: 71.7 us -> 94.5 us  [send(): lax.ppermute(value, axis, [(place, place_of(place)) for place in range(si...]
    ppermute x57, waiting for transfers between devices: 100 us -> 84 us  [send(): lax.ppermute(value, axis, [(place, place_of(place)) for place in range(si...]
    pallas_call x3, Pallas kernels: 24 us -> 15.8 us  [drags(): pl.pallas_call(functools.partial(drags_body, group, (len(elec_pieces), le...]
  transfers between devices with their start and end apart: 57 -> 57, of which waited for: 34 -> 36; matrix products, arithmetic and copies ran while one was open for 0% -> 0% of each run, Pallas kernels for 1% -> 1%
where the time goes in v7:
time: 204 us
  starting transfers between devices  94.5 us (46%)
  waiting for transfers between devices  84 us (41%)
  Pallas kernels  22.6 us (11%)
    ppermute x57, starting transfers between devices, send(): lax.ppermute(value, axis, [(place, place_of(place)) for place in range(si...  94.5 us
    ppermute x57, waiting for transfers between devices, send(): lax.ppermute(value, axis, [(place, place_of(place)) for place in range(si...  84 us
    pallas_call x3, Pallas kernels, drags(): pl.pallas_call(functools.partial(drags_body, group, (len(elec_pieces), le...  15.8 us
  transfers between devices with their start and end apart: 57, of which 36 were waited for; matrix products, arithmetic and copies ran while one was open for 0% of the time, Pallas kernels for 1%

profile of v7, /device:TPU:0, one launch (start us, length us, event | category | flops | bytes accessed | tf_op | source)
XLA Modules:
  0.0 204.1 jit_solution(17009556094268355095)
XLA Ops:
  6.6 3.7 %collective-permute-start.2 = (bf16[4,96,256]{2,1,0:T(8,128)(2,1)S(1)}, bf16[4,96,256]{2,1,0:T(8,128)(2,1)S(1)}, u32[]{:S(2)}, u32[]{:S(2)}) collective-permute-start(bf16[4,96,256]{2,1,0:T(8,128)(2,1)S(1)} %convert_element_type.9.refs_6_), channel_id=1, source_target_pairs={{0,6},{1,7},{2,4},{3,5},{4,2},{5,3},{6,0},{7,1},{8,14},{9,15},{10,... | collective-permute-start | bytes 589832 | tf_op jit(solution)/shard_map/ppermute | solution.py:30
  11.1 7.4 %collective-permute-done.5.far.refs_16_ = bf16[12,96,256]{2,1,0:T(8,128)(2,1)S(1)} collective-permute-done((bf16[12,96,256]{2,1,0:T(8,128)(2,1)S(1)}, bf16[12,96,256]{2,1,0:T(8,128)(2,1)S(1)}, u32[]{:S(2)}, u32[]{:S(2)}) %collective-permute-start.5) | collective-permute-done | bytes 589856 | tf_op jit(solution)/shard_map/ppermute | solution.py:30
  30.3 5.2 %shard_map.114 = (f32[16,96,256]{2,1,0:T(8,128)S(1)}, f32[16,96,256]{2,1,0:T(8,128)S(1)}, f32[12,96,256]{2,1,0:T(8,128)S(1)}, f32[12,96,256]{2,1,0:T(8,128)S(1)}...) custom-call(s32[128]{0:T(128)S(1)} %get-tuple-element.133.refs_0_, s32[128]{0:T(128)S(1)} %get-tuple-element.132.refs_1_, ...), custom_call_target="tpu_custom_call" | custom-call | flops 3221225472 | bytes 33554432 | tf_op jit(solution)/shard_map/pallas_call | solution.py:138
  39.7 5.6 %collective-permute-start.12 = (s16[400,256]{1,0:T(8,128)(2,1)S(1)}, s16[400,256]{1,0:T(8,128)(2,1)S(1)}, u32[]{:S(2)}, u32[]{:S(2)}) collective-permute-start(s16[400,256]{1,0:T(8,128)(2,1)S(1)} %get-tuple-element.74), channel_id=1, source_target_pairs={{0,2},{1,3},{2,0},{3,1},{4,6},{5,7},{6,4},{7,5},{8,10},{9,11},{10,... | collective-permute-start | bytes 614408 | tf_op jit(solution)/shard_map/ppermute | solution.py:30
  45.3 3.9 %collective-permute-start.13 = (s16[400,256]{1,0:T(8,128)(2,1)S(1)}, s16[400,256]{1,0:T(8,128)(2,1)S(1)}, u32[]{:S(2)}, u32[]{:S(2)}) collective-permute-start(s16[400,256]{1,0:T(8,128)(2,1)S(1)} %get-tuple-element.75), channel_id=1, source_target_pairs={{0,4},{1,5},{2,6},{3,7},{4,0},{5,1},{6,2},{7,3},{8,12},{9,13},{10,... | collective-permute-start | bytes 614408 | tf_op jit(solution)/shard_map/ppermute | solution.py:30
  55.5 5.8 %collective-permute-start.17 = (s16[592,256]{1,0:T(8,128)(2,1)S(1)}, s16[592,256]{1,0:T(8,128)(2,1)S(1)}, u32[]{:S(2)}, u32[]{:S(2)}) collective-permute-start(s16[592,256]{1,0:T(8,128)(2,1)S(1)} %get-tuple-element.83), channel_id=1, source_target_pairs={{0,8},{8,0},{16,24},{24,16},{1,9},{9,1},{17,25},{25,17},{2,10},{10... | collective-permute-start | bytes 909320 | tf_op jit(solution)/shard_map/ppermute | solution.py:30
  63.7 5.2 %collective-permute-done.14.refs_2_ = s16[400,256]{1,0:T(8,128)(2,1)S(1)} collective-permute-done((s16[400,256]{1,0:T(8,128)(2,1)S(1)}, s16[400,256]{1,0:T(8,128)(2,1)S(1)}, u32[]{:S(2)}, u32[]{:S(2)}) %collective-permute-start.14) | collective-permute-done | bytes 204832 | tf_op jit(solution)/shard_map/ppermute | solution.py:30
  72.2 3.6 %collective-permute-start.21 = (bf16[4,96,256]{2,1,0:T(8,128)(2,1)S(1)}, bf16[4,96,256]{2,1,0:T(8,128)(2,1)S(1)}, u32[]{:S(2)}, u32[]{:S(2)}) collective-permute-start(bf16[4,96,256]{2,1,0:T(8,128)(2,1)S(1)} %shard_map.118.refs_6_), channel_id=1, source_target_pairs={{0,6},{1,7},{2,4},{3,5},{4,2},{5,3},{6,0},{7,1},{8,14},{9,15},{10,... | collective-permute-start | bytes 589832 | tf_op jit(solution)/shard_map/ppermute | solution.py:30
  77.5 4.0 %collective-permute-done.24.far.refs_16_ = bf16[12,96,256]{2,1,0:T(8,128)(2,1)S(1)} collective-permute-done((bf16[12,96,256]{2,1,0:T(8,128)(2,1)S(1)}, bf16[12,96,256]{2,1,0:T(8,128)(2,1)S(1)}, u32[]{:S(2)}, u32[]{:S(2)}) %collective-permute-start.24) | collective-permute-done | bytes 589856 | tf_op jit(solution)/shard_map/ppermute | solution.py:30
  85.8 5.6 %collective-permute-done.20.refs_8_ = bf16[4,96,256]{2,1,0:T(8,128)(2,1)S(1)} collective-permute-done((bf16[4,96,256]{2,1,0:T(8,128)(2,1)S(1)}, bf16[4,96,256]{2,1,0:T(8,128)(2,1)S(1)}, u32[]{:S(2)}, u32[]{:S(2)}) %collective-permute-start.20) | collective-permute-done | bytes 196640 | tf_op jit(solution)/shard_map/ppermute | solution.py:30
  93.4 5.4 %shard_map.120 = (f32[16,96,256]{2,1,0:T(8,128)S(1)}, f32[16,96,256]{2,1,0:T(8,128)S(1)}, f32[12,96,256]{2,1,0:T(8,128)S(1)}, f32[12,96,256]{2,1,0:T(8,128)S(1)}...) custom-call(s32[128]{0:T(128)S(1)} %get-tuple-element.133.refs_0_, s32[128]{0:T(128)S(1)} %get-tuple-element.132.refs_1_, ...), custom_call_target="tpu_custom_call" | custom-call | flops 3221225472 | bytes 33554432 | tf_op jit(solution)/shard_map/pallas_call | solution.py:138
  104.8 8.2 %collective-permute-start.31 = (s16[400,256]{1,0:T(8,128)(2,1)S(1)}, s16[400,256]{1,0:T(8,128)(2,1)S(1)}, u32[]{:S(2)}, u32[]{:S(2)}) collective-permute-start(s16[400,256]{1,0:T(8,128)(2,1)S(1)} %get-tuple-element.95), channel_id=1, source_target_pairs={{0,2},{1,3},{2,0},{3,1},{4,6},{5,7},{6,4},{7,5},{8,10},{9,11},{10,... | collective-permute-start | bytes 614408 | tf_op jit(solution)/shard_map/ppermute | solution.py:30
  117.0 5.8 %collective-permute-done.31.refs_0_ = s16[400,256]{1,0:T(8,128)(2,1)S(1)} collective-permute-done((s16[400,256]{1,0:T(8,128)(2,1)S(1)}, s16[400,256]{1,0:T(8,128)(2,1)S(1)}, u32[]{:S(2)}, u32[]{:S(2)}) %collective-permute-start.31) | collective-permute-done | bytes 204832 | tf_op jit(solution)/shard_map/ppermute | solution.py:30
  123.1 5.8 %collective-permute-start.36 = (s16[592,256]{1,0:T(8,128)(2,1)S(1)}, s16[592,256]{1,0:T(8,128)(2,1)S(1)}, u32[]{:S(2)}, u32[]{:S(2)}) collective-permute-start(s16[592,256]{1,0:T(8,128)(2,1)S(1)} %get-tuple-element.104), channel_id=1, source_target_pairs={{0,8},{8,0},{16,24},{24,16},{1,9},{9,1},{17,25},{25,17},{2,10},{10... | collective-permute-start | bytes 909320 | tf_op jit(solution)/shard_map/ppermute | solution.py:30
  130.6 6.0 %collective-permute-done.33.refs_2_ = s16[400,256]{1,0:T(8,128)(2,1)S(1)} collective-permute-done((s16[400,256]{1,0:T(8,128)(2,1)S(1)}, s16[400,256]{1,0:T(8,128)(2,1)S(1)}, u32[]{:S(2)}, u32[]{:S(2)}) %collective-permute-start.33) | collective-permute-done | bytes 204832 | tf_op jit(solution)/shard_map/ppermute | solution.py:30
  141.4 4.6 %collective-permute-start.39 = (bf16[4,96,256]{2,1,0:T(8,128)(2,1)S(1)}, bf16[4,96,256]{2,1,0:T(8,128)(2,1)S(1)}, u32[]{:S(2)}, u32[]{:S(2)}) collective-permute-start(bf16[4,96,256]{2,1,0:T(8,128)(2,1)S(1)} %shard_map.124.refs_6_), channel_id=1, source_target_pairs={{0,4},{1,5},{2,6},{3,7},{4,0},{5,1},{6,2},{7,3},{8,12},{9,13},{10,... | collective-permute-start | bytes 589832 | tf_op jit(solution)/shard_map/ppermute | solution.py:30
  150.4 7.7 %collective-permute-done.39.refs_8_ = bf16[4,96,256]{2,1,0:T(8,128)(2,1)S(1)} collective-permute-done((bf16[4,96,256]{2,1,0:T(8,128)(2,1)S(1)}, bf16[4,96,256]{2,1,0:T(8,128)(2,1)S(1)}, u32[]{:S(2)}, u32[]{:S(2)}) %collective-permute-start.39) | collective-permute-done | bytes 196640 | tf_op jit(solution)/shard_map/ppermute | solution.py:30
  160.0 5.2 %shard_map.126 = (f32[16,96,256]{2,1,0:T(8,128)S(1)}, f32[16,96,256]{2,1,0:T(8,128)S(1)}, f32[12,96,256]{2,1,0:T(8,128)S(1)}, f32[12,96,256]{2,1,0:T(8,128)S(1)}...) custom-call(s32[128]{0:T(128)S(1)} %get-tuple-element.133.refs_0_, s32[128]{0:T(128)S(1)} %get-tuple-element.132.refs_1_, ...), custom_call_target="tpu_custom_call" | custom-call | flops 3221225472 | bytes 33554432 | tf_op jit(solution)/shard_map/pallas_call | solution.py:138
  171.3 6.7 %collective-permute-start.50 = (s16[400,256]{1,0:T(8,128)(2,1)S(1)}, s16[400,256]{1,0:T(8,128)(2,1)S(1)}, u32[]{:S(2)}, u32[]{:S(2)}) collective-permute-start(s16[400,256]{1,0:T(8,128)(2,1)S(1)} %get-tuple-element.116), channel_id=1, source_target_pairs={{0,2},{1,3},{2,0},{3,1},{4,6},{5,7},{6,4},{7,5},{8,10},{9,11},{10,... | collective-permute-start | bytes 614408 | tf_op jit(solution)/shard_map/ppermute | solution.py:30
  178.0 4.4 %collective-permute-start.51 = (s16[400,256]{1,0:T(8,128)(2,1)S(1)}, s16[400,256]{1,0:T(8,128)(2,1)S(1)}, u32[]{:S(2)}, u32[]{:S(2)}) collective-permute-start(s16[400,256]{1,0:T(8,128)(2,1)S(1)} %get-tuple-element.117), channel_id=1, source_target_pairs={{0,4},{1,5},{2,6},{3,7},{4,0},{5,1},{6,2},{7,3},{8,12},{9,13},{10,... | collective-permute-start | bytes 614408 | tf_op jit(solution)/shard_map/ppermute | solution.py:30
  183.5 4.3 %collective-permute-done.51.refs_1_ = s16[400,256]{1,0:T(8,128)(2,1)S(1)} collective-permute-done((s16[400,256]{1,0:T(8,128)(2,1)S(1)}, s16[400,256]{1,0:T(8,128)(2,1)S(1)}, u32[]{:S(2)}, u32[]{:S(2)}) %collective-permute-start.51) | collective-permute-done | bytes 204832 | tf_op jit(solution)/shard_map/ppermute | solution.py:30
  188.1 3.4 %collective-permute-start.55 = (s16[592,256]{1,0:T(8,128)(2,1)S(1)}, s16[592,256]{1,0:T(8,128)(2,1)S(1)}, u32[]{:S(2)}, u32[]{:S(2)}) collective-permute-start(s16[592,256]{1,0:T(8,128)(2,1)S(1)} %get-tuple-element.125), channel_id=1, source_target_pairs={{0,8},{8,0},{16,24},{24,16},{1,9},{9,1},{17,25},{25,17},{2,10},{10... | collective-permute-start | bytes 909320 | tf_op jit(solution)/shard_map/ppermute | solution.py:30
  191.5 5.3 %collective-permute-start.52 = (s16[400,256]{1,0:T(8,128)(2,1)S(1)}, s16[400,256]{1,0:T(8,128)(2,1)S(1)}, u32[]{:S(2)}, u32[]{:S(2)}) collective-permute-start(s16[400,256]{1,0:T(8,128)(2,1)S(1)} %get-tuple-element.118), channel_id=1, source_target_pairs={{0,6},{1,7},{2,4},{3,5},{4,2},{5,3},{6,0},{7,1},{8,14},{9,15},{10,... | collective-permute-start | bytes 614408 | tf_op jit(solution)/shard_map/ppermute | solution.py:30
  196.8 4.9 %collective-permute-done.52.refs_2_ = s16[400,256]{1,0:T(8,128)(2,1)S(1)} collective-permute-done((s16[400,256]{1,0:T(8,128)(2,1)S(1)}, s16[400,256]{1,0:T(8,128)(2,1)S(1)}, u32[]{:S(2)}, u32[]{:S(2)}) %collective-permute-start.52) | collective-permute-done | bytes 204832 | tf_op jit(solution)/shard_map/ppermute | solution.py:30
  (126 shorter events, 75.2 us)
Async XLA Ops:
  2.0 16.4 %collective-permute-start.5 = (bf16[12,96,256]{2,1,0:T(8,128)(2,1)S(1)}, bf16[12,96,256]{2,1,0:T(8,128)(2,1)S(1)}, u32[]{:S(2)}, u32[]{:S(2)}) collective-permute-start(bf16[12,96,256]{2,1,0:T(8,128)(2,1)S(1)} %convert_bitcast_fusion.refs_14_), channel_id=1, source_target_pairs={{0,16},{8,24},{16,0},{24,8},{1,17},{9,25},{17,1},{25,9},{2,18},{10... | collective-permute-start | bytes 1769480 | tf_op jit(solution)/shard_map/ppermute | solution.py:30
  5.1 14.8 %collective-permute-start.4 = (bf16[12,96,256]{2,1,0:T(8,128)(2,1)S(1)}, bf16[12,96,256]{2,1,0:T(8,128)(2,1)S(1)}, u32[]{:S(2)}, u32[]{:S(2)}) collective-permute-start(bf16[12,96,256]{2,1,0:T(8,128)(2,1)S(1)} %convert_bitcast_fusion.refs_14_), channel_id=1, source_target_pairs={{0,8},{8,0},{16,24},{24,16},{1,9},{9,1},{17,25},{25,17},{2,10},{10... | collective-permute-start | bytes 1769480 | tf_op jit(solution)/shard_map/ppermute | solution.py:30
  6.6 15.6 %collective-permute-start.2 = (bf16[4,96,256]{2,1,0:T(8,128)(2,1)S(1)}, bf16[4,96,256]{2,1,0:T(8,128)(2,1)S(1)}, u32[]{:S(2)}, u32[]{:S(2)}) collective-permute-start(bf16[4,96,256]{2,1,0:T(8,128)(2,1)S(1)} %convert_element_type.9.refs_6_), channel_id=1, source_target_pairs={{0,6},{1,7},{2,4},{3,5},{4,2},{5,3},{6,0},{7,1},{8,14},{9,15},{10,... | collective-permute-start | bytes 589832 | tf_op jit(solution)/shard_map/ppermute | solution.py:30
  10.3 16.1 %collective-permute-start.1 = (bf16[4,96,256]{2,1,0:T(8,128)(2,1)S(1)}, bf16[4,96,256]{2,1,0:T(8,128)(2,1)S(1)}, u32[]{:S(2)}, u32[]{:S(2)}) collective-permute-start(bf16[4,96,256]{2,1,0:T(8,128)(2,1)S(1)} %convert_element_type.9.refs_6_), channel_id=1, source_target_pairs={{0,4},{1,5},{2,6},{3,7},{4,0},{5,1},{6,2},{7,3},{8,12},{9,13},{10,... | collective-permute-start | bytes 589832 | tf_op jit(solution)/shard_map/ppermute | solution.py:30
  10.3 16.1 %collective-permute-start = (bf16[4,96,256]{2,1,0:T(8,128)(2,1)S(1)}, bf16[4,96,256]{2,1,0:T(8,128)(2,1)S(1)}, u32[]{:S(2)}, u32[]{:S(2)}) collective-permute-start(bf16[4,96,256]{2,1,0:T(8,128)(2,1)S(1)} %convert_element_type.9.refs_6_), channel_id=1, source_target_pairs={{0,2},{1,3},{2,0},{3,1},{4,6},{5,7},{6,4},{7,5},{8,10},{9,11},{10,... | collective-permute-start | bytes 589832 | tf_op jit(solution)/shard_map/ppermute | solution.py:30
  36.3 15.5 %collective-permute-start.15 = (s16[1168,256]{1,0:T(8,128)(2,1)S(1)}, s16[1168,256]{1,0:T(8,128)(2,1)S(1)}, u32[]{:S(2)}, u32[]{:S(2)}) collective-permute-start(s16[1168,256]{1,0:T(8,128)(2,1)S(1)} %get-tuple-element.78), channel_id=1, source_target_pairs={{0,8},{8,0},{16,24},{24,16},{1,9},{9,1},{17,25},{25,17},{2,10},{10... | collective-permute-start | bytes 1794056 | tf_op jit(solution)/shard_map/ppermute | solution.py:30
  36.3 15.6 %collective-permute-start.16 = (s16[1168,256]{1,0:T(8,128)(2,1)S(1)}, s16[1168,256]{1,0:T(8,128)(2,1)S(1)}, u32[]{:S(2)}, u32[]{:S(2)}) collective-permute-start(s16[1168,256]{1,0:T(8,128)(2,1)S(1)} %get-tuple-element.79), channel_id=1, source_target_pairs={{0,16},{8,24},{16,0},{24,8},{1,17},{9,25},{17,1},{25,9},{2,18},{10... | collective-permute-start | bytes 1794056 | tf_op jit(solution)/shard_map/ppermute | solution.py:30
  39.7 15.4 %collective-permute-start.12 = (s16[400,256]{1,0:T(8,128)(2,1)S(1)}, s16[400,256]{1,0:T(8,128)(2,1)S(1)}, u32[]{:S(2)}, u32[]{:S(2)}) collective-permute-start(s16[400,256]{1,0:T(8,128)(2,1)S(1)} %get-tuple-element.74), channel_id=1, source_target_pairs={{0,2},{1,3},{2,0},{3,1},{4,6},{5,7},{6,4},{7,5},{8,10},{9,11},{10,... | collective-permute-start | bytes 614408 | tf_op jit(solution)/shard_map/ppermute | solution.py:30
  55.5 13.4 %collective-permute-start.17 = (s16[592,256]{1,0:T(8,128)(2,1)S(1)}, s16[592,256]{1,0:T(8,128)(2,1)S(1)}, u32[]{:S(2)}, u32[]{:S(2)}) collective-permute-start(s16[592,256]{1,0:T(8,128)(2,1)S(1)} %get-tuple-element.83), channel_id=1, source_target_pairs={{0,8},{8,0},{16,24},{24,16},{1,9},{9,1},{17,25},{25,17},{2,10},{10... | collective-permute-start | bytes 909320 | tf_op jit(solution)/shard_map/ppermute | solution.py:30
  69.4 12.2 %collective-permute-start.24 = (bf16[12,96,256]{2,1,0:T(8,128)(2,1)S(1)}, bf16[12,96,256]{2,1,0:T(8,128)(2,1)S(1)}, u32[]{:S(2)}, u32[]{:S(2)}) collective-permute-start(bf16[12,96,256]{2,1,0:T(8,128)(2,1)S(1)} %shard_map.117.refs_14_), channel_id=1, source_target_pairs={{0,16},{8,24},{16,0},{24,8},{1,17},{9,25},{17,1},{25,9},{2,18},{10... | collective-permute-start | bytes 1769480 | tf_op jit(solution)/shard_map/ppermute | solution.py:30
  71.5 12.1 %collective-permute-start.23 = (bf16[12,96,256]{2,1,0:T(8,128)(2,1)S(1)}, bf16[12,96,256]{2,1,0:T(8,128)(2,1)S(1)}, u32[]{:S(2)}, u32[]{:S(2)}) collective-permute-start(bf16[12,96,256]{2,1,0:T(8,128)(2,1)S(1)} %shard_map.117.refs_14_), channel_id=1, source_target_pairs={{0,8},{8,0},{16,24},{24,16},{1,9},{9,1},{17,25},{25,17},{2,10},{10... | collective-permute-start | bytes 1769480 | tf_op jit(solution)/shard_map/ppermute | solution.py:30
  72.2 13.2 %collective-permute-start.21 = (bf16[4,96,256]{2,1,0:T(8,128)(2,1)S(1)}, bf16[4,96,256]{2,1,0:T(8,128)(2,1)S(1)}, u32[]{:S(2)}, u32[]{:S(2)}) collective-permute-start(bf16[4,96,256]{2,1,0:T(8,128)(2,1)S(1)} %shard_map.118.refs_6_), channel_id=1, source_target_pairs={{0,6},{1,7},{2,4},{3,5},{4,2},{5,3},{6,0},{7,1},{8,14},{9,15},{10,... | collective-permute-start | bytes 589832 | tf_op jit(solution)/shard_map/ppermute | solution.py:30
  75.8 15.5 %collective-permute-start.20 = (bf16[4,96,256]{2,1,0:T(8,128)(2,1)S(1)}, bf16[4,96,256]{2,1,0:T(8,128)(2,1)S(1)}, u32[]{:S(2)}, u32[]{:S(2)}) collective-permute-start(bf16[4,96,256]{2,1,0:T(8,128)(2,1)S(1)} %shard_map.118.refs_6_), channel_id=1, source_target_pairs={{0,4},{1,5},{2,6},{3,7},{4,0},{5,1},{6,2},{7,3},{8,12},{9,13},{10,... | collective-permute-start | bytes 589832 | tf_op jit(solution)/shard_map/ppermute | solution.py:30
  77.5 13.9 %collective-permute-start.19 = (bf16[4,96,256]{2,1,0:T(8,128)(2,1)S(1)}, bf16[4,96,256]{2,1,0:T(8,128)(2,1)S(1)}, u32[]{:S(2)}, u32[]{:S(2)}) collective-permute-start(bf16[4,96,256]{2,1,0:T(8,128)(2,1)S(1)} %shard_map.118.refs_6_), channel_id=1, source_target_pairs={{0,2},{1,3},{2,0},{3,1},{4,6},{5,7},{6,4},{7,5},{8,10},{9,11},{10,... | collective-permute-start | bytes 589832 | tf_op jit(solution)/shard_map/ppermute | solution.py:30
  101.4 15.5 %collective-permute-start.34 = (s16[1168,256]{1,0:T(8,128)(2,1)S(1)}, s16[1168,256]{1,0:T(8,128)(2,1)S(1)}, u32[]{:S(2)}, u32[]{:S(2)}) collective-permute-start(s16[1168,256]{1,0:T(8,128)(2,1)S(1)} %get-tuple-element.99), channel_id=1, source_target_pairs={{0,8},{8,0},{16,24},{24,16},{1,9},{9,1},{17,25},{25,17},{2,10},{10... | collective-permute-start | bytes 1794056 | tf_op jit(solution)/shard_map/ppermute | solution.py:30
  101.4 15.6 %collective-permute-start.35 = (s16[1168,256]{1,0:T(8,128)(2,1)S(1)}, s16[1168,256]{1,0:T(8,128)(2,1)S(1)}, u32[]{:S(2)}, u32[]{:S(2)}) collective-permute-start(s16[1168,256]{1,0:T(8,128)(2,1)S(1)} %get-tuple-element.100), channel_id=1, source_target_pairs={{0,16},{8,24},{16,0},{24,8},{1,17},{9,25},{17,1},{25,9},{2,18},{10... | collective-permute-start | bytes 1794056 | tf_op jit(solution)/shard_map/ppermute | solution.py:30
  104.8 18.0 %collective-permute-start.31 = (s16[400,256]{1,0:T(8,128)(2,1)S(1)}, s16[400,256]{1,0:T(8,128)(2,1)S(1)}, u32[]{:S(2)}, u32[]{:S(2)}) collective-permute-start(s16[400,256]{1,0:T(8,128)(2,1)S(1)} %get-tuple-element.95), channel_id=1, source_target_pairs={{0,2},{1,3},{2,0},{3,1},{4,6},{5,7},{6,4},{7,5},{8,10},{9,11},{10,... | collective-permute-start | bytes 614408 | tf_op jit(solution)/shard_map/ppermute | solution.py:30
  123.1 13.4 %collective-permute-start.36 = (s16[592,256]{1,0:T(8,128)(2,1)S(1)}, s16[592,256]{1,0:T(8,128)(2,1)S(1)}, u32[]{:S(2)}, u32[]{:S(2)}) collective-permute-start(s16[592,256]{1,0:T(8,128)(2,1)S(1)} %get-tuple-element.104), channel_id=1, source_target_pairs={{0,8},{8,0},{16,24},{24,16},{1,9},{9,1},{17,25},{25,17},{2,10},{10... | collective-permute-start | bytes 909320 | tf_op jit(solution)/shard_map/ppermute | solution.py:30
  141.4 16.7 %collective-permute-start.39 = (bf16[4,96,256]{2,1,0:T(8,128)(2,1)S(1)}, bf16[4,96,256]{2,1,0:T(8,128)(2,1)S(1)}, u32[]{:S(2)}, u32[]{:S(2)}) collective-permute-start(bf16[4,96,256]{2,1,0:T(8,128)(2,1)S(1)} %shard_map.124.refs_6_), channel_id=1, source_target_pairs={{0,4},{1,5},{2,6},{3,7},{4,0},{5,1},{6,2},{7,3},{8,12},{9,13},{10,... | collective-permute-start | bytes 589832 | tf_op jit(solution)/shard_map/ppermute | solution.py:30
  146.0 12.0 %collective-permute-start.38 = (bf16[4,96,256]{2,1,0:T(8,128)(2,1)S(1)}, bf16[4,96,256]{2,1,0:T(8,128)(2,1)S(1)}, u32[]{:S(2)}, u32[]{:S(2)}) collective-permute-start(bf16[4,96,256]{2,1,0:T(8,128)(2,1)S(1)} %shard_map.124.refs_6_), channel_id=1, source_target_pairs={{0,2},{1,3},{2,0},{3,1},{4,6},{5,7},{6,4},{7,5},{8,10},{9,11},{10,... | collective-permute-start | bytes 589832 | tf_op jit(solution)/shard_map/ppermute | solution.py:30
  167.9 15.5 %collective-permute-start.53 = (s16[1168,256]{1,0:T(8,128)(2,1)S(1)}, s16[1168,256]{1,0:T(8,128)(2,1)S(1)}, u32[]{:S(2)}, u32[]{:S(2)}) collective-permute-start(s16[1168,256]{1,0:T(8,128)(2,1)S(1)} %get-tuple-element.120), channel_id=1, source_target_pairs={{0,8},{8,0},{16,24},{24,16},{1,9},{9,1},{17,25},{25,17},{2,10},{10... | collective-permute-start | bytes 1794056 | tf_op jit(solution)/shard_map/ppermute | solution.py:30
  167.9 15.6 %collective-permute-start.54 = (s16[1168,256]{1,0:T(8,128)(2,1)S(1)}, s16[1168,256]{1,0:T(8,128)(2,1)S(1)}, u32[]{:S(2)}, u32[]{:S(2)}) collective-permute-start(s16[1168,256]{1,0:T(8,128)(2,1)S(1)} %get-tuple-element.121), channel_id=1, source_target_pairs={{0,16},{8,24},{16,0},{24,8},{1,17},{9,25},{17,1},{25,9},{2,18},{10... | collective-permute-start | bytes 1794056 | tf_op jit(solution)/shard_map/ppermute | solution.py:30
  171.3 12.2 %collective-permute-start.50 = (s16[400,256]{1,0:T(8,128)(2,1)S(1)}, s16[400,256]{1,0:T(8,128)(2,1)S(1)}, u32[]{:S(2)}, u32[]{:S(2)}) collective-permute-start(s16[400,256]{1,0:T(8,128)(2,1)S(1)} %get-tuple-element.116), channel_id=1, source_target_pairs={{0,2},{1,3},{2,0},{3,1},{4,6},{5,7},{6,4},{7,5},{8,10},{9,11},{10,... | collective-permute-start | bytes 614408 | tf_op jit(solution)/shard_map/ppermute | solution.py:30
  188.1 13.5 %collective-permute-start.55 = (s16[592,256]{1,0:T(8,128)(2,1)S(1)}, s16[592,256]{1,0:T(8,128)(2,1)S(1)}, u32[]{:S(2)}, u32[]{:S(2)}) collective-permute-start(s16[592,256]{1,0:T(8,128)(2,1)S(1)} %get-tuple-element.125), channel_id=1, source_target_pairs={{0,8},{8,0},{16,24},{24,16},{1,9},{9,1},{17,25},{25,17},{2,10},{10... | collective-permute-start | bytes 909320 | tf_op jit(solution)/shard_map/ppermute | solution.py:30
  (40 other events, 343.3 us)
